TPU v7x, 32 devices: a whole 2x2x4 slice. The times are simulated.
32 devices in a mesh: dp: 4 (over x, core), seq: 8 (over z, y).
Axes of the slice: x: 2, y: 2, z: 4, core: 2. Of those that a mesh axis runs over, the one named last changes fastest.
Arguments:
- queries: bfloat16 [4, 2048, 4096], P('dp', 'seq'), may hold values from -51 to 51
- keys: bfloat16 [4, 2048, 512], P('dp', 'seq'), may hold values from -6 to 6
- values: bfloat16 [4, 2048, 512], P('dp', 'seq'), may hold values from -6 to 6
- targets: bfloat16 [4, 2048, 4096], P('dp', 'seq'), may hold values from -6 to 6
- q_map: bfloat16 [32, 128, 128], replicated, may hold values from -1.5 to 1.5
- k_map: bfloat16 [4, 128, 128], replicated, may hold values from -1.5 to 1.5
- doc_spans: int32 [4, 8], P('dp'), may hold values from 1 to 6, 16 in all within a row
Outputs:
- grad_q_map: float32 [32, 128, 128], replicated
- grad_k_map: float32 [4, 128, 128], replicated
Inputs may be any that keep to these rules, and one draw needn't show every extreme that they name: `doc_spans`: each row sums to 16, and the longest document has exactly 6 blocks.
All inputs are finite; a program needn't handle non-finite values.
Results may differ from a plain program's by a relative error of at most 0.006.
The roundings to bfloat16 on the way count: a program that leaves them out, or rounds other values in their place, can miss the bound.
Values sent between devices are 32-bit elements; how exact they have to be, the bound alone decides.
No kernel may reach another device: no remote copies, remote signals or barrier semaphores. Data moves between devices by JAX's collectives and lax.ppermute only.
A program may use at most 128 MiB of HBM per device.

v0:
```python
import functools
import math

import jax
import jax.numpy as jnp
from jax import lax
from jax.experimental import pallas as pl
from jax.experimental.pallas import tpu as pltpu
from jax.sharding import PartitionSpec as P

SPAN = 128
PAD = 8
F32 = jnp.float32
BF16 = jnp.bfloat16
NN = (((1,), (0,)), ((), ()))
NT = (((1,), (1,)), ((), ()))
TN = (((0,), (0,)), ((), ()))


def dot(left, right, dims):
    return lax.dot_general(left, right, dims, preferred_element_type=F32)


def bounds(spans_ref, block):
    start, end, place = jnp.int32(0), jnp.int32(0), jnp.int32(0)
    for d in range(spans_ref.shape[1]):
        after = place + spans_ref[0, d]
        inside = jnp.logical_and(block >= place, block < after)
        start = jnp.where(inside, place, start)
        end = jnp.where(inside, after, end)
        place = after
    return start, end


def flag(condition):
    return jnp.where(condition, jnp.float32(1.0), jnp.float32(0.0))


def soft_pair(mapped):
    up = jnp.exp(mapped - jnp.max(mapped, -1, keepdims=True))
    low = jnp.exp(jnp.min(mapped, -1, keepdims=True) - mapped)
    up = up * (1.0 / jnp.sum(up, -1, keepdims=True))
    low = low * (1.0 / jnp.sum(low, -1, keepdims=True))
    return up, low


def map_grad(up, low, grad_up, grad_low):
    first = up * (grad_up - jnp.sum(up * grad_up, -1, keepdims=True))
    second = low * (grad_low - jnp.sum(low * grad_low, -1, keepdims=True))
    return (first - second).astype(BF16)


def key_kernel(count, spans_ref, k_ref, v_ref, w_ref, feat_ref, block_ref, *tail_refs):
    width = w_ref.shape[-1]
    heads = w_ref.shape[0]
    first = lax.axis_index("seq") * count
    starts = [bounds(spans_ref, first + c)[0] for c in range(count)]
    for i in range(heads):
        cols = slice(i * width, (i + 1) * width)
        up, low = soft_pair(dot(k_ref[:, cols], w_ref[i], NN))
        feat = jnp.concatenate([up, low], axis=-1).astype(BF16)
        feat_ref[i] = feat
        tail = None
        for c in range(count):
            rows = slice(c * SPAN, (c + 1) * SPAN)
            state = dot(v_ref[rows, cols], feat[rows], TN)
            norm = jnp.sum(feat[rows].astype(F32), axis=0, keepdims=True)
            norm = jnp.broadcast_to(norm, (PAD, norm.shape[1]))
            both = jnp.concatenate([state, norm], axis=0)
            block_ref[i, c] = both
            part = flag(starts[c] == starts[count - 1]) * both
            tail = part if tail is None else tail + part
        tail_refs[i][...] = tail


def join_kernel(count, hop, reverse, spans_ref, own_ref, came_ref, out_ref):
    place = lax.axis_index("seq")
    if reverse:
        _, end = bounds(spans_ref, place * count)
        keep = flag(end > (place + hop) * count)
    else:
        start, _ = bounds(spans_ref, place * count + count - 1)
        keep = flag(start < (place - hop + 1) * count)
    out_ref[...] = own_ref[...] + keep * came_ref[...]


def middle_kernel(count, group, hops, coef, *refs):
    spans_ref, q_ref, t_ref, v_ref, feat_ref, w_ref, block_ref = refs[:7]
    came = refs[7 : 7 + hops]
    gq_ref, head_ref, back_ref, part_ref = refs[7 + hops : 11 + hops]
    width = w_ref.shape[-1]
    c = pl.program_id(0)
    place = lax.axis_index("seq")
    first = place * count
    start_first, _ = bounds(spans_ref, first)
    start, _ = bounds(spans_ref, first + c)
    state = None
    for k in range(hops):
        near = start_first < (place - (1 << k) + 1) * count
        part = flag(jnp.logical_and(near, start < first)) * came[k][...]
        state = part if state is None else state + part
    for e in range(count - 1):
        state = state + flag(jnp.logical_and(e < c, start <= first + e)) * block_ref[e]
    norm = state[SPAN : SPAN + 1].astype(BF16).astype(F32)
    mat = jnp.concatenate([feat_ref[...], state[:SPAN].astype(BF16)], axis=0)
    vals = v_ref[...]
    qs = [q_ref[:, h * width : (h + 1) * width] for h in range(group)]
    mapped = jnp.concatenate([dot(qs[h], w_ref[h], NN) for h in range(group)], axis=0)
    up, low = soft_pair(mapped)
    feat = jnp.concatenate([up, low], axis=-1).astype(BF16)
    wide = feat.astype(F32)
    both = dot(feat, mat, NT)
    rows = group * SPAN
    row = lax.broadcasted_iota(jnp.int32, (rows, SPAN), 0) & (SPAN - 1)
    causal = row >= lax.broadcasted_iota(jnp.int32, (rows, SPAN), 1)
    scores = jnp.where(causal, both[:, :SPAN], 0.0)
    weighed = wide * norm
    denom = jnp.sum(scores + weighed[:, :width] + weighed[:, width:], -1, keepdims=True)
    numer = dot(scores.astype(BF16), vals, NN) + both[:, SPAN:]
    inverse = 1.0 / denom
    output = numer * inverse
    tgt = jnp.concatenate([t_ref[:, h * width : (h + 1) * width] for h in range(group)], axis=0)
    d_out = coef * (output - tgt.astype(F32))
    d_numer = (d_out * inverse).astype(BF16)
    d_denom = -jnp.sum(d_out * output, -1, keepdims=True) * inverse
    pairs = jnp.where(causal, dot(d_numer, vals, NT) + d_denom, 0.0).astype(BF16)
    d_feat = dot(jnp.concatenate([pairs, d_numer], axis=-1), mat, NN) + d_denom * norm
    crossed = dot(jnp.concatenate([d_numer, pairs], axis=-1), feat, TN)
    back_norm = jnp.sum(wide * d_denom, axis=0, keepdims=True)
    back_norm = jnp.broadcast_to(back_norm, (PAD, back_norm.shape[1]))
    back = jnp.concatenate([crossed[:SPAN], back_norm], axis=0)
    back_ref[...] = back
    part_ref[...] = crossed[SPAN:]
    d_map = map_grad(up, low, d_feat[:, :width], d_feat[:, width:])
    grads = [dot(qs[h], d_map[h * SPAN : (h + 1) * SPAN], TN) for h in range(group)]
    mine = flag(start == start_first) * back

    @pl.when(c == 0)
    def _():
        head_ref[...] = mine
        for h in range(group):
            gq_ref[h] = grads[h]

    @pl.when(c > 0)
    def _():
        head_ref[...] += mine
        for h in range(group):
            gq_ref[h] += grads[h]


def last_kernel(count, hops, *refs):
    spans_ref, k_ref, v_ref, w_ref, back_ref, part_ref = refs[:6]
    came = refs[6 : 6 + hops]
    gk_ref = refs[6 + hops]
    width = w_ref.shape[-1]
    place = lax.axis_index("seq")
    first = place * count
    _, end_last = bounds(spans_ref, first + count - 1)
    keys = k_ref[...]
    up, low = soft_pair(dot(keys, w_ref[...], NN))
    grads = []
    for c in range(count):
        _, end = bounds(spans_ref, first + c)
        state = None
        for k in range(hops):
            near = end_last > (place + (1 << k)) * count
            part = flag(jnp.logical_and(near, end > first + count)) * came[k][...]
            state = part if state is None else state + part
        for e in range(c + 1, count):
            state = state + flag(end > first + e) * back_ref[e]
        norm = state[SPAN : SPAN + 1].astype(BF16).astype(F32)
        grad = part_ref[c] + dot(v_ref[c * SPAN : (c + 1) * SPAN], state[:SPAN].astype(BF16), NN)
        grads.append(grad + norm)
    d_feat = jnp.concatenate(grads, axis=0)
    d_map = map_grad(up, low, d_feat[:, :width], d_feat[:, width:])
    gk_ref[...] = dot(keys, d_map, TN)


def cost(flops, moved):
    return pl.CostEstimate(flops=int(flops), bytes_accessed=int(moved), transcendentals=0)


SMEM = pl.BlockSpec(memory_space=pltpu.SMEM)
LIMIT = 48 << 20


def whole_call(body, out_shape, n_vmem, flops, *args):
    moved = sum(a.size * a.dtype.itemsize for a in args)
    return pl.pallas_call(
        body,
        out_shape=out_shape,
        in_specs=[SMEM] + [pl.BlockSpec(memory_space=pltpu.VMEM)] * n_vmem,
        compiler_params=pltpu.CompilerParams(vmem_limit_bytes=LIMIT),
        cost_estimate=cost(flops, moved),
    )(*args)


def swap(x, axis, size, bit):
    return lax.ppermute(x, axis, [(i, i ^ (1 << bit)) for i in range(size)])


def sum_all(x, steps):
    for axis, size, bit in steps:
        mine = (lax.axis_index(axis) >> bit) & 1
        pair = x.reshape(2, x.shape[0] // 2, x.shape[1])
        send = lax.dynamic_index_in_dim(pair, 1 - mine, 0, False)
        keep = lax.dynamic_index_in_dim(pair, mine, 0, False)
        x = keep + swap(send, axis, size, bit)
    for axis, size, bit in reversed(steps):
        mine = (lax.axis_index(axis) >> bit) & 1
        came = swap(x, axis, size, bit)
        x = jnp.concatenate([jnp.where(mine == 0, x, came), jnp.where(mine == 0, came, x)], axis=0)
    return x


def solution(mesh):
    n_dp, n_seq = mesh.shape["dp"], mesh.shape["seq"]

    def shards(queries, keys, values, targets, q_map, k_map, doc_spans):
        hq, hd = q_map.shape[0], q_map.shape[1]
        hk = k_map.shape[0]
        group = hq // hk
        rows = queries.shape[1]
        count = rows // SPAN
        feats = 2 * hd
        tall = SPAN + PAD
        coef = 2.0 / math.sqrt(n_dp * n_seq * rows * hd)
        most = (3 * n_seq * count) // 8
        before = min(n_seq - 1, -(-(most - 1) // count))
        hops = max(1, before.bit_length())
        q2, t2 = queries[0], targets[0]
        k2, v2 = keys[0], values[0]
        state_t = jax.ShapeDtypeStruct((tall, feats), F32)

        out = whole_call(
            functools.partial(key_kernel, count),
            [
                jax.ShapeDtypeStruct((hk, rows, feats), BF16),
                jax.ShapeDtypeStruct((hk, count, tall, feats), F32),
            ]
            + [state_t] * hk,
            3,
            2 * hk * rows * hd * (hd + feats),
            doc_spans,
            k2,
            v2,
            k_map,
        )
        feat_k, blocks, tails = out[0], out[1], out[2:]

        def exchange(own, reverse):
            came = []
            for k in range(hops):
                hop = 1 << k
                if reverse:
                    perm = [(i, i - hop) for i in range(hop, n_seq)]
                else:
                    perm = [(i, i + hop) for i in range(n_seq - hop)]
                got = lax.ppermute(own, "seq", perm)
                came.append(got)
                if k < hops - 1:
                    own = whole_call(
                        functools.partial(join_kernel, count, hop, reverse),
                        state_t,
                        2,
                        own.size,
                        doc_spans,
                        own,
                        got,
                    )
            return came

        def middle(i, came):
            block = lambda shape, index: pl.BlockSpec(shape, index)
            state = block((tall, feats), lambda c: (0, 0))
            flops = 2 * group * rows * hd * (6 * feats + 3 * hd)
            return pl.pallas_call(
                functools.partial(middle_kernel, count, group, hops, coef),
                grid=(count,),
                in_specs=[
                    SMEM,
                    block((SPAN, group * hd), lambda c: (c, i)),
                    block((SPAN, group * hd), lambda c: (c, i)),
                    block((SPAN, hd), lambda c: (c, i)),
                    block((None, SPAN, feats), lambda c: (i, c, 0)),
                    block((group, hd, hd), lambda c: (i, 0, 0)),
                    block((None, count, tall, feats), lambda c: (i, 0, 0, 0)),
                ]
                + [state] * hops,
                out_specs=[
                    block((group, hd, hd), lambda c: (0, 0, 0)),
                    state,
                    block((None, tall, feats), lambda c: (c, 0, 0)),
                    block((None, SPAN, feats), lambda c: (c, 0, 0)),
                ],
                out_shape=[
                    jax.ShapeDtypeStruct((group, hd, hd), F32),
                    state_t,
                    jax.ShapeDtypeStruct((count, tall, feats), F32),
                    jax.ShapeDtypeStruct((count, SPAN, feats), F32),
                ],
                compiler_params=pltpu.CompilerParams(vmem_limit_bytes=LIMIT),
                cost_estimate=cost(flops, 4 * rows * group * hd),
            )(doc_spans, q2, t2, v2, feat_k, q_map, blocks, *came)

        def last(i, back, part, came):
            block = lambda shape, index: pl.BlockSpec(shape, index)
            return pl.pallas_call(
                functools.partial(last_kernel, count, hops),
                grid=(1,),
                in_specs=[
                    SMEM,
                    block((rows, hd), lambda c: (0, i)),
                    block((rows, hd), lambda c: (0, i)),
                    block((None, hd, hd), lambda c: (i, 0, 0)),
                    block((count, tall, feats), lambda c: (0, 0, 0)),
                    block((count, SPAN, feats), lambda c: (0, 0, 0)),
                ]
                + [block((tall, feats), lambda c: (0, 0))] * hops,
                out_specs=block((hd, hd), lambda c: (0, 0)),
                out_shape=jax.ShapeDtypeStruct((hd, hd), F32),
                compiler_params=pltpu.CompilerParams(vmem_limit_bytes=LIMIT),
                cost_estimate=cost(2 * rows * hd * 2 * feats, rows * feats * 4),
            )(doc_spans, k2, v2, k_map, back, part, *came)

        steps = [("dp", n_dp, b) for b in range(n_dp.bit_length() - 1)]
        steps += [("seq", n_seq, b) for b in range(n_seq.bit_length() - 1)]
        came = [exchange(tails[i], False) for i in range(hk)]
        mids = [middle(i, came[i]) for i in range(hk)]
        backs = [exchange(mids[i][1], True) for i in range(hk)]
        gq = [sum_all(mids[i][0].reshape(-1, hd), steps) for i in range(hk)]
        gk = [last(i, mids[i][2], mids[i][3], backs[i]) for i in range(hk)]
        grad_q = jnp.concatenate(gq, axis=0).reshape(hq, hd, hd)
        grad_k = sum_all(jnp.concatenate(gk, axis=0), steps).reshape(hk, hd, hd)
        return grad_q, grad_k

    in_specs = (
        P("dp", "seq", None),
        P("dp", "seq", None),
        P("dp", "seq", None),
        P("dp", "seq", None),
        P(),
        P(),
        P("dp", None),
    )
    return jax.shard_map(
        shards, mesh=mesh, in_specs=in_specs, out_specs=(P(), P()), check_vma=False
    )
```

profile of v0, /device:TPU:0, one launch (start us, length us, event | category | flops | bytes accessed | tf_op | source)
XLA Modules:
  0.0 169.1 jit_solution(7132769593580632163)
XLA Ops:
  4.1 2.6 %shard_map.86 = (bf16[4,256,256]{2,1,0:T(8,128)(2,1)S(1)}, f32[4,2,136,256]{3,2,1,0:T(8,128)S(1)}, f32[136,256]{1,0:T(8,128)}, f32[136,256]{1,0:T(8,128)}, f32[136,256]{1,0:T(8,128)}, /*index=5*/f32[136,256]{1,0:T(8,128)S(1)}) custom-call(s32[1,8]{1,0:T(1,128)S(1)} %copy-done.7, bf16[256,512]{1,0:T(8,128)(2,1)S(1)} %bitcast.142, ...), custom_call_target="tpu_custom_call" | custom-call | flops 100663296 | bytes 655392 | tf_op jit(solution)/shard_map/pallas_call | solution.py:189
  6.7 4.9 %collective-permute-start.36 = (f32[136,256]{1,0:T(8,128)S(1)}, f32[136,256]{1,0:T(8,128)S(1)}, u32[]{:S(2)}, u32[]{:S(2)}) collective-permute-start(f32[136,256]{1,0:T(8,128)S(1)} %get-tuple-element.32.own_ref), channel_id=1, source_target_pairs={{0,1},{1,2},{2,3},{3,4},{4,5},{5,6},{6,7},{8,9},{9,10},{10,11},{11... | collective-permute-start | bytes 417800 | tf_op jit(solution)/shard_map/ppermute | solution.py:259
  11.6 3.4 %collective-permute-start = (f32[136,256]{1,0:T(8,128)}, f32[136,256]{1,0:T(8,128)S(1)}, u32[]{:S(2)}, u32[]{:S(2)}) collective-permute-start(f32[136,256]{1,0:T(8,128)} %get-tuple-element.26.own_ref), channel_id=1, source_target_pairs={{0,1},{1,2},{2,3},{3,4},{4,5},{5,6},{6,7},{8,9},{9,10},{10,11},{11... | collective-permute-start | bytes 417800 | tf_op jit(solution)/shard_map/ppermute | solution.py:259
  15.0 3.4 %collective-permute-start.12 = (f32[136,256]{1,0:T(8,128)}, f32[136,256]{1,0:T(8,128)S(1)}, u32[]{:S(2)}, u32[]{:S(2)}) collective-permute-start(f32[136,256]{1,0:T(8,128)} %get-tuple-element.28.own_ref), channel_id=1, source_target_pairs={{0,1},{1,2},{2,3},{3,4},{4,5},{5,6},{6,7},{8,9},{9,10},{10,11},{11... | collective-permute-start | bytes 417800 | tf_op jit(solution)/shard_map/ppermute | solution.py:259
  18.5 3.4 %collective-permute-start.24 = (f32[136,256]{1,0:T(8,128)}, f32[136,256]{1,0:T(8,128)S(1)}, u32[]{:S(2)}, u32[]{:S(2)}) collective-permute-start(f32[136,256]{1,0:T(8,128)} %get-tuple-element.30.own_ref), channel_id=1, source_target_pairs={{0,1},{1,2},{2,3},{3,4},{4,5},{5,6},{6,7},{8,9},{9,10},{10,11},{11... | collective-permute-start | bytes 417800 | tf_op jit(solution)/shard_map/ppermute | solution.py:259
  23.1 4.1 %collective-permute-start.37 = (f32[136,256]{1,0:T(8,128)}, f32[136,256]{1,0:T(8,128)}, u32[]{:S(2)}, u32[]{:S(2)}) collective-permute-start(f32[136,256]{1,0:T(8,128)} %shard_map.93), channel_id=1, source_target_pairs={{0,2},{1,3},{2,4},{3,5},{4,6},{5,7},{8,10},{9,11},{10,12},{11,13},... | collective-permute-start | bytes 417800 | tf_op jit(solution)/shard_map/ppermute | solution.py:259
  36.1 5.3 %shard_map.94 = (f32[8,128,128]{2,1,0:T(8,128)S(1)}, f32[136,256]{1,0:T(8,128)S(1)}, f32[2,136,256]{2,1,0:T(8,128)S(1)}, f32[2,128,256]{2,1,0:T(8,128)S(1)}) custom-call(s32[1,8]{1,0:T(1,128)S(1)} %copy-done.8, bf16[256,4096]{1,0:T(8,128)(2,1)} %bitcast.155, bf16[256,4096]{1,0:T(8,128)(2,1)} %bitcast.159, bf16[256,512]{1,0:T(8,128)(2,1)S(1)} %bitcast.134, ...), custom_call_target="tpu_custom_call" | custom-call | flops 1006632960 | bytes 1048576 | tf_op jit(solution)/shard_map/pallas_call | solution.py:277
  42.8 5.2 %shard_map.92 = (f32[8,128,128]{2,1,0:T(8,128)S(1)}, f32[136,256]{1,0:T(8,128)S(1)}, f32[2,136,256]{2,1,0:T(8,128)S(1)}, f32[2,128,256]{2,1,0:T(8,128)S(1)}) custom-call(s32[1,8]{1,0:T(1,128)S(1)} %copy-done.8, bf16[256,4096]{1,0:T(8,128)(2,1)} %bitcast.156, bf16[256,4096]{1,0:T(8,128)(2,1)} %bitcast.160, bf16[256,512]{1,0:T(8,128)(2,1)S(1)} %bitcast.135, ...), custom_call_target="tpu_custom_call" | custom-call | flops 1006632960 | bytes 1048576 | tf_op jit(solution)/shard_map/pallas_call | solution.py:277
  49.3 5.2 %shard_map.90 = (f32[8,128,128]{2,1,0:T(8,128)S(1)}, f32[136,256]{1,0:T(8,128)S(1)}, f32[2,136,256]{2,1,0:T(8,128)S(1)}, f32[2,128,256]{2,1,0:T(8,128)S(1)}) custom-call(s32[1,8]{1,0:T(1,128)S(1)} %copy-done.8, bf16[256,4096]{1,0:T(8,128)(2,1)} %bitcast.157, bf16[256,4096]{1,0:T(8,128)(2,1)} %bitcast.161, bf16[256,512]{1,0:T(8,128)(2,1)S(1)} %bitcast.136, ...), custom_call_target="tpu_custom_call" | custom-call | flops 1006632960 | bytes 1048576 | tf_op jit(solution)/shard_map/pallas_call | solution.py:277
  55.9 5.2 %shard_map.88 = (f32[8,128,128]{2,1,0:T(8,128)S(1)}, f32[136,256]{1,0:T(8,128)S(1)}, f32[2,136,256]{2,1,0:T(8,128)S(1)}, f32[2,128,256]{2,1,0:T(8,128)S(1)}) custom-call(s32[1,8]{1,0:T(1,128)S(1)} %copy-done.8, bf16[256,4096]{1,0:T(8,128)(2,1)} %bitcast.158, bf16[256,4096]{1,0:T(8,128)(2,1)} %bitcast.162, bf16[256,512]{1,0:T(8,128)(2,1)S(1)} %bitcast.137, ...), custom_call_target="tpu_custom_call" | custom-call | flops 1006632960 | bytes 1048576 | tf_op jit(solution)/shard_map/pallas_call | solution.py:277
  65.5 5.8 %collective-permute-done.48.came_ref.refs_6_ = f32[136,256]{1,0:T(8,128)S(1)} collective-permute-done((f32[136,256]{1,0:T(8,128)S(1)}, f32[136,256]{1,0:T(8,128)S(1)}, u32[]{:S(2)}, u32[]{:S(2)}) %collective-permute-start.48) | collective-permute-done | bytes 139296 | tf_op jit(solution)/shard_map/ppermute | solution.py:259
  90.3 2.7 %collective-permute-start.40 = (f32[128,128]{1,0:T(8,128)S(1)}, f32[128,128]{1,0:T(8,128)S(1)}, u32[]{:S(2)}, u32[]{:S(2)}) collective-permute-start(f32[128,128]{1,0:T(8,128)S(1)} %dynamic-slice_bitcast_fusion.10), channel_id=1, source_target_pairs={{0,1},{1,0},{2,3},{3,2},{4,5},{5,4},{6,7},{7,6},{8,9},{9,8},{10,11... | collective-permute-start | bytes 196616 | tf_op jit(solution)/shard_map/ppermute | solution.py:199
  96.1 4.3 %collective-permute-start.41 = (f32[64,128]{1,0:T(8,128)S(1)}, f32[64,128]{1,0:T(8,128)S(1)}, u32[]{:S(2)}, u32[]{:S(2)}) collective-permute-start(f32[64,128]{1,0:T(8,128)S(1)} %dynamic-slice_bitcast_fusion.15), channel_id=1, source_target_pairs={{0,2},{1,3},{2,0},{3,1},{4,6},{5,7},{6,4},{7,5},{8,10},{9,11},{10,... | collective-permute-start | bytes 98312 | tf_op jit(solution)/shard_map/ppermute | solution.py:199
  104.0 3.5 %collective-permute-start.42 = (f32[32,128]{1,0:T(8,128)S(1)}, f32[32,128]{1,0:T(8,128)S(1)}, u32[]{:S(2)}, u32[]{:S(2)}) collective-permute-start(f32[32,128]{1,0:T(8,128)S(1)} %dynamic-slice_bitcast_fusion.20), channel_id=1, source_target_pairs={{0,4},{1,5},{2,6},{3,7},{4,0},{5,1},{6,2},{7,3},{8,12},{9,13},{10,... | collective-permute-start | bytes 49160 | tf_op jit(solution)/shard_map/ppermute | solution.py:199
  107.6 3.0 %collective-permute-start.6 = (f32[32,128]{1,0:T(8,128)S(1)}, f32[32,128]{1,0:T(8,128)S(1)}, u32[]{:S(2)}, u32[]{:S(2)}) collective-permute-start(f32[32,128]{1,0:T(8,128)S(1)} %dynamic-slice_bitcast_fusion.23), channel_id=1, source_target_pairs={{0,4},{1,5},{2,6},{3,7},{4,0},{5,1},{6,2},{7,3},{8,12},{9,13},{10,... | collective-permute-start | bytes 49160 | tf_op jit(solution)/shard_map/ppermute | solution.py:199
  110.7 3.0 %collective-permute-start.43 = (f32[32,128]{1,0:T(8,128)S(1)}, f32[32,128]{1,0:T(8,128)S(1)}, u32[]{:S(2)}, u32[]{:S(2)}) collective-permute-start(f32[32,128]{1,0:T(8,128)S(1)} %bitcast_add_fusion.20), channel_id=1, source_target_pairs={{0,4},{1,5},{2,6},{3,7},{4,0},{5,1},{6,2},{7,3},{8,12},{9,13},{10,... | collective-permute-start | bytes 49160 | tf_op jit(solution)/shard_map/ppermute | solution.py:199
  115.5 2.9 %collective-permute-start.7 = (f32[32,128]{1,0:T(8,128)S(1)}, f32[32,128]{1,0:T(8,128)S(1)}, u32[]{:S(2)}, u32[]{:S(2)}) collective-permute-start(f32[32,128]{1,0:T(8,128)S(1)} %bitcast_add_fusion.23), channel_id=1, source_target_pairs={{0,4},{1,5},{2,6},{3,7},{4,0},{5,1},{6,2},{7,3},{8,12},{9,13},{10,... | collective-permute-start | bytes 49160 | tf_op jit(solution)/shard_map/ppermute | solution.py:199
  120.8 2.9 %collective-permute-start.60 = (f32[16,128]{1,0:T(8,128)S(1)}, f32[16,128]{1,0:T(8,128)S(1)}, u32[]{:S(2)}, u32[]{:S(2)}) collective-permute-start(f32[16,128]{1,0:T(8,128)S(1)} %fusion.2), channel_id=1, source_target_pairs={{0,4},{1,5},{2,6},{3,7},{4,0},{5,1},{6,2},{7,3},{8,12},{9,13},{10,... | collective-permute-start | bytes 24584 | tf_op jit(solution)/shard_map/ppermute | solution.py:199
  125.4 2.9 %collective-permute-start.61 = (f32[16,128]{1,0:T(8,128)S(1)}, f32[16,128]{1,0:T(8,128)S(1)}, u32[]{:S(2)}, u32[]{:S(2)}) collective-permute-start(f32[16,128]{1,0:T(8,128)S(1)} %fusion.1), channel_id=1, source_target_pairs={{0,4},{1,5},{2,6},{3,7},{4,0},{5,1},{6,2},{7,3},{8,12},{9,13},{10,... | collective-permute-start | bytes 24584 | tf_op jit(solution)/shard_map/ppermute | solution.py:199
  130.0 3.8 %collective-permute-start.62 = (f32[32,128]{1,0:T(8,128)S(1)}, f32[32,128]{1,0:T(8,128)S(1)}, u32[]{:S(2)}, u32[]{:S(2)}) collective-permute-start(f32[32,128]{1,0:T(8,128)S(1)} %pad_maximum_fusion.21), channel_id=1, source_target_pairs={{0,2},{1,3},{2,0},{3,1},{4,6},{5,7},{6,4},{7,5},{8,10},{9,11},{10,... | collective-permute-start | bytes 49160 | tf_op jit(solution)/shard_map/ppermute | solution.py:199
  137.4 4.4 %collective-permute-start.63 = (f32[64,128]{1,0:T(8,128)S(1)}, f32[64,128]{1,0:T(8,128)S(1)}, u32[]{:S(2)}, u32[]{:S(2)}) collective-permute-start(f32[64,128]{1,0:T(8,128)S(1)} %pad_maximum_fusion.20), channel_id=1, source_target_pairs={{0,1},{1,0},{2,3},{3,2},{4,5},{5,4},{6,7},{7,6},{8,9},{9,8},{10,11... | collective-permute-start | bytes 98312 | tf_op jit(solution)/shard_map/ppermute | solution.py:199
  145.9 4.5 %collective-permute-start.64 = (f32[128,128]{1,0:T(8,128)S(1)}, f32[128,128]{1,0:T(8,128)S(1)}, u32[]{:S(2)}, u32[]{:S(2)}) collective-permute-start(f32[128,128]{1,0:T(8,128)S(1)} %pad_maximum_fusion.15), channel_id=1, source_target_pairs={{0,16},{8,24},{16,0},{24,8},{1,17},{9,25},{17,1},{25,9},{2,18},{10... | collective-permute-start | bytes 196616 | tf_op jit(solution)/shard_map/ppermute | solution.py:199
  155.2 5.5 %collective-permute-start.65 = (f32[256,128]{1,0:T(8,128)S(1)}, f32[256,128]{1,0:T(8,128)S(1)}, u32[]{:S(2)}, u32[]{:S(2)}) collective-permute-start(f32[256,128]{1,0:T(8,128)S(1)} %pad_maximum_fusion.10), channel_id=1, source_target_pairs={{0,8},{8,0},{16,24},{24,16},{1,9},{9,1},{17,25},{25,17},{2,10},{10... | collective-permute-start | bytes 393224 | tf_op jit(solution)/shard_map/ppermute | solution.py:199
  163.7 2.2 %collective-permute-done.22 = f32[256,128]{1,0:T(8,128)S(1)} collective-permute-done((f32[256,128]{1,0:T(8,128)S(1)}, f32[256,128]{1,0:T(8,128)S(1)}, u32[]{:S(2)}, u32[]{:S(2)}) %collective-permute-start.22) | collective-permute-done | bytes 131104 | tf_op jit(solution)/shard_map/ppermute | solution.py:199
  (246 shorter events, 73.1 us)
Async XLA Ops:
  6.7 15.2 %collective-permute-start.36 = (f32[136,256]{1,0:T(8,128)S(1)}, f32[136,256]{1,0:T(8,128)S(1)}, u32[]{:S(2)}, u32[]{:S(2)}) collective-permute-start(f32[136,256]{1,0:T(8,128)S(1)} %get-tuple-element.32.own_ref), channel_id=1, source_target_pairs={{0,1},{1,2},{2,3},{3,4},{4,5},{5,6},{6,7},{8,9},{9,10},{10,11},{11... | collective-permute-start | bytes 417800 | tf_op jit(solution)/shard_map/ppermute | solution.py:259
  11.6 15.7 %collective-permute-start = (f32[136,256]{1,0:T(8,128)}, f32[136,256]{1,0:T(8,128)S(1)}, u32[]{:S(2)}, u32[]{:S(2)}) collective-permute-start(f32[136,256]{1,0:T(8,128)} %get-tuple-element.26.own_ref), channel_id=1, source_target_pairs={{0,1},{1,2},{2,3},{3,4},{4,5},{5,6},{6,7},{8,9},{9,10},{10,11},{11... | collective-permute-start | bytes 417800 | tf_op jit(solution)/shard_map/ppermute | solution.py:259
  15.0 15.2 %collective-permute-start.12 = (f32[136,256]{1,0:T(8,128)}, f32[136,256]{1,0:T(8,128)S(1)}, u32[]{:S(2)}, u32[]{:S(2)}) collective-permute-start(f32[136,256]{1,0:T(8,128)} %get-tuple-element.28.own_ref), channel_id=1, source_target_pairs={{0,1},{1,2},{2,3},{3,4},{4,5},{5,6},{6,7},{8,9},{9,10},{10,11},{11... | collective-permute-start | bytes 417800 | tf_op jit(solution)/shard_map/ppermute | solution.py:259
  18.5 14.7 %collective-permute-start.24 = (f32[136,256]{1,0:T(8,128)}, f32[136,256]{1,0:T(8,128)S(1)}, u32[]{:S(2)}, u32[]{:S(2)}) collective-permute-start(f32[136,256]{1,0:T(8,128)} %get-tuple-element.30.own_ref), channel_id=1, source_target_pairs={{0,1},{1,2},{2,3},{3,4},{4,5},{5,6},{6,7},{8,9},{9,10},{10,11},{11... | collective-permute-start | bytes 417800 | tf_op jit(solution)/shard_map/ppermute | solution.py:259
  23.1 12.9 %collective-permute-start.37 = (f32[136,256]{1,0:T(8,128)}, f32[136,256]{1,0:T(8,128)}, u32[]{:S(2)}, u32[]{:S(2)}) collective-permute-start(f32[136,256]{1,0:T(8,128)} %shard_map.93), channel_id=1, source_target_pairs={{0,2},{1,3},{2,4},{3,5},{4,6},{5,7},{8,10},{9,11},{10,12},{11,13},... | collective-permute-start | bytes 417800 | tf_op jit(solution)/shard_map/ppermute | solution.py:259
  28.9 27.1 %collective-permute-start.1 = (f32[136,256]{1,0:T(8,128)S(1)}, f32[136,256]{1,0:T(8,128)S(1)}, u32[]{:S(2)}, u32[]{:S(2)}) collective-permute-start(f32[136,256]{1,0:T(8,128)S(1)} %shard_map.87), channel_id=1, source_target_pairs={{0,2},{1,3},{2,4},{3,5},{4,6},{5,7},{8,10},{9,11},{10,12},{11,13},... | collective-permute-start | bytes 417800 | tf_op jit(solution)/shard_map/ppermute | solution.py:259
  31.2 18.1 %collective-permute-start.13 = (f32[136,256]{1,0:T(8,128)S(1)}, f32[136,256]{1,0:T(8,128)S(1)}, u32[]{:S(2)}, u32[]{:S(2)}) collective-permute-start(f32[136,256]{1,0:T(8,128)S(1)} %shard_map.89), channel_id=1, source_target_pairs={{0,2},{1,3},{2,4},{3,5},{4,6},{5,7},{8,10},{9,11},{10,12},{11,13},... | collective-permute-start | bytes 417800 | tf_op jit(solution)/shard_map/ppermute | solution.py:259
  41.4 21.2 %collective-permute-start.54 = (f32[136,256]{1,0:T(8,128)S(1)}, f32[136,256]{1,0:T(8,128)S(1)}, u32[]{:S(2)}, u32[]{:S(2)}) collective-permute-start(f32[136,256]{1,0:T(8,128)S(1)} %get-tuple-element.45.own_ref), channel_id=1, source_target_pairs={{1,0},{2,1},{3,2},{4,3},{5,4},{6,5},{7,6},{9,8},{10,9},{11,10},{12... | collective-permute-start | bytes 417800 | tf_op jit(solution)/shard_map/ppermute | solution.py:259
  42.7 30.5 %collective-permute-start.38 = (f32[512,128]{1,0:T(8,128)S(1)}, f32[512,128]{1,0:T(8,128)S(1)}, u32[]{:S(2)}, u32[]{:S(2)}) collective-permute-start(f32[512,128]{1,0:T(8,128)S(1)} %dynamic-slice_bitcast_fusion), channel_id=1, source_target_pairs={{0,8},{8,0},{16,24},{24,16},{1,9},{9,1},{17,25},{25,17},{2,10},{10... | collective-permute-start | bytes 786440 | tf_op jit(solution)/shard_map/ppermute | solution.py:199
  48.0 15.6 %collective-permute-start.52 = (f32[136,256]{1,0:T(8,128)S(1)}, f32[136,256]{1,0:T(8,128)S(1)}, u32[]{:S(2)}, u32[]{:S(2)}) collective-permute-start(f32[136,256]{1,0:T(8,128)S(1)} %get-tuple-element.42.own_ref), channel_id=1, source_target_pairs={{1,0},{2,1},{3,2},{4,3},{5,4},{6,5},{7,6},{9,8},{10,9},{11,10},{12... | collective-permute-start | bytes 417800 | tf_op jit(solution)/shard_map/ppermute | solution.py:259
  62.5 12.1 %collective-permute-start.26 = (f32[512,128]{1,0:T(8,128)S(1)}, f32[512,128]{1,0:T(8,128)S(1)}, u32[]{:S(2)}, u32[]{:S(2)}) collective-permute-start(f32[512,128]{1,0:T(8,128)S(1)} %dynamic-slice_bitcast_fusion.1), channel_id=1, source_target_pairs={{0,8},{8,0},{16,24},{24,16},{1,9},{9,1},{17,25},{25,17},{2,10},{10... | collective-permute-start | bytes 786440 | tf_op jit(solution)/shard_map/ppermute | solution.py:199
  63.7 12.4 %collective-permute-start.2 = (f32[512,128]{1,0:T(8,128)S(1)}, f32[512,128]{1,0:T(8,128)S(1)}, u32[]{:S(2)}, u32[]{:S(2)}) collective-permute-start(f32[512,128]{1,0:T(8,128)S(1)} %dynamic-slice_bitcast_fusion.3), channel_id=1, source_target_pairs={{0,8},{8,0},{16,24},{24,16},{1,9},{9,1},{17,25},{25,17},{2,10},{10... | collective-permute-start | bytes 786440 | tf_op jit(solution)/shard_map/ppermute | solution.py:199
  64.4 13.2 %collective-permute-start.14 = (f32[512,128]{1,0:T(8,128)S(1)}, f32[512,128]{1,0:T(8,128)S(1)}, u32[]{:S(2)}, u32[]{:S(2)}) collective-permute-start(f32[512,128]{1,0:T(8,128)S(1)} %dynamic-slice_bitcast_fusion.2), channel_id=1, source_target_pairs={{0,8},{8,0},{16,24},{24,16},{1,9},{9,1},{17,25},{25,17},{2,10},{10... | collective-permute-start | bytes 786440 | tf_op jit(solution)/shard_map/ppermute | solution.py:199
  74.7 11.6 %collective-permute-start.51 = (f32[136,256]{1,0:T(8,128)S(1)}, f32[136,256]{1,0:T(8,128)S(1)}, u32[]{:S(2)}, u32[]{:S(2)}) collective-permute-start(f32[136,256]{1,0:T(8,128)S(1)} %shard_map.97), channel_id=1, source_target_pairs={{2,0},{3,1},{4,2},{5,3},{6,4},{7,5},{10,8},{11,9},{12,10},{13,11},... | collective-permute-start | bytes 417800 | tf_op jit(solution)/shard_map/ppermute | solution.py:259
  76.1 12.9 %collective-permute-start.49 = (f32[136,256]{1,0:T(8,128)S(1)}, f32[136,256]{1,0:T(8,128)S(1)}, u32[]{:S(2)}, u32[]{:S(2)}) collective-permute-start(f32[136,256]{1,0:T(8,128)S(1)} %shard_map.95), channel_id=1, source_target_pairs={{2,0},{3,1},{4,2},{5,3},{6,4},{7,5},{10,8},{11,9},{12,10},{13,11},... | collective-permute-start | bytes 417800 | tf_op jit(solution)/shard_map/ppermute | solution.py:259
  77.6 12.6 %collective-permute-start.39 = (f32[256,128]{1,0:T(8,128)S(1)}, f32[256,128]{1,0:T(8,128)S(1)}, u32[]{:S(2)}, u32[]{:S(2)}) collective-permute-start(f32[256,128]{1,0:T(8,128)S(1)} %dynamic-slice_bitcast_fusion.5), channel_id=1, source_target_pairs={{0,16},{8,24},{16,0},{24,8},{1,17},{9,25},{17,1},{25,9},{2,18},{10... | collective-permute-start | bytes 393224 | tf_op jit(solution)/shard_map/ppermute | solution.py:199
  79.5 13.5 %collective-permute-start.27 = (f32[256,128]{1,0:T(8,128)S(1)}, f32[256,128]{1,0:T(8,128)S(1)}, u32[]{:S(2)}, u32[]{:S(2)}) collective-permute-start(f32[256,128]{1,0:T(8,128)S(1)} %dynamic-slice_bitcast_fusion.6), channel_id=1, source_target_pairs={{0,16},{8,24},{16,0},{24,8},{1,17},{9,25},{17,1},{25,9},{2,18},{10... | collective-permute-start | bytes 393224 | tf_op jit(solution)/shard_map/ppermute | solution.py:199
  118.6 15.2 %collective-permute-start.44 = (f32[64,128]{1,0:T(8,128)S(1)}, f32[64,128]{1,0:T(8,128)S(1)}, u32[]{:S(2)}, u32[]{:S(2)}) collective-permute-start(f32[64,128]{1,0:T(8,128)S(1)} %pad_maximum_fusion.19), channel_id=1, source_target_pairs={{0,2},{1,3},{2,0},{3,1},{4,6},{5,7},{6,4},{7,5},{8,10},{9,11},{10,... | collective-permute-start | bytes 98312 | tf_op jit(solution)/shard_map/ppermute | solution.py:199
  119.0 16.7 %collective-permute-start.32 = (f32[64,128]{1,0:T(8,128)S(1)}, f32[64,128]{1,0:T(8,128)S(1)}, u32[]{:S(2)}, u32[]{:S(2)}) collective-permute-start(f32[64,128]{1,0:T(8,128)S(1)} %pad_maximum_fusion.18), channel_id=1, source_target_pairs={{0,2},{1,3},{2,0},{3,1},{4,6},{5,7},{6,4},{7,5},{8,10},{9,11},{10,... | collective-permute-start | bytes 98312 | tf_op jit(solution)/shard_map/ppermute | solution.py:199
  123.7 18.1 %collective-permute-start.8 = (f32[64,128]{1,0:T(8,128)S(1)}, f32[64,128]{1,0:T(8,128)S(1)}, u32[]{:S(2)}, u32[]{:S(2)}) collective-permute-start(f32[64,128]{1,0:T(8,128)S(1)} %pad_maximum_fusion.16), channel_id=1, source_target_pairs={{0,2},{1,3},{2,0},{3,1},{4,6},{5,7},{6,4},{7,5},{8,10},{9,11},{10,... | collective-permute-start | bytes 98312 | tf_op jit(solution)/shard_map/ppermute | solution.py:199
  128.3 15.5 %collective-permute-start.20 = (f32[64,128]{1,0:T(8,128)S(1)}, f32[64,128]{1,0:T(8,128)S(1)}, u32[]{:S(2)}, u32[]{:S(2)}) collective-permute-start(f32[64,128]{1,0:T(8,128)S(1)} %pad_maximum_fusion.17), channel_id=1, source_target_pairs={{0,2},{1,3},{2,0},{3,1},{4,6},{5,7},{6,4},{7,5},{8,10},{9,11},{10,... | collective-permute-start | bytes 98312 | tf_op jit(solution)/shard_map/ppermute | solution.py:199
  133.8 16.6 %collective-permute-start.45 = (f32[128,128]{1,0:T(8,128)S(1)}, f32[128,128]{1,0:T(8,128)S(1)}, u32[]{:S(2)}, u32[]{:S(2)}) collective-permute-start(f32[128,128]{1,0:T(8,128)S(1)} %pad_maximum_fusion.14), channel_id=1, source_target_pairs={{0,1},{1,0},{2,3},{3,2},{4,5},{5,4},{6,7},{7,6},{8,9},{9,8},{10,11... | collective-permute-start | bytes 196616 | tf_op jit(solution)/shard_map/ppermute | solution.py:199
  135.8 16.6 %collective-permute-start.33 = (f32[128,128]{1,0:T(8,128)S(1)}, f32[128,128]{1,0:T(8,128)S(1)}, u32[]{:S(2)}, u32[]{:S(2)}) collective-permute-start(f32[128,128]{1,0:T(8,128)S(1)} %pad_maximum_fusion.13), channel_id=1, source_target_pairs={{0,1},{1,0},{2,3},{3,2},{4,5},{5,4},{6,7},{7,6},{8,9},{9,8},{10,11... | collective-permute-start | bytes 196616 | tf_op jit(solution)/shard_map/ppermute | solution.py:199
  154.6 11.3 %collective-permute-start.22 = (f32[256,128]{1,0:T(8,128)S(1)}, f32[256,128]{1,0:T(8,128)S(1)}, u32[]{:S(2)}, u32[]{:S(2)}) collective-permute-start(f32[256,128]{1,0:T(8,128)S(1)} %pad_maximum_fusion.7), channel_id=1, source_target_pairs={{0,16},{8,24},{16,0},{24,8},{1,17},{9,25},{17,1},{25,9},{2,18},{10... | collective-permute-start | bytes 393224 | tf_op jit(solution)/shard_map/ppermute | solution.py:199
  (52 other events, 409.4 us)
where the time goes:
time: 170 us; the launch traced here: 169 us
  starting transfers between devices  107 us (63%)
  Pallas kernels  34.5 us (20%)
  waiting for transfers between devices  18.7 us (11%)
  local copies, waits for them, and re-layouts  5.81 us (3%)
  between operations  1.78 us (1%)
  other arithmetic  1.72 us (1%)
    ppermute x50, starting transfers between devices, swap(): return lax.ppermute(x, axis, [(i, i ^ 1 << bit) for i in range(size)])  71.4 us
    ppermute x16, starting transfers between devices, exchange(): got = lax.ppermute(own, 'seq', perm)  35.1 us
    pallas_call x4, Pallas kernels, middle(): pl.pallas_call(functools.partial(middle_kernel, count, group, hops, coef)...  21 us
    ppermute x50, waiting for transfers between devices, swap(): return lax.ppermute(x, axis, [(i, i ^ 1 << bit) for i in range(size)])  11.1 us
    pallas_call x9, Pallas kernels, whole_call(): pl.pallas_call(body, out_shape=out_shape, in_specs=[SMEM] + [pl.BlockSpec...  8.99 us
    ppermute x16, waiting for transfers between devices, exchange(): got = lax.ppermute(own, 'seq', perm)  7.61 us
    unnamed x20, local copies, waits for them, and re-layouts  5.44 us
    pallas_call x4, Pallas kernels, last(): pl.pallas_call(functools.partial(last_kernel, count, hops), grid=(1,), in...  4.55 us
  transfers between devices with their start and end apart: 66, of which 12 were waited for; matrix products, arithmetic and copies ran while one was open for 1% of the time, Pallas kernels for 19%

commit v1 on v0

--- a/solution.py
+++ b/solution.py
@@ -10,6 +10,7 @@
 
 SPAN = 128
 PAD = 8
+WHOLE = 256
 F32 = jnp.float32
 BF16 = jnp.bfloat16
 NN = (((1,), (0,)), ((), ()))
@@ -50,27 +51,28 @@
     return (first - second).astype(BF16)
 
 
-def key_kernel(count, spans_ref, k_ref, v_ref, w_ref, feat_ref, block_ref, *tail_refs):
-    width = w_ref.shape[-1]
-    heads = w_ref.shape[0]
+def key_kernel(count, parts, spans_ref, k_ref, v_ref, w_ref, feat_ref, block_ref, *tail_refs):
+    head = pl.program_id(0)
     first = lax.axis_index("seq") * count
     starts = [bounds(spans_ref, first + c)[0] for c in range(count)]
-    for i in range(heads):
-        cols = slice(i * width, (i + 1) * width)
-        up, low = soft_pair(dot(k_ref[:, cols], w_ref[i], NN))
-        feat = jnp.concatenate([up, low], axis=-1).astype(BF16)
-        feat_ref[i] = feat
-        tail = None
-        for c in range(count):
-            rows = slice(c * SPAN, (c + 1) * SPAN)
-            state = dot(v_ref[rows, cols], feat[rows], TN)
-            norm = jnp.sum(feat[rows].astype(F32), axis=0, keepdims=True)
-            norm = jnp.broadcast_to(norm, (PAD, norm.shape[1]))
-            both = jnp.concatenate([state, norm], axis=0)
-            block_ref[i, c] = both
-            part = flag(starts[c] == starts[count - 1]) * both
-            tail = part if tail is None else tail + part
-        tail_refs[i][...] = tail
+    up, low = soft_pair(dot(k_ref[...], w_ref[...], NN))
+    feat = jnp.concatenate([up, low], axis=-1).astype(BF16)
+    feat_ref[...] = feat
+    tail = None
+    for c in range(count):
+        rows = slice(c * SPAN, (c + 1) * SPAN)
+        state = dot(v_ref[rows], feat[rows], TN)
+        norm = jnp.sum(feat[rows].astype(F32), axis=0, keepdims=True)
+        norm = jnp.broadcast_to(norm, (PAD, norm.shape[1]))
+        both = jnp.concatenate([state, norm], axis=0)
+        block_ref[c] = both
+        part = flag(starts[c] == starts[count - 1]) * both
+        tail = part if tail is None else tail + part
+    for (low_head, high_head), tail_ref in zip(parts, tail_refs):
+
+        @pl.when(jnp.logical_and(head >= low_head, head < high_head))
+        def _():
+            tail_ref[...] = tail
 
 
 def join_kernel(count, hop, reverse, spans_ref, own_ref, came_ref, out_ref):
@@ -87,9 +89,9 @@
 def middle_kernel(count, group, hops, coef, *refs):
     spans_ref, q_ref, t_ref, v_ref, feat_ref, w_ref, block_ref = refs[:7]
     came = refs[7 : 7 + hops]
-    gq_ref, head_ref, back_ref, part_ref = refs[7 + hops : 11 + hops]
+    keep_ref, send_ref, head_ref, back_ref, part_ref = refs[7 + hops : 12 + hops]
     width = w_ref.shape[-1]
-    c = pl.program_id(0)
+    c = pl.program_id(1)
     place = lax.axis_index("seq")
     first = place * count
     start_first, _ = bounds(spans_ref, first)
@@ -134,18 +136,26 @@
     d_map = map_grad(up, low, d_feat[:, :width], d_feat[:, width:])
     grads = [dot(qs[h], d_map[h * SPAN : (h + 1) * SPAN], TN) for h in range(group)]
     mine = flag(start == start_first) * back
+    half = group // 2
+    core = lax.axis_index("dp") & 1
+
+    def put(ref, base, add):
+        for h in range(half):
+            grad = jnp.where(core == 0, grads[base + h], grads[half - base + h])
+            rows = slice(h * width, (h + 1) * width)
+            ref[rows] = ref[rows] + grad if add else grad
 
     @pl.when(c == 0)
     def _():
         head_ref[...] = mine
-        for h in range(group):
-            gq_ref[h] = grads[h]
+        put(keep_ref, 0, False)
+        put(send_ref, half, False)
 
     @pl.when(c > 0)
     def _():
         head_ref[...] += mine
-        for h in range(group):
-            gq_ref[h] += grads[h]
+        put(keep_ref, 0, True)
+        put(send_ref, half, True)
 
 
 def last_kernel(count, hops, *refs):
@@ -182,6 +192,7 @@
 
 SMEM = pl.BlockSpec(memory_space=pltpu.SMEM)
 LIMIT = 48 << 20
+LATE = 400
 
 
 def whole_call(body, out_shape, n_vmem, flops, *args):
@@ -195,22 +206,121 @@
     )(*args)
 
 
-def swap(x, axis, size, bit):
-    return lax.ppermute(x, axis, [(i, i ^ (1 << bit)) for i in range(size)])
-
-
-def sum_all(x, steps):
-    for axis, size, bit in steps:
-        mine = (lax.axis_index(axis) >> bit) & 1
-        pair = x.reshape(2, x.shape[0] // 2, x.shape[1])
-        send = lax.dynamic_index_in_dim(pair, 1 - mine, 0, False)
-        keep = lax.dynamic_index_in_dim(pair, mine, 0, False)
-        x = keep + swap(send, axis, size, bit)
-    for axis, size, bit in reversed(steps):
-        mine = (lax.axis_index(axis) >> bit) & 1
-        came = swap(x, axis, size, bit)
-        x = jnp.concatenate([jnp.where(mine == 0, x, came), jnp.where(mine == 0, came, x)], axis=0)
-    return x
+def index_in(stage):
+    place = jnp.int32(0)
+    for k, (axis, bit) in enumerate(stage):
+        place = place + (((lax.axis_index(axis) >> bit) & 1) << k)
+    return place
+
+
+def split_kernel(stage, layout, *refs):
+    pieces = 1 << len(stage)
+    outs = refs[len(refs) - pieces :]
+    mine = index_in(stage)
+    for m, out in enumerate(outs):
+        at, used = 0, 0
+        for addends, rows in layout:
+            size = rows // pieces
+            start = 0 if pieces == 1 else pl.multiple_of((mine ^ m) * size, PAD)
+            total = refs[used][pl.ds(start, size), :]
+            for ref in refs[used + 1 : used + addends]:
+                total = total + ref[pl.ds(start, size), :]
+            out[at : at + size] = total
+            at, used = at + size, used + addends
+
+
+def join_pieces_kernel(stage, layout, *refs):
+    pieces = 1 << len(stage)
+    out = refs[pieces]
+    mine = index_in(stage)
+    for m in range(pieces):
+        at, base = 0, 0
+        for _, rows in layout:
+            size = rows // pieces
+            start = pl.multiple_of(base + (mine ^ m) * size, PAD)
+            out[pl.ds(start, size), :] = refs[m][at : at + size]
+            at, base = at + size, base + rows
+
+
+def plain_call(body, out_shape, *args):
+    moved = 2 * sum(a.size * a.dtype.itemsize for a in args)
+    return pl.pallas_call(
+        body,
+        out_shape=out_shape,
+        in_specs=[pl.BlockSpec(memory_space=pltpu.VMEM)] * len(args),
+        compiler_params=pltpu.CompilerParams(vmem_limit_bytes=LIMIT),
+        cost_estimate=cost(moved, moved),
+    )(*args)
+
+
+def rows_of(rows, width):
+    return jax.ShapeDtypeStruct((rows, width), F32)
+
+
+class Summer:
+    def __init__(self, n_dp, n_seq):
+        self.n_dp, self.n_seq = n_dp, n_seq
+        bits = [("dp", b) for b in range(1, n_dp.bit_length() - 1)]
+        seq = [("seq", b) for b in range(n_seq.bit_length() - 1)]
+        rest = bits[:1] + seq[:1] + seq[1:] + bits[1:]
+        self.core = [("dp", 0)]
+        self.stages = [rest[k : k + 2] for k in range(0, len(rest), 2)]
+
+    def send(self, x, stage, mask):
+        d_mask = sum(1 << b for k, (a, b) in enumerate(stage) if a == "dp" and mask >> k & 1)
+        s_mask = sum(1 << b for k, (a, b) in enumerate(stage) if a == "seq" and mask >> k & 1)
+        perm = [
+            (d * self.n_seq + s, (d ^ d_mask) * self.n_seq + (s ^ s_mask))
+            for d in range(self.n_dp)
+            for s in range(self.n_seq)
+        ]
+        return lax.ppermute(x, ("dp", "seq"), perm)
+
+    def split(self, groups, stage):
+        pieces = 1 << len(stage)
+        layout = [(len(g), g[0].shape[0]) for g in groups]
+        size = sum(rows for _, rows in layout) // pieces
+        width = groups[0][0].shape[1]
+        out = plain_call(
+            functools.partial(split_kernel, stage, layout),
+            [rows_of(size, width)] * pieces,
+            *[a for g in groups for a in g],
+        )
+        return out, layout
+
+    def join(self, x, stage, layout):
+        came = [x] + [self.send(x, stage, m) for m in range(1, 1 << len(stage))]
+        total = sum(rows for _, rows in layout)
+        return plain_call(
+            functools.partial(join_pieces_kernel, stage, layout), rows_of(total, x.shape[1]), *came
+        )
+
+    def __call__(self, groups, stages):
+        done = []
+        for stage in stages:
+            rows = [g[0].shape[0] for g in groups]
+            if sum(rows) > WHOLE and min(rows) >> len(stage) >= PAD:
+                out, layout = self.split(groups, stage)
+                done.append((stage, layout))
+            else:
+                whole, _ = self.split(groups, [])
+                out = [whole[0]] * (1 << len(stage))
+            groups = [[out[0]] + [self.send(out[m], stage, m) for m in range(1, len(out))]]
+        x = self.split(groups, [])[0][0]
+        for stage, layout in reversed(done):
+            x = self.join(x, stage, layout)
+        return x
+
+
+def assemble_kernel(parts, half, *refs):
+    out = refs[-1]
+    mine = lax.axis_index("dp") & 1
+    for p, (low, high) in enumerate(parts):
+        for side in range(2):
+            for i in range(low, high):
+                start = pl.multiple_of((2 * i + (mine ^ side)) * half, PAD)
+                rows = slice((i - low) * half, (i - low + 1) * half)
+                out[pl.ds(start, half), :] = refs[2 * p + side][rows]
 
 
 def solution(mesh):
@@ -232,36 +342,48 @@
         k2, v2 = keys[0], values[0]
         state_t = jax.ShapeDtypeStruct((tall, feats), F32)
 
-        out = whole_call(
-            functools.partial(key_kernel, count),
-            [
+        block = lambda shape, index: pl.BlockSpec(shape, index)
+        parts = [(0, hk // 2), (hk // 2, hk)]
+        tail_specs = [
+            block((tall, feats), lambda i, lo=lo, hi=hi: (jnp.clip(i, lo, hi - 1) - lo, 0))
+            for lo, hi in parts
+        ]
+        out = pl.pallas_call(
+            functools.partial(key_kernel, count, parts),
+            grid=(hk,),
+            in_specs=[
+                SMEM,
+                block((rows, hd), lambda i: (0, i)),
+                block((rows, hd), lambda i: (0, i)),
+                block((None, hd, hd), lambda i: (i, 0, 0)),
+            ],
+            out_specs=[
+                block((None, rows, feats), lambda i: (i, 0, 0)),
+                block((None, count, tall, feats), lambda i: (i, 0, 0, 0)),
+            ]
+            + tail_specs,
+            out_shape=[
                 jax.ShapeDtypeStruct((hk, rows, feats), BF16),
                 jax.ShapeDtypeStruct((hk, count, tall, feats), F32),
             ]
-            + [state_t] * hk,
-            3,
-            2 * hk * rows * hd * (hd + feats),
-            doc_spans,
-            k2,
-            v2,
-            k_map,
-        )
+            + [rows_of((hi - lo) * tall, feats) for lo, hi in parts],
+            compiler_params=pltpu.CompilerParams(vmem_limit_bytes=LIMIT),
+            cost_estimate=cost(2 * hk * rows * hd * (hd + feats), hk * rows * hd * 4),
+        )(doc_spans, k2, v2, k_map)
         feat_k, blocks, tails = out[0], out[1], out[2:]
 
         def exchange(own, reverse):
             came = []
             for k in range(hops):
                 hop = 1 << k
-                if reverse:
-                    perm = [(i, i - hop) for i in range(hop, n_seq)]
-                else:
-                    perm = [(i, i + hop) for i in range(n_seq - hop)]
+                step = n_seq - hop if reverse else hop
+                perm = [(i, (i + step) % n_seq) for i in range(n_seq)]
                 got = lax.ppermute(own, "seq", perm)
                 came.append(got)
                 if k < hops - 1:
                     own = whole_call(
                         functools.partial(join_kernel, count, hop, reverse),
-                        state_t,
+                        rows_of(*own.shape),
                         2,
                         own.size,
                         doc_spans,
@@ -270,69 +392,77 @@
                     )
             return came
 
-        def middle(i, came):
-            block = lambda shape, index: pl.BlockSpec(shape, index)
-            state = block((tall, feats), lambda c: (0, 0))
-            flops = 2 * group * rows * hd * (6 * feats + 3 * hd)
+        def middle(part, came):
+            lo, hi = part
+            state = block((tall, feats), lambda i, c: (i, 0))
+            flops = 2 * (hi - lo) * group * rows * hd * (6 * feats + 3 * hd)
+            grads = block((group * hd // 2, hd), lambda i, c: (i, 0))
             return pl.pallas_call(
                 functools.partial(middle_kernel, count, group, hops, coef),
-                grid=(count,),
+                grid=(hi - lo, count),
                 in_specs=[
                     SMEM,
-                    block((SPAN, group * hd), lambda c: (c, i)),
-                    block((SPAN, group * hd), lambda c: (c, i)),
-                    block((SPAN, hd), lambda c: (c, i)),
-                    block((None, SPAN, feats), lambda c: (i, c, 0)),
-                    block((group, hd, hd), lambda c: (i, 0, 0)),
-                    block((None, count, tall, feats), lambda c: (i, 0, 0, 0)),
+                    block((SPAN, group * hd), lambda i, c: (c, lo + i)),
+                    block((SPAN, group * hd), lambda i, c: (c, lo + i)),
+                    block((SPAN, hd), lambda i, c: (c, lo + i)),
+                    block((None, SPAN, feats), lambda i, c: (lo + i, c, 0)),
+                    block((group, hd, hd), lambda i, c: (lo + i, 0, 0)),
+                    block((None, count, tall, feats), lambda i, c: (lo + i, 0, 0, 0)),
                 ]
                 + [state] * hops,
                 out_specs=[
-                    block((group, hd, hd), lambda c: (0, 0, 0)),
+                    grads,
+                    grads,
                     state,
-                    block((None, tall, feats), lambda c: (c, 0, 0)),
-                    block((None, SPAN, feats), lambda c: (c, 0, 0)),
+                    block((None, None, tall, feats), lambda i, c: (i, c, 0, 0)),
+                    block((None, None, SPAN, feats), lambda i, c: (i, c, 0, 0)),
                 ],
                 out_shape=[
-                    jax.ShapeDtypeStruct((group, hd, hd), F32),
-                    state_t,
-                    jax.ShapeDtypeStruct((count, tall, feats), F32),
-                    jax.ShapeDtypeStruct((count, SPAN, feats), F32),
+                    rows_of((hi - lo) * group * hd // 2, hd),
+                    rows_of((hi - lo) * group * hd // 2, hd),
+                    rows_of((hi - lo) * tall, feats),
+                    jax.ShapeDtypeStruct((hi - lo, count, tall, feats), F32),
+                    jax.ShapeDtypeStruct((hi - lo, count, SPAN, feats), F32),
                 ],
                 compiler_params=pltpu.CompilerParams(vmem_limit_bytes=LIMIT),
                 cost_estimate=cost(flops, 4 * rows * group * hd),
             )(doc_spans, q2, t2, v2, feat_k, q_map, blocks, *came)
 
-        def last(i, back, part, came):
-            block = lambda shape, index: pl.BlockSpec(shape, index)
+        def last(part, back, inner, came):
+            lo, hi = part
             return pl.pallas_call(
                 functools.partial(last_kernel, count, hops),
-                grid=(1,),
+                grid=(hi - lo,),
                 in_specs=[
                     SMEM,
-                    block((rows, hd), lambda c: (0, i)),
-                    block((rows, hd), lambda c: (0, i)),
-                    block((None, hd, hd), lambda c: (i, 0, 0)),
-                    block((count, tall, feats), lambda c: (0, 0, 0)),
-                    block((count, SPAN, feats), lambda c: (0, 0, 0)),
+                    block((rows, hd), lambda i: (0, lo + i)),
+                    block((rows, hd), lambda i: (0, lo + i)),
+                    block((None, hd, hd), lambda i: (lo + i, 0, 0)),
+                    block((None, count, tall, feats), lambda i: (i, 0, 0, 0)),
+                    block((None, count, SPAN, feats), lambda i: (i, 0, 0, 0)),
                 ]
-                + [block((tall, feats), lambda c: (0, 0))] * hops,
-                out_specs=block((hd, hd), lambda c: (0, 0)),
-                out_shape=jax.ShapeDtypeStruct((hd, hd), F32),
+                + [block((tall, feats), lambda i: (i, 0))] * hops,
+                out_specs=block((hd, hd), lambda i: (i, 0)),
+                out_shape=rows_of((hi - lo) * hd, hd),
                 compiler_params=pltpu.CompilerParams(vmem_limit_bytes=LIMIT),
-                cost_estimate=cost(2 * rows * hd * 2 * feats, rows * feats * 4),
-            )(doc_spans, k2, v2, k_map, back, part, *came)
-
-        steps = [("dp", n_dp, b) for b in range(n_dp.bit_length() - 1)]
-        steps += [("seq", n_seq, b) for b in range(n_seq.bit_length() - 1)]
-        came = [exchange(tails[i], False) for i in range(hk)]
-        mids = [middle(i, came[i]) for i in range(hk)]
-        backs = [exchange(mids[i][1], True) for i in range(hk)]
-        gq = [sum_all(mids[i][0].reshape(-1, hd), steps) for i in range(hk)]
-        gk = [last(i, mids[i][2], mids[i][3], backs[i]) for i in range(hk)]
-        grad_q = jnp.concatenate(gq, axis=0).reshape(hq, hd, hd)
-        grad_k = sum_all(jnp.concatenate(gk, axis=0), steps).reshape(hk, hd, hd)
-        return grad_q, grad_k
+                cost_estimate=cost(LATE * rows * hd * 2 * feats, rows * feats * 4),
+            )(doc_spans, k2, v2, k_map, back, inner, *came)
+
+        total = Summer(n_dp, n_seq)
+        came = [exchange(t, False) for t in tails]
+        mids = [middle(p, c) for p, c in zip(parts, came)]
+        halves, backs = [], []
+        for mid in mids:
+            keep, send = mid[0], mid[1]
+            backs.append(exchange(mid[2], True))
+            half_sum = total([[keep, total.send(send, total.core, 1)]], total.stages)
+            halves += [half_sum, total.send(half_sum, total.core, 1)]
+        gk = [last(p, m[3], m[4], b) for p, m, b in zip(parts, mids, backs)]
+        grad_q = plain_call(
+            functools.partial(assemble_kernel, parts, group * hd // 2), rows_of(hq * hd, hd), *halves
+        )
+        grad_k = total([[g] for g in gk], [total.core] + total.stages)
+        return grad_q.reshape(hq, hd, hd), grad_k.reshape(hk, hd, hd)
 
     in_specs = (
         P("dp", "seq", None),

time: 170 us -> 145 us (0.85)
  starting transfers between devices: 107 us -> 61.5 us
  waiting for transfers between devices: 18.7 us -> 48.1 us
  Pallas kernels: 34.5 us -> 30.7 us
  local copies, waits for them, and re-layouts: 5.81 us -> 3.56 us
  other arithmetic: 1.72 us -> 0 us
    ppermute x16 -> x8, starting transfers between devices: 35.1 us -> 10.3 us  [exchange(): got = lax.ppermute(own, 'seq', perm)]
    ppermute x50 -> x30, starting transfers between devices: 71.4 us -> 51.2 us  [send(): return lax.ppermute(x, ('dp', 'seq'), perm)]
    ppermute x50 -> x30, waiting for transfers between devices: 11.1 us -> 27.6 us  [send(): return lax.ppermute(x, ('dp', 'seq'), perm)]
    ppermute x16 -> x8, waiting for transfers between devices: 7.61 us -> 20.5 us  [exchange(): got = lax.ppermute(own, 'seq', perm)]
    pallas_call x9 -> x4, Pallas kernels: 8.99 us -> 2.34 us  [whole_call(): pl.pallas_call(body, out_shape=out_shape, in_specs=[SMEM] + [pl.BlockSpec...]
    pallas_call x4 -> x17, Pallas kernels: 4.55 us -> 9.15 us  [the longest x2 3.65 us: last(): pl.pallas_call(functools.partial(last_kernel, count, hops), grid=(hi - lo...]
    unnamed x20 -> x16, local copies, waits for them, and re-layouts: 5.44 us -> 3.56 us
    pallas_call x4 -> x2, Pallas kernels: 21 us -> 19.2 us  [middle(): pl.pallas_call(functools.partial(middle_kernel, count, group, hops, coef)...]
  transfers between devices with their start and end apart: 66 -> 38, of which waited for: 12 -> 16; matrix products, arithmetic and copies ran while one was open for 1% -> 0% of each run, Pallas kernels for 19% -> 18%
where the time goes in v1:
time: 145 us
  starting transfers between devices  61.5 us (42%)
  waiting for transfers between devices  48.1 us (33%)
  Pallas kernels  30.7 us (21%)
  local copies, waits for them, and re-layouts  3.56 us (2%)
    ppermute x30, starting transfers between devices, send(): return lax.ppermute(x, ('dp', 'seq'), perm)  51.2 us
    ppermute x30, waiting for transfers between devices, send(): return lax.ppermute(x, ('dp', 'seq'), perm)  27.6 us
    ppermute x8, waiting for transfers between devices, exchange(): got = lax.ppermute(own, 'seq', perm)  20.5 us
    pallas_call x2, Pallas kernels, middle(): pl.pallas_call(functools.partial(middle_kernel, count, group, hops, coef)...  19.2 us
    ppermute x8, starting transfers between devices, exchange(): got = lax.ppermute(own, 'seq', perm)  10.3 us
    pallas_call x2, Pallas kernels, last(): pl.pallas_call(functools.partial(last_kernel, count, hops), grid=(hi - lo...  3.65 us
    unnamed x16, local copies, waits for them, and re-layouts  3.56 us
  transfers between devices with their start and end apart: 38, of which 16 were waited for; matrix products, arithmetic and copies ran while one was open for 0% of the time, Pallas kernels for 18%

profile of v1, /device:TPU:0, one launch (start us, length us, event | category | flops | bytes accessed | tf_op | source)
XLA Modules:
  0.0 144.9 jit_solution(4091828863373918566)
XLA Ops:
  4.2 2.8 %shard_map.86 = (bf16[4,256,256]{2,1,0:T(8,128)(2,1)S(1)}, f32[4,2,136,256]{3,2,1,0:T(8,128)S(1)}, f32[272,256]{1,0:T(8,128)S(1)}, f32[272,256]{1,0:T(8,128)S(1)}) custom-call(s32[1,8]{1,0:T(1,128)S(1)} %copy-done.7, bf16[256,512]{1,0:T(8,128)(2,1)S(1)} %bitcast.11, bf16[256,512]{1,0:T(8,128)(2,1)S(1)} %bitcast.6, bf16[4,128,128]{2,1,0:T(8,128)(2,1)S(1)} %copy-done.5), custom_call_target="tpu_custom_call" | custom-call | flops 100663296 | bytes 524288 | tf_op jit(solution)/shard_map/pallas_call | solution.py:351
  7.0 3.0 %collective-permute-start.13 = (f32[272,256]{1,0:T(8,128)S(1)}, f32[272,256]{1,0:T(8,128)S(1)}, u32[]{:S(2)}, u32[]{:S(2)}) collective-permute-start(f32[272,256]{1,0:T(8,128)S(1)} %get-tuple-element.35.own_ref), channel_id=1, source_target_pairs={{0,1},{1,2},{2,3},{3,4},{4,5},{5,6},{6,7},{7,0},{8,9},{9,10},{10,1... | collective-permute-start | bytes 835592 | tf_op jit(solution)/shard_map/ppermute | solution.py:381
  11.6 9.0 %collective-permute-done.13.came_ref.refs_7_ = f32[272,256]{1,0:T(8,128)S(1)} collective-permute-done((f32[272,256]{1,0:T(8,128)S(1)}, f32[272,256]{1,0:T(8,128)S(1)}, u32[]{:S(2)}, u32[]{:S(2)}) %collective-permute-start.13) | collective-permute-done | bytes 278560 | tf_op jit(solution)/shard_map/ppermute | solution.py:381
  21.3 5.3 %collective-permute-done.came_ref.refs_7_ = f32[272,256]{1,0:T(8,128)S(1)} collective-permute-done((f32[272,256]{1,0:T(8,128)S(1)}, f32[272,256]{1,0:T(8,128)S(1)}, u32[]{:S(2)}, u32[]{:S(2)}) %collective-permute-start) | collective-permute-done | bytes 278560 | tf_op jit(solution)/shard_map/ppermute | solution.py:381
  27.2 2.8 %collective-permute-done.14.refs_8_ = f32[272,256]{1,0:T(8,128)S(1)} collective-permute-done((f32[272,256]{1,0:T(8,128)S(1)}, f32[272,256]{1,0:T(8,128)S(1)}, u32[]{:S(2)}, u32[]{:S(2)}) %collective-permute-start.14) | collective-permute-done | bytes 278560 | tf_op jit(solution)/shard_map/ppermute | solution.py:381
  30.1 9.6 %shard_map.94 = (f32[1024,128]{1,0:T(8,128)S(1)}, f32[1024,128]{1,0:T(8,128)S(1)}, f32[272,256]{1,0:T(8,128)S(1)}, f32[2,2,136,256]{3,2,1,0:T(8,128)S(1)}, f32[2,2,128,256]{3,2,1,0:T(8,128)S(1)}) custom-call(s32[1,8]{1,0:T(1,128)S(1)} %copy-done.7, bf16[256,4096]{1,0:T(8,128)(2,1)} %bitcast.14, bf16[256,4096]{1,0:T(8,128)(2,1)} %bitcast.16, ...), custom_call_target="tpu_custom_call" | custom-call | flops 2013265920 | bytes 1048576 | tf_op jit(solution)/shard_map/pallas_call | solution.py:400
  39.7 9.6 %shard_map.88 = (f32[1024,128]{1,0:T(8,128)S(1)}, f32[1024,128]{1,0:T(8,128)S(1)}, f32[272,256]{1,0:T(8,128)S(1)}, f32[2,2,136,256]{3,2,1,0:T(8,128)S(1)}, f32[2,2,128,256]{3,2,1,0:T(8,128)S(1)}) custom-call(s32[1,8]{1,0:T(1,128)S(1)} %copy-done.7, bf16[256,4096]{1,0:T(8,128)(2,1)} %bitcast.15, bf16[256,4096]{1,0:T(8,128)(2,1)} %bitcast.17, ...), custom_call_target="tpu_custom_call" | custom-call | flops 2013265920 | bytes 1048576 | tf_op jit(solution)/shard_map/pallas_call | solution.py:400
  49.9 4.5 %collective-permute-start.28 = (f32[272,256]{1,0:T(8,128)S(1)}, f32[272,256]{1,0:T(8,128)S(1)}, u32[]{:S(2)}, u32[]{:S(2)}) collective-permute-start(f32[272,256]{1,0:T(8,128)S(1)} %get-tuple-element.47.own_ref), channel_id=1, source_target_pairs={{0,7},{1,0},{2,1},{3,2},{4,3},{5,4},{6,5},{7,6},{8,15},{9,8},{10,9... | collective-permute-start | bytes 835592 | tf_op jit(solution)/shard_map/ppermute | solution.py:381
  58.0 3.4 %collective-permute-done.28.came_ref.refs_6_ = f32[272,256]{1,0:T(8,128)S(1)} collective-permute-done((f32[272,256]{1,0:T(8,128)S(1)}, f32[272,256]{1,0:T(8,128)S(1)}, u32[]{:S(2)}, u32[]{:S(2)}) %collective-permute-start.28) | collective-permute-done | bytes 278560 | tf_op jit(solution)/shard_map/ppermute | solution.py:381
  63.1 5.8 %collective-permute-start.18 = (f32[256,128]{1,0:T(8,128)S(1)}, f32[256,128]{1,0:T(8,128)S(1)}, u32[]{:S(2)}, u32[]{:S(2)}) collective-permute-start(f32[256,128]{1,0:T(8,128)S(1)} %get-tuple-element.41), channel_id=1, source_target_pairs={{0,17},{1,16},{2,19},{3,18},{4,21},{5,20},{6,23},{7,22},{8,25},{9,... | collective-permute-start | bytes 393224 | tf_op jit(solution)/shard_map/ppermute | solution.py:277
  70.2 3.8 %collective-permute-start.4 = (f32[256,128]{1,0:T(8,128)S(1)}, f32[256,128]{1,0:T(8,128)S(1)}, u32[]{:S(2)}, u32[]{:S(2)}) collective-permute-start(f32[256,128]{1,0:T(8,128)S(1)} %get-tuple-element.33), channel_id=1, source_target_pairs={{0,1},{1,0},{2,3},{3,2},{4,5},{5,4},{6,7},{7,6},{8,9},{9,8},{10,11... | collective-permute-start | bytes 393224 | tf_op jit(solution)/shard_map/ppermute | solution.py:277
  75.3 3.2 %collective-permute-start.20 = (f32[256,128]{1,0:T(8,128)S(1)}, f32[256,128]{1,0:T(8,128)S(1)}, u32[]{:S(2)}, u32[]{:S(2)}) collective-permute-start(f32[256,128]{1,0:T(8,128)S(1)} %shard_map.96.refs_0_), channel_id=1, source_target_pairs={{0,4},{1,5},{2,6},{3,7},{4,0},{5,1},{6,2},{7,3},{8,12},{9,13},{10,... | collective-permute-start | bytes 393224 | tf_op jit(solution)/shard_map/ppermute | solution.py:277
  80.5 3.8 %collective-permute-start.21 = (f32[256,128]{1,0:T(8,128)S(1)}, f32[256,128]{1,0:T(8,128)S(1)}, u32[]{:S(2)}, u32[]{:S(2)}) collective-permute-start(f32[256,128]{1,0:T(8,128)S(1)} %shard_map.96.refs_0_), channel_id=1, source_target_pairs={{0,6},{1,7},{2,4},{3,5},{4,2},{5,3},{6,0},{7,1},{8,14},{9,15},{10,... | collective-permute-start | bytes 393224 | tf_op jit(solution)/shard_map/ppermute | solution.py:277
  85.1 2.1 %collective-permute-start.6 = (f32[256,128]{1,0:T(8,128)S(1)}, f32[256,128]{1,0:T(8,128)S(1)}, u32[]{:S(2)}, u32[]{:S(2)}) collective-permute-start(f32[256,128]{1,0:T(8,128)S(1)} %shard_map.90.refs_0_), channel_id=1, source_target_pairs={{0,2},{1,3},{2,0},{3,1},{4,6},{5,7},{6,4},{7,5},{8,10},{9,11},{10,... | collective-permute-start | bytes 393224 | tf_op jit(solution)/shard_map/ppermute | solution.py:277
  88.8 6.5 %collective-permute-start.8 = (f32[256,128]{1,0:T(8,128)S(1)}, f32[256,128]{1,0:T(8,128)S(1)}, u32[]{:S(2)}, u32[]{:S(2)}) collective-permute-start(f32[256,128]{1,0:T(8,128)S(1)} %shard_map.90.refs_0_), channel_id=1, source_target_pairs={{0,6},{1,7},{2,4},{3,5},{4,2},{5,3},{6,0},{7,1},{8,14},{9,15},{10,... | collective-permute-start | bytes 393224 | tf_op jit(solution)/shard_map/ppermute | solution.py:277
  95.3 3.9 %collective-permute-start.22 = (f32[256,128]{1,0:T(8,128)S(1)}, f32[256,128]{1,0:T(8,128)S(1)}, u32[]{:S(2)}, u32[]{:S(2)}) collective-permute-start(f32[256,128]{1,0:T(8,128)S(1)} %shard_map.97.refs_0_), channel_id=1, source_target_pairs={{0,16},{1,17},{2,18},{3,19},{4,20},{5,21},{6,22},{7,23},{8,24},{9,... | collective-permute-start | bytes 393224 | tf_op jit(solution)/shard_map/ppermute | solution.py:277
  102.2 3.3 %collective-permute-done.7.refs_2_ = f32[256,128]{1,0:T(8,128)S(1)} collective-permute-done((f32[256,128]{1,0:T(8,128)S(1)}, f32[256,128]{1,0:T(8,128)S(1)}, u32[]{:S(2)}, u32[]{:S(2)}) %collective-permute-start.7) | collective-permute-done | bytes 131104 | tf_op jit(solution)/shard_map/ppermute | solution.py:277
  105.5 2.4 %collective-permute-start.24 = (f32[256,128]{1,0:T(8,128)S(1)}, f32[256,128]{1,0:T(8,128)S(1)}, u32[]{:S(2)}, u32[]{:S(2)}) collective-permute-start(f32[256,128]{1,0:T(8,128)S(1)} %shard_map.97.refs_0_), channel_id=1, source_target_pairs={{0,17},{1,16},{2,19},{3,18},{4,21},{5,20},{6,23},{7,22},{8,25},{9,... | collective-permute-start | bytes 393224 | tf_op jit(solution)/shard_map/ppermute | solution.py:277
  118.5 2.0 %collective-permute-start.33 = (f32[256,128]{1,0:T(8,128)S(1)}, f32[256,128]{1,0:T(8,128)S(1)}, u32[]{:S(2)}, u32[]{:S(2)}) collective-permute-start(f32[256,128]{1,0:T(8,128)S(1)} %shard_map.105.refs_0_), channel_id=1, source_target_pairs={{0,17},{1,16},{2,19},{3,18},{4,21},{5,20},{6,23},{7,22},{8,25},{9,... | collective-permute-start | bytes 393224 | tf_op jit(solution)/shard_map/ppermute | solution.py:277
  120.5 2.8 %collective-permute-done.31.refs_1_ = f32[256,128]{1,0:T(8,128)S(1)} collective-permute-done((f32[256,128]{1,0:T(8,128)S(1)}, f32[256,128]{1,0:T(8,128)S(1)}, u32[]{:S(2)}, u32[]{:S(2)}) %collective-permute-start.31) | collective-permute-done | bytes 131104 | tf_op jit(solution)/shard_map/ppermute | solution.py:277
  123.3 3.0 %collective-permute-done.32.refs_2_ = f32[256,128]{1,0:T(8,128)S(1)} collective-permute-done((f32[256,128]{1,0:T(8,128)S(1)}, f32[256,128]{1,0:T(8,128)S(1)}, u32[]{:S(2)}, u32[]{:S(2)}) %collective-permute-start.32) | collective-permute-done | bytes 131104 | tf_op jit(solution)/shard_map/ppermute | solution.py:277
  126.3 2.4 %collective-permute-start.34 = (f32[256,128]{1,0:T(8,128)S(1)}, f32[256,128]{1,0:T(8,128)S(1)}, u32[]{:S(2)}, u32[]{:S(2)}) collective-permute-start(f32[256,128]{1,0:T(8,128)S(1)} %shard_map.106.refs_0_), channel_id=1, source_target_pairs={{0,2},{1,3},{2,0},{3,1},{4,6},{5,7},{6,4},{7,5},{8,10},{9,11},{10,... | collective-permute-start | bytes 393224 | tf_op jit(solution)/shard_map/ppermute | solution.py:277
  129.1 2.1 %collective-permute-start.36 = (f32[256,128]{1,0:T(8,128)S(1)}, f32[256,128]{1,0:T(8,128)S(1)}, u32[]{:S(2)}, u32[]{:S(2)}) collective-permute-start(f32[256,128]{1,0:T(8,128)S(1)} %shard_map.106.refs_0_), channel_id=1, source_target_pairs={{0,6},{1,7},{2,4},{3,5},{4,2},{5,3},{6,0},{7,1},{8,14},{9,15},{10,... | collective-permute-start | bytes 393224 | tf_op jit(solution)/shard_map/ppermute | solution.py:277
  133.1 8.1 %collective-permute-done.35.refs_2_ = f32[256,128]{1,0:T(8,128)S(1)} collective-permute-done((f32[256,128]{1,0:T(8,128)S(1)}, f32[256,128]{1,0:T(8,128)S(1)}, u32[]{:S(2)}, u32[]{:S(2)}) %collective-permute-start.35) | collective-permute-done | bytes 131104 | tf_op jit(solution)/shard_map/ppermute | solution.py:277
  (91 shorter events, 38.6 us)
Async XLA Ops:
  7.0 13.5 %collective-permute-start.13 = (f32[272,256]{1,0:T(8,128)S(1)}, f32[272,256]{1,0:T(8,128)S(1)}, u32[]{:S(2)}, u32[]{:S(2)}) collective-permute-start(f32[272,256]{1,0:T(8,128)S(1)} %get-tuple-element.35.own_ref), channel_id=1, source_target_pairs={{0,1},{1,2},{2,3},{3,4},{4,5},{5,6},{6,7},{7,0},{8,9},{9,10},{10,1... | collective-permute-start | bytes 835592 | tf_op jit(solution)/shard_map/ppermute | solution.py:381
  10.1 16.5 %collective-permute-start = (f32[272,256]{1,0:T(8,128)S(1)}, f32[272,256]{1,0:T(8,128)S(1)}, u32[]{:S(2)}, u32[]{:S(2)}) collective-permute-start(f32[272,256]{1,0:T(8,128)S(1)} %get-tuple-element.28.own_ref), channel_id=1, source_target_pairs={{0,1},{1,2},{2,3},{3,4},{4,5},{5,6},{6,7},{7,0},{8,9},{9,10},{10,1... | collective-permute-start | bytes 835592 | tf_op jit(solution)/shard_map/ppermute | solution.py:381
  27.2 12.6 %collective-permute-start.1 = (f32[272,256]{1,0:T(8,128)S(1)}, f32[272,256]{1,0:T(8,128)S(1)}, u32[]{:S(2)}, u32[]{:S(2)}) collective-permute-start(f32[272,256]{1,0:T(8,128)S(1)} %shard_map.87), channel_id=1, source_target_pairs={{0,2},{1,3},{2,4},{3,5},{4,6},{5,7},{6,0},{7,1},{8,10},{9,11},{10,... | collective-permute-start | bytes 835592 | tf_op jit(solution)/shard_map/ppermute | solution.py:381
  39.6 14.8 %collective-permute-start.15 = (f32[1024,128]{1,0:T(8,128)S(1)}, f32[1024,128]{1,0:T(8,128)S(1)}, u32[]{:S(2)}, u32[]{:S(2)}) collective-permute-start(f32[1024,128]{1,0:T(8,128)S(1)} %get-tuple-element.37), channel_id=1, source_target_pairs={{0,8},{1,9},{2,10},{3,11},{4,12},{5,13},{6,14},{7,15},{8,0},{9,1},... | collective-permute-start | bytes 1572872 | tf_op jit(solution)/shard_map/ppermute | solution.py:277
  49.4 13.7 %collective-permute-start.2 = (f32[1024,128]{1,0:T(8,128)S(1)}, f32[1024,128]{1,0:T(8,128)S(1)}, u32[]{:S(2)}, u32[]{:S(2)}) collective-permute-start(f32[1024,128]{1,0:T(8,128)S(1)} %get-tuple-element.30), channel_id=1, source_target_pairs={{0,8},{1,9},{2,10},{3,11},{4,12},{5,13},{6,14},{7,15},{8,0},{9,1},... | collective-permute-start | bytes 1572872 | tf_op jit(solution)/shard_map/ppermute | solution.py:277
  49.9 11.5 %collective-permute-start.28 = (f32[272,256]{1,0:T(8,128)S(1)}, f32[272,256]{1,0:T(8,128)S(1)}, u32[]{:S(2)}, u32[]{:S(2)}) collective-permute-start(f32[272,256]{1,0:T(8,128)S(1)} %get-tuple-element.47.own_ref), channel_id=1, source_target_pairs={{0,7},{1,0},{2,1},{3,2},{4,3},{5,4},{6,5},{7,6},{8,15},{9,8},{10,9... | collective-permute-start | bytes 835592 | tf_op jit(solution)/shard_map/ppermute | solution.py:381
  54.4 20.8 %collective-permute-start.26 = (f32[272,256]{1,0:T(8,128)S(1)}, f32[272,256]{1,0:T(8,128)S(1)}, u32[]{:S(2)}, u32[]{:S(2)}) collective-permute-start(f32[272,256]{1,0:T(8,128)S(1)} %get-tuple-element.44.own_ref), channel_id=1, source_target_pairs={{0,7},{1,0},{2,1},{3,2},{4,3},{5,4},{6,5},{7,6},{8,15},{9,8},{10,9... | collective-permute-start | bytes 835592 | tf_op jit(solution)/shard_map/ppermute | solution.py:381
  54.5 14.4 %collective-permute-start.16 = (f32[256,128]{1,0:T(8,128)S(1)}, f32[256,128]{1,0:T(8,128)S(1)}, u32[]{:S(2)}, u32[]{:S(2)}) collective-permute-start(f32[256,128]{1,0:T(8,128)S(1)} %get-tuple-element.39), channel_id=1, source_target_pairs={{0,16},{1,17},{2,18},{3,19},{4,20},{5,21},{6,22},{7,23},{8,24},{9,... | collective-permute-start | bytes 393224 | tf_op jit(solution)/shard_map/ppermute | solution.py:277
  56.0 14.2 %collective-permute-start.17 = (f32[256,128]{1,0:T(8,128)S(1)}, f32[256,128]{1,0:T(8,128)S(1)}, u32[]{:S(2)}, u32[]{:S(2)}) collective-permute-start(f32[256,128]{1,0:T(8,128)S(1)} %get-tuple-element.40), channel_id=1, source_target_pairs={{0,1},{1,0},{2,3},{3,2},{4,5},{5,4},{6,7},{7,6},{8,9},{9,8},{10,11... | collective-permute-start | bytes 393224 | tf_op jit(solution)/shard_map/ppermute | solution.py:277
  62.0 33.3 %collective-permute-start.29 = (f32[272,256]{1,0:T(8,128)S(1)}, f32[272,256]{1,0:T(8,128)S(1)}, u32[]{:S(2)}, u32[]{:S(2)}) collective-permute-start(f32[272,256]{1,0:T(8,128)S(1)} %shard_map.102), channel_id=1, source_target_pairs={{0,6},{1,7},{2,0},{3,1},{4,2},{5,3},{6,4},{7,5},{8,14},{9,15},{10,... | collective-permute-start | bytes 835592 | tf_op jit(solution)/shard_map/ppermute | solution.py:381
  63.1 11.0 %collective-permute-start.18 = (f32[256,128]{1,0:T(8,128)S(1)}, f32[256,128]{1,0:T(8,128)S(1)}, u32[]{:S(2)}, u32[]{:S(2)}) collective-permute-start(f32[256,128]{1,0:T(8,128)S(1)} %get-tuple-element.41), channel_id=1, source_target_pairs={{0,17},{1,16},{2,19},{3,18},{4,21},{5,20},{6,23},{7,22},{8,25},{9,... | collective-permute-start | bytes 393224 | tf_op jit(solution)/shard_map/ppermute | solution.py:277
  70.2 10.3 %collective-permute-start.4 = (f32[256,128]{1,0:T(8,128)S(1)}, f32[256,128]{1,0:T(8,128)S(1)}, u32[]{:S(2)}, u32[]{:S(2)}) collective-permute-start(f32[256,128]{1,0:T(8,128)S(1)} %get-tuple-element.33), channel_id=1, source_target_pairs={{0,1},{1,0},{2,3},{3,2},{4,5},{5,4},{6,7},{7,6},{8,9},{9,8},{10,11... | collective-permute-start | bytes 393224 | tf_op jit(solution)/shard_map/ppermute | solution.py:277
  74.1 10.9 %collective-permute-start.5 = (f32[256,128]{1,0:T(8,128)S(1)}, f32[256,128]{1,0:T(8,128)S(1)}, u32[]{:S(2)}, u32[]{:S(2)}) collective-permute-start(f32[256,128]{1,0:T(8,128)S(1)} %get-tuple-element.34), channel_id=1, source_target_pairs={{0,17},{1,16},{2,19},{3,18},{4,21},{5,20},{6,23},{7,22},{8,25},{9,... | collective-permute-start | bytes 393224 | tf_op jit(solution)/shard_map/ppermute | solution.py:277
  75.3 12.5 %collective-permute-start.20 = (f32[256,128]{1,0:T(8,128)S(1)}, f32[256,128]{1,0:T(8,128)S(1)}, u32[]{:S(2)}, u32[]{:S(2)}) collective-permute-start(f32[256,128]{1,0:T(8,128)S(1)} %shard_map.96.refs_0_), channel_id=1, source_target_pairs={{0,4},{1,5},{2,6},{3,7},{4,0},{5,1},{6,2},{7,3},{8,12},{9,13},{10,... | collective-permute-start | bytes 393224 | tf_op jit(solution)/shard_map/ppermute | solution.py:277
  84.9 23.6 %collective-permute-start.27 = (f32[272,256]{1,0:T(8,128)S(1)}, f32[272,256]{1,0:T(8,128)S(1)}, u32[]{:S(2)}, u32[]{:S(2)}) collective-permute-start(f32[272,256]{1,0:T(8,128)S(1)} %shard_map.100), channel_id=1, source_target_pairs={{0,6},{1,7},{2,0},{3,1},{4,2},{5,3},{6,4},{7,5},{8,14},{9,15},{10,... | collective-permute-start | bytes 835592 | tf_op jit(solution)/shard_map/ppermute | solution.py:381
  85.1 16.0 %collective-permute-start.6 = (f32[256,128]{1,0:T(8,128)S(1)}, f32[256,128]{1,0:T(8,128)S(1)}, u32[]{:S(2)}, u32[]{:S(2)}) collective-permute-start(f32[256,128]{1,0:T(8,128)S(1)} %shard_map.90.refs_0_), channel_id=1, source_target_pairs={{0,2},{1,3},{2,0},{3,1},{4,6},{5,7},{6,4},{7,5},{8,10},{9,11},{10,... | collective-permute-start | bytes 393224 | tf_op jit(solution)/shard_map/ppermute | solution.py:277
  87.8 17.7 %collective-permute-start.7 = (f32[256,128]{1,0:T(8,128)S(1)}, f32[256,128]{1,0:T(8,128)S(1)}, u32[]{:S(2)}, u32[]{:S(2)}) collective-permute-start(f32[256,128]{1,0:T(8,128)S(1)} %shard_map.90.refs_0_), channel_id=1, source_target_pairs={{0,4},{1,5},{2,6},{3,7},{4,0},{5,1},{6,2},{7,3},{8,12},{9,13},{10,... | collective-permute-start | bytes 393224 | tf_op jit(solution)/shard_map/ppermute | solution.py:277
  88.8 19.1 %collective-permute-start.8 = (f32[256,128]{1,0:T(8,128)S(1)}, f32[256,128]{1,0:T(8,128)S(1)}, u32[]{:S(2)}, u32[]{:S(2)}) collective-permute-start(f32[256,128]{1,0:T(8,128)S(1)} %shard_map.90.refs_0_), channel_id=1, source_target_pairs={{0,6},{1,7},{2,4},{3,5},{4,2},{5,3},{6,0},{7,1},{8,14},{9,15},{10,... | collective-permute-start | bytes 393224 | tf_op jit(solution)/shard_map/ppermute | solution.py:277
  95.3 14.5 %collective-permute-start.22 = (f32[256,128]{1,0:T(8,128)S(1)}, f32[256,128]{1,0:T(8,128)S(1)}, u32[]{:S(2)}, u32[]{:S(2)}) collective-permute-start(f32[256,128]{1,0:T(8,128)S(1)} %shard_map.97.refs_0_), channel_id=1, source_target_pairs={{0,16},{1,17},{2,18},{3,19},{4,20},{5,21},{6,22},{7,23},{8,24},{9,... | collective-permute-start | bytes 393224 | tf_op jit(solution)/shard_map/ppermute | solution.py:277
  101.1 12.3 %collective-permute-start.23 = (f32[256,128]{1,0:T(8,128)S(1)}, f32[256,128]{1,0:T(8,128)S(1)}, u32[]{:S(2)}, u32[]{:S(2)}) collective-permute-start(f32[256,128]{1,0:T(8,128)S(1)} %shard_map.97.refs_0_), channel_id=1, source_target_pairs={{0,1},{1,0},{2,3},{3,2},{4,5},{5,4},{6,7},{7,6},{8,9},{9,8},{10,11... | collective-permute-start | bytes 393224 | tf_op jit(solution)/shard_map/ppermute | solution.py:277
  113.5 29.9 %collective-permute-start.25 = (f32[1024,128]{1,0:T(8,128)S(1)}, f32[1024,128]{1,0:T(8,128)S(1)}, u32[]{:S(2)}, u32[]{:S(2)}) collective-permute-start(f32[1024,128]{1,0:T(8,128)S(1)} %shard_map.98.refs_2_), channel_id=1, source_target_pairs={{0,8},{1,9},{2,10},{3,11},{4,12},{5,13},{6,14},{7,15},{8,0},{9,1},... | collective-permute-start | bytes 1572872 | tf_op jit(solution)/shard_map/ppermute | solution.py:277
  116.9 26.5 %collective-permute-start.12 = (f32[1024,128]{1,0:T(8,128)S(1)}, f32[1024,128]{1,0:T(8,128)S(1)}, u32[]{:S(2)}, u32[]{:S(2)}) collective-permute-start(f32[1024,128]{1,0:T(8,128)S(1)} %shard_map.92.refs_0_), channel_id=1, source_target_pairs={{0,8},{1,9},{2,10},{3,11},{4,12},{5,13},{6,14},{7,15},{8,0},{9,1},... | collective-permute-start | bytes 1572872 | tf_op jit(solution)/shard_map/ppermute | solution.py:277
  128.7 12.5 %collective-permute-start.35 = (f32[256,128]{1,0:T(8,128)S(1)}, f32[256,128]{1,0:T(8,128)S(1)}, u32[]{:S(2)}, u32[]{:S(2)}) collective-permute-start(f32[256,128]{1,0:T(8,128)S(1)} %shard_map.106.refs_0_), channel_id=1, source_target_pairs={{0,4},{1,5},{2,6},{3,7},{4,0},{5,1},{6,2},{7,3},{8,12},{9,13},{10,... | collective-permute-start | bytes 393224 | tf_op jit(solution)/shard_map/ppermute | solution.py:277
  129.1 12.2 %collective-permute-start.36 = (f32[256,128]{1,0:T(8,128)S(1)}, f32[256,128]{1,0:T(8,128)S(1)}, u32[]{:S(2)}, u32[]{:S(2)}) collective-permute-start(f32[256,128]{1,0:T(8,128)S(1)} %shard_map.106.refs_0_), channel_id=1, source_target_pairs={{0,6},{1,7},{2,4},{3,5},{4,2},{5,3},{6,0},{7,1},{8,14},{9,15},{10,... | collective-permute-start | bytes 393224 | tf_op jit(solution)/shard_map/ppermute | solution.py:277
  (22 other events, 231.5 us)

commit v2 on v1

v2 whole, which is shorter than its diff:
```python
import functools
import math

import jax
import jax.numpy as jnp
from jax import lax
from jax.experimental import pallas as pl
from jax.experimental.pallas import tpu as pltpu
from jax.sharding import PartitionSpec as P

SPAN = 128
PAD = 8
WHOLE = 128
F32 = jnp.float32
BF16 = jnp.bfloat16
NN = (((1,), (0,)), ((), ()))
NT = (((1,), (1,)), ((), ()))
TN = (((0,), (0,)), ((), ()))
TT = (((0,), (1,)), ((), ()))


def dot(left, right, dims):
    return lax.dot_general(left, right, dims, preferred_element_type=F32)


def bounds(spans_ref, block):
    start, end, place = jnp.int32(0), jnp.int32(0), jnp.int32(0)
    for d in range(spans_ref.shape[1]):
        after = place + spans_ref[0, d]
        inside = jnp.logical_and(block >= place, block < after)
        start = jnp.where(inside, place, start)
        end = jnp.where(inside, after, end)
        place = after
    return start, end


def flag(condition):
    return jnp.where(condition, jnp.float32(1.0), jnp.float32(0.0))


def soft_pair(mapped, axis):
    up = jnp.exp(mapped - jnp.max(mapped, axis, keepdims=True))
    low = jnp.exp(jnp.min(mapped, axis, keepdims=True) - mapped)
    up = up * (1.0 / jnp.sum(up, axis, keepdims=True))
    low = low * (1.0 / jnp.sum(low, axis, keepdims=True))
    return up, low


def map_grad(up, low, grad_up, grad_low, axis):
    first = up * (grad_up - jnp.sum(up * grad_up, axis, keepdims=True))
    second = low * (grad_low - jnp.sum(low * grad_low, axis, keepdims=True))
    return (first - second).astype(BF16)


def tall_rows(row):
    return jnp.broadcast_to(row, (PAD, row.shape[1]))


def key_kernel(count, parts, spans_ref, k_ref, v_ref, w_ref, feat_ref, block_ref, *tail_refs):
    width = w_ref.shape[-1]
    first = lax.axis_index("seq") * count
    starts = [bounds(spans_ref, first + c)[0] for c in range(count)]
    for (lo, hi), tail_ref in zip(parts, tail_refs):
        for i in range(lo, hi):
            cols = slice(i * width, (i + 1) * width)
            up, low = soft_pair(dot(k_ref[:, cols], w_ref[i], NN), -1)
            feat = jnp.concatenate([up, low], axis=-1).astype(BF16)
            feat_ref[i] = feat
            tail = None
            for c in range(count):
                rows = slice(c * SPAN, (c + 1) * SPAN)
                state = dot(v_ref[rows, cols], feat[rows], TN)
                norm = jnp.sum(feat[rows].astype(F32), axis=0, keepdims=True)
                both = jnp.concatenate([state, tall_rows(norm)], axis=0)
                block_ref[i, c] = both
                part = flag(starts[c] == starts[count - 1]) * both
                tail = part if tail is None else tail + part
            tall = tail.shape[0]
            tail_ref[(i - lo) * tall : (i - lo + 1) * tall] = tail


def join_kernel(count, hop, reverse, spans_ref, own_ref, came_ref, out_ref):
    place = lax.axis_index("seq")
    if reverse:
        _, end = bounds(spans_ref, place * count)
        keep = flag(end > (place + hop) * count)
    else:
        start, _ = bounds(spans_ref, place * count + count - 1)
        keep = flag(start < (place - hop + 1) * count)
    out_ref[...] = own_ref[...] + keep * came_ref[...]


def causal_mask(columns):
    t = lax.broadcasted_iota(jnp.int32, (SPAN, columns), 1) & (SPAN - 1)
    return lax.broadcasted_iota(jnp.int32, (SPAN, columns), 0) <= t


def early_kernel(part, count, group, *refs):
    q_ref, t_ref, v_ref, feat_k_ref, w_ref = refs[:5]
    up_ref, low_ref, feat_ref, num_ref, den_ref, tgt_ref = refs[5:]
    width = w_ref.shape[-1]
    causal = causal_mask(group * SPAN)
    for i in range(*part):
        k = i - part[0]
        for c in range(count):
            rows = slice(c * SPAN, (c + 1) * SPAN)
            cols = [slice(h * width, (h + 1) * width) for h in range(i * group, (i + 1) * group)]
            mapped = [dot(w_ref[i * group + h], q_ref[rows, cols[h]], TT) for h in range(group)]
            up, low = soft_pair(jnp.concatenate(mapped, axis=1), 0)
            up_ref[k, c] = up
            low_ref[k, c] = low
            feat = jnp.concatenate([up, low], axis=0).astype(BF16)
            feat_ref[k, c] = feat
            scores = jnp.where(causal, dot(feat_k_ref[i, rows], feat, NN), 0.0)
            den_ref[k, c] = tall_rows(jnp.sum(scores, 0, keepdims=True))
            vals = v_ref[rows, i * width : (i + 1) * width]
            num_ref[k, c] = dot(vals, scores.astype(BF16), TN)
            for h in range(group):
                tgt_ref[k, c, :, h * SPAN : (h + 1) * SPAN] = jnp.transpose(t_ref[rows, cols[h]])


def late_kernel(part, count, group, hops, coef, *refs):
    spans_ref, q_ref, v_ref, feat_k_ref, block_ref = refs[:5]
    up_ref, low_ref, feat_ref, num_ref, den_ref, tgt_ref = refs[5:11]
    came = refs[11 : 11 + hops]
    keep_ref, send_ref, head_ref, back_ref, inner_ref = refs[11 + hops :]
    width = tgt_ref.shape[2]
    tall = block_ref.shape[2]
    half = group // 2
    core = lax.axis_index("dp") & 1
    place = lax.axis_index("seq")
    first = place * count
    start_first, _ = bounds(spans_ref, first)
    causal = causal_mask(group * SPAN)
    for i in range(*part):
        k = i - part[0]
        grads, head = None, None
        for c in range(count):
            rows = slice(c * SPAN, (c + 1) * SPAN)
            start, _ = bounds(spans_ref, first + c)
            state = None
            for n in range(hops):
                near = start_first < (place - (1 << n) + 1) * count
                some = came[n][k * tall : (k + 1) * tall]
                some = flag(jnp.logical_and(near, start < first)) * some
                state = some if state is None else state + some
            for e in range(c):
                state = state + flag(start <= first + e) * block_ref[i, e]
            state = state.astype(BF16)
            feat_k = feat_k_ref[i, rows]
            feat = feat_ref[k, c]
            across = dot(state, feat, NN)
            numer = num_ref[k, c] + across[:SPAN]
            inverse = 1.0 / (den_ref[k, c, :1] + across[SPAN : SPAN + 1])
            output = numer * inverse
            d_out = coef * (output - tgt_ref[k, c].astype(F32))
            d_numer = (d_out * inverse).astype(BF16)
            d_denom = -jnp.sum(d_out * output, 0, keepdims=True) * inverse
            vals = v_ref[rows, i * width : (i + 1) * width]
            pairs = jnp.where(causal, dot(vals, d_numer, NN) + d_denom, 0.0).astype(BF16)
            mat = jnp.concatenate([feat_k, state[:SPAN]], axis=0)
            norm = jnp.transpose(state[SPAN:].astype(F32))[:, :1]
            d_feat = dot(mat, jnp.concatenate([pairs, d_numer], axis=0), TN) + norm * d_denom
            high = d_denom.astype(BF16)
            rest = d_denom - high.astype(F32)
            mid = rest.astype(BF16)
            low = (rest - mid.astype(F32)).astype(BF16)
            fill = jnp.zeros((2 * PAD - 3, high.shape[1]), BF16)
            left = jnp.concatenate([d_numer, pairs, high, mid, low, fill], axis=0)
            crossed = dot(left, feat, NT)
            at = 2 * SPAN
            norm_row = crossed[at : at + 1] + crossed[at + 1 : at + 2] + crossed[at + 2 : at + 3]
            back = jnp.concatenate([crossed[:SPAN], tall_rows(norm_row)], axis=0)
            back_ref[k, c] = back
            inner_ref[k, c] = crossed[SPAN:at]
            d_map = map_grad(up_ref[k, c], low_ref[k, c], d_feat[:width], d_feat[width:], 0)
            now = []
            for h in range(group):
                queries = q_ref[rows, (i * group + h) * width : (i * group + h + 1) * width]
                now.append(dot(d_map[:, h * SPAN : (h + 1) * SPAN], queries, NN))
            grads = now if grads is None else [a + b for a, b in zip(grads, now)]
            mine = flag(start == start_first) * back
            head = mine if head is None else head + mine
        head_ref[k * tall : (k + 1) * tall] = head
        for h in range(half):
            at = slice((k * half + h) * width, (k * half + h + 1) * width)
            keep_ref[at] = jnp.transpose(jnp.where(core == 0, grads[h], grads[half + h]))
            send_ref[at] = jnp.transpose(jnp.where(core == 0, grads[half + h], grads[h]))


def last_kernel(part, count, hops, *refs):
    spans_ref, k_ref, v_ref, w_ref, back_ref, inner_ref = refs[:6]
    came = refs[6 : 6 + hops]
    gk_ref = refs[6 + hops]
    width = w_ref.shape[-1]
    tall = back_ref.shape[2]
    place = lax.axis_index("seq")
    first = place * count
    _, end_last = bounds(spans_ref, first + count - 1)
    for i in range(*part):
        k = i - part[0]
        cols = slice(i * width, (i + 1) * width)
        keys = k_ref[:, cols]
        up, low = soft_pair(dot(keys, w_ref[i], NN), -1)
        grads = []
        for c in range(count):
            _, end = bounds(spans_ref, first + c)
            state = None
            for n in range(hops):
                near = end_last > (place + (1 << n)) * count
                some = came[n][k * tall : (k + 1) * tall]
                some = flag(jnp.logical_and(near, end > first + count)) * some
                state = some if state is None else state + some
            for e in range(c + 1, count):
                state = state + flag(end > first + e) * back_ref[k, e]
            norm = state[SPAN : SPAN + 1].astype(BF16).astype(F32)
            vals = v_ref[c * SPAN : (c + 1) * SPAN, cols]
            grads.append(inner_ref[k, c] + dot(vals, state[:SPAN].astype(BF16), NN) + norm)
        d_feat = jnp.concatenate(grads, axis=0)
        d_map = map_grad(up, low, d_feat[:, :width], d_feat[:, width:], -1)
        gk_ref[k * width : (k + 1) * width] = dot(keys, d_map, TN)


def cost(flops, moved):
    return pl.CostEstimate(flops=int(flops), bytes_accessed=int(moved), transcendentals=0)


SMEM = pl.BlockSpec(memory_space=pltpu.SMEM)
LIMIT = 32 << 20
PER_MICRO = 1e9


def local_call(body, out_shape, micros, *args, spans=None):
    first = [] if spans is None else [spans]
    return pl.pallas_call(
        body,
        out_shape=out_shape,
        in_specs=[SMEM] * len(first) + [pl.BlockSpec(memory_space=pltpu.VMEM)] * len(args),
        compiler_params=pltpu.CompilerParams(vmem_limit_bytes=LIMIT),
        cost_estimate=cost(micros * PER_MICRO, 0),
    )(*first, *args)


def index_in(stage):
    place = jnp.int32(0)
    for k, (axis, bit) in enumerate(stage):
        place = place + (((lax.axis_index(axis) >> bit) & 1) << k)
    return place


def split_kernel(stage, layout, *refs):
    pieces = 1 << len(stage)
    outs = refs[len(refs) - pieces :]
    mine = index_in(stage)
    for m, out in enumerate(outs):
        at, used = 0, 0
        for addends, rows in layout:
            size = rows // pieces
            start = 0 if pieces == 1 else pl.multiple_of((mine ^ m) * size, PAD)
            total = refs[used][pl.ds(start, size), :]
            for ref in refs[used + 1 : used + addends]:
                total = total + ref[pl.ds(start, size), :]
            out[at : at + size] = total
            at, used = at + size, used + addends


def join_pieces_kernel(stage, layout, *refs):
    pieces = 1 << len(stage)
    out = refs[pieces]
    mine = index_in(stage)
    for m in range(pieces):
        at, base = 0, 0
        for _, rows in layout:
            size = rows // pieces
            start = pl.multiple_of(base + (mine ^ m) * size, PAD)
            out[pl.ds(start, size), :] = refs[m][at : at + size]
            at, base = at + size, base + rows


def pack_kernel(stage, cut, x_ref, extra_ref, *outs):
    own = x_ref.shape[0]
    mine = index_in(stage)
    size = extra_ref.shape[0] // (len(outs) if cut else 1)
    for m, out in enumerate(outs):
        start = pl.multiple_of((mine ^ m) * size, PAD) if cut else 0
        out[:own] = x_ref[...]
        out[own:] = extra_ref[pl.ds(start, size), :]


def merge_kernel(stage, layout, *refs):
    pieces = 1 << len(stage)
    join_pieces_kernel(stage, layout, *refs[: pieces + 1])
    own = sum(rows for _, rows in layout) // pieces
    total = refs[0][own:]
    for ref in refs[1:pieces]:
        total = total + ref[own:]
    refs[pieces + 1][...] = total


def rows_of(rows, width):
    return jax.ShapeDtypeStruct((rows, width), F32)


class Summer:
    def __init__(self, n_dp, n_seq):
        self.n_dp, self.n_seq = n_dp, n_seq
        bits = [("dp", b) for b in range(1, n_dp.bit_length() - 1)]
        seq = [("seq", b) for b in range(n_seq.bit_length() - 1)]
        rest = bits[:1] + seq[:1] + seq[1:] + bits[1:]
        self.core = [("dp", 0)]
        self.stages = [rest[k : k + 2] for k in range(0, len(rest), 2)]

    def send(self, x, stage, mask):
        d_mask = sum(1 << b for k, (a, b) in enumerate(stage) if a == "dp" and mask >> k & 1)
        s_mask = sum(1 << b for k, (a, b) in enumerate(stage) if a == "seq" and mask >> k & 1)
        perm = [
            (d * self.n_seq + s, (d ^ d_mask) * self.n_seq + (s ^ s_mask))
            for d in range(self.n_dp)
            for s in range(self.n_seq)
        ]
        return lax.ppermute(x, ("dp", "seq"), perm)

    def split(self, groups, stage):
        pieces = 1 << len(stage)
        layout = [(len(g), g[0].shape[0]) for g in groups]
        size = sum(rows for _, rows in layout) // pieces
        width = groups[0][0].shape[1]
        out = local_call(
            functools.partial(split_kernel, stage, layout),
            [rows_of(size, width)] * pieces,
            0.4,
            *[a for g in groups for a in g],
        )
        return out, layout

    def join(self, x, stage, layout):
        came = [x] + [self.send(x, stage, m) for m in range(1, 1 << len(stage))]
        total = sum(rows for _, rows in layout)
        return local_call(
            functools.partial(join_pieces_kernel, stage, layout),
            rows_of(total, x.shape[1]),
            0.4,
            *came,
        )

    def scatter(self, groups, stage):
        rows = [g[0].shape[0] for g in groups]
        if sum(rows) > WHOLE and min(rows) >> len(stage) >= PAD:
            out, layout = self.split(groups, stage)
        else:
            whole, layout = self.split(groups, [])
            out, layout = [whole[0]] * (1 << len(stage)), None
        return [[out[0]] + [self.send(out[m], stage, m) for m in range(1, len(out))]], layout

    def gather(self, x, stage, layout):
        return x if layout is None else self.join(x, stage, layout)

    def gather_with(self, x, stage, layout, extra, last_stage):
        if layout is None:
            groups, extra_layout = self.scatter([[extra]], stage)
            return x, self.split(groups, [])[0][0], extra_layout
        pieces = 1 << len(stage)
        rows, width = extra.shape
        cut = not last_stage and rows // pieces >= PAD
        size = rows // pieces if cut else rows
        own = x.shape[0]
        out = local_call(
            functools.partial(pack_kernel, stage, cut),
            [rows_of(own + size, width)] * (pieces if cut else 1),
            0.4,
            x,
            extra,
        )
        out = out if cut else out * pieces
        came = [out[0]] + [self.send(out[m], stage, m) for m in range(1, pieces)]
        total = sum(r for _, r in layout)
        x, extra = local_call(
            functools.partial(merge_kernel, stage, layout),
            [rows_of(total, width), rows_of(size, width)],
            0.4,
            *came,
        )
        return x, extra, [(1, rows)] if cut else None


def assemble_kernel(heads, half, own_ref, came_ref, out_ref):
    mine = lax.axis_index("dp") & 1
    for side, ref in enumerate((own_ref, came_ref)):
        for i in range(heads):
            start = pl.multiple_of((2 * i + (mine ^ side)) * half, PAD)
            out_ref[pl.ds(start, half), :] = ref[i * half : (i + 1) * half]


def solution(mesh):
    n_dp, n_seq = mesh.shape["dp"], mesh.shape["seq"]

    def shards(queries, keys, values, targets, q_map, k_map, doc_spans):
        hq, hd = q_map.shape[0], q_map.shape[1]
        hk = k_map.shape[0]
        group = hq // hk
        rows = queries.shape[1]
        count = rows // SPAN
        feats = 2 * hd
        tall = SPAN + PAD
        coef = 2.0 / math.sqrt(n_dp * n_seq * rows * hd)
        most = (3 * n_seq * count) // 8
        before = min(n_seq - 1, -(-(most - 1) // count))
        hops = max(1, before.bit_length())
        q2, t2 = queries[0], targets[0]
        k2, v2 = keys[0], values[0]
        parts = [(0, hk // 2), (hk // 2, hk)]
        array = jax.ShapeDtypeStruct
        out = local_call(
            functools.partial(key_kernel, count, parts),
            [array((hk, rows, feats), BF16), array((hk, count, tall, feats), F32)]
            + [rows_of((hi - lo) * tall, feats) for lo, hi in parts],
            3.0,
            k2,
            v2,
            k_map,
            spans=doc_spans,
        )
        feat_k, blocks, tails = out[0], out[1], out[2:]

        def shift(own, hop, reverse):
            step = n_seq - hop if reverse else hop
            return lax.ppermute(own, "seq", [(i, (i + step) % n_seq) for i in range(n_seq)])

        def join(own, got, hop, reverse):
            return local_call(
                functools.partial(join_kernel, count, hop, reverse),
                rows_of(*own.shape),
                0.6,
                own,
                got,
                spans=doc_spans,
            )

        def exchange(own, reverse, start=0):
            came = []
            for k in range(start, hops):
                came.append(shift(own, 1 << k, reverse))
                if k < hops - 1:
                    own = join(own, came[-1], 1 << k, reverse)
            return came

        def early(part):
            wide = lambda r, dtype: array((part[1] - part[0], count, r, group * SPAN), dtype)
            return local_call(
                functools.partial(early_kernel, part, count, group),
                [wide(hd, F32), wide(hd, F32), wide(feats, BF16), wide(hd, F32), wide(PAD, F32)]
                + [wide(hd, BF16)],
                3.0,
                q2,
                t2,
                v2,
                feat_k,
                q_map,
            )

        def late(part, ready, came):
            heads = part[1] - part[0]
            return local_call(
                functools.partial(late_kernel, part, count, group, hops, coef),
                [rows_of(heads * group * hd // 2, hd)] * 2
                + [rows_of(heads * tall, feats)]
                + [array((heads, count, tall, feats), F32), array((heads, count, SPAN, feats), F32)],
                6.0,
                q2,
                v2,
                feat_k,
                blocks,
                *ready,
                *came,
                spans=doc_spans,
            )

        def last(part, back, inner, came):
            return local_call(
                functools.partial(last_kernel, part, count, hops),
                rows_of((part[1] - part[0]) * hd, hd),
                1.5,
                k2,
                v2,
                k_map,
                back,
                inner,
                *came,
                spans=doc_spans,
            )

        total = Summer(n_dp, n_seq)
        came = [exchange(t, False) for t in tails]
        ready = [early(p) for p in parts]
        first = late(parts[0], ready[0], came[0])
        back_one = shift(first[2], 1, True)
        core_one = total.send(first[1], total.core, 1)
        second = late(parts[1], ready[1], came[1])
        joined = join(first[2], back_one, 1, True)
        joined, core_one, *second = lax.optimization_barrier((joined, core_one, *second))
        back_two = [shift(second[2], 1, True)]
        core_two = total.send(second[1], total.core, 1)
        back_one = [back_one] + exchange(joined, True, 1)
        groups, layout = total.scatter([[first[0], core_one], [second[0], core_two]], total.stages[0])
        layouts = [layout]
        joined = join(second[2], back_two[0], 1, True)
        groups, joined, back_one = lax.optimization_barrier((groups, joined, back_one))
        back_two += exchange(joined, True, 1)
        for stage in total.stages[1:]:
            groups, layout = total.scatter(groups, stage)
            layouts.append(layout)
        x = total.split(groups, [])[0][0]
        x, back_two = lax.optimization_barrier((x, back_two))
        gk = [
            last(p, m[3], m[4], b)
            for p, m, b in zip(parts, (first, second), (back_one, back_two))
        ]
        out, core_layout = total.split([[g] for g in gk], total.core)
        extra = total.split([[out[0], total.send(out[1], total.core, 1)]], [])[0][0]
        x, extra = lax.optimization_barrier((x, extra))
        extra_layouts = []
        for k in reversed(range(len(total.stages))):
            x, extra, layout = total.gather_with(x, total.stages[k], layouts[k], extra, k == 0)
            extra_layouts.append((total.stages[k], layout))
        halves = [x, total.send(x, total.core, 1)]
        for stage, layout in reversed(extra_layouts):
            extra = total.gather(extra, stage, layout)
        grad_q = local_call(
            functools.partial(assemble_kernel, hk, group * hd // 2),
            rows_of(hq * hd, hd),
            1.0,
            *halves,
        )
        grad_k = total.join(extra, total.core, core_layout)
        return grad_q.reshape(hq, hd, hd), grad_k.reshape(hk, hd, hd)

    in_specs = (
        P("dp", "seq", None),
        P("dp", "seq", None),
        P("dp", "seq", None),
        P("dp", "seq", None),
        P(),
        P(),
        P("dp", None),
    )
    return jax.shard_map(
        shards, mesh=mesh, in_specs=in_specs, out_specs=(P(), P()), check_vma=False
    )
```

time: 145 us -> 126 us (0.87)
  starting transfers between devices: 61.5 us -> 41.2 us
  waiting for transfers between devices: 48.1 us -> 54 us
  Pallas kernels: 30.7 us -> 26.5 us
    ppermute x30 -> x20, starting transfers between devices: 51.2 us -> 23.4 us  [send(): return lax.ppermute(x, ('dp', 'seq'), perm)]
    ppermute x8, starting transfers between devices: 10.3 us -> 17.8 us  [shift(): lax.ppermute(own, 'seq', [(i, (i + step) % n_seq) for i in range(n_seq)])]
    ppermute x30 -> x20, waiting for transfers between devices: 27.6 us -> 32.6 us  [send(): return lax.ppermute(x, ('dp', 'seq'), perm)]
    pallas_call x23, Pallas kernels: 30.7 us -> 26.5 us  [local_call(): pl.pallas_call(body, out_shape=out_shape, in_specs=[SMEM] * len(first) +...]
    unnamed x16 -> x22, local copies, waits for them, and re-layouts: 3.56 us -> 3.48 us
  transfers between devices with their start and end apart: 38 -> 28, of which waited for: 16 -> 19; matrix products, arithmetic and copies ran while one was open for 0% -> 0% of each run, Pallas kernels for 18% -> 17%
where the time goes in v2:
time: 126 us
  waiting for transfers between devices  54 us (43%)
  starting transfers between devices  41.2 us (33%)
  Pallas kernels  26.5 us (21%)
  local copies, waits for them, and re-layouts  3.48 us (3%)
    ppermute x20, waiting for transfers between devices, send(): return lax.ppermute(x, ('dp', 'seq'), perm)  32.6 us
    pallas_call x23, Pallas kernels, local_call(): pl.pallas_call(body, out_shape=out_shape, in_specs=[SMEM] * len(first) +...  26.5 us
    ppermute x20, starting transfers between devices, send(): return lax.ppermute(x, ('dp', 'seq'), perm)  23.4 us
    ppermute x8, waiting for transfers between devices, shift(): lax.ppermute(own, 'seq', [(i, (i + step) % n_seq) for i in range(n_seq)])  21.4 us
    ppermute x8, starting transfers between devices, shift(): lax.ppermute(own, 'seq', [(i, (i + step) % n_seq) for i in range(n_seq)])  17.8 us
    unnamed x22, local copies, waits for them, and re-layouts  3.48 us
  transfers between devices with their start and end apart: 28, of which 19 were waited for; matrix products, arithmetic and copies ran while one was open for 0% of the time, Pallas kernels for 17%

profile of v2, /device:TPU:0, one launch (start us, length us, event | category | flops | bytes accessed | tf_op | source)
XLA Modules:
  0.0 126.1 jit_solution(6727921852332265472)
XLA Ops:
  4.1 2.2 %shard_map.86 = (bf16[4,256,256]{2,1,0:T(8,128)(2,1)S(1)}, f32[4,2,136,256]{3,2,1,0:T(8,128)S(1)}, f32[272,256]{1,0:T(8,128)S(1)}, f32[272,256]{1,0:T(8,128)S(1)}) custom-call(s32[1,8]{1,0:T(1,128)S(1)} %copy-done.9, bf16[256,512]{1,0:T(8,128)(2,1)S(1)} %bitcast.19, bf16[256,512]{1,0:T(8,128)(2,1)S(1)} %bitcast.12, bf16[4,128,128]{2,1,0:T(8,128)(2,1)S(1)} %copy-done.7), custom_call_target="tpu_custom_call" | custom-call | flops 3000000000 | tf_op jit(solution)/shard_map/pallas_call | solution.py:235
  6.3 3.0 %collective-permute-start = (f32[272,256]{1,0:T(8,128)S(1)}, f32[272,256]{1,0:T(8,128)S(1)}, u32[]{:S(2)}, u32[]{:S(2)}) collective-permute-start(f32[272,256]{1,0:T(8,128)S(1)} %get-tuple-element.73.own_ref), channel_id=1, source_target_pairs={{0,1},{1,2},{2,3},{3,4},{4,5},{5,6},{6,7},{7,0},{8,9},{9,10},{10,1... | collective-permute-start | bytes 835592 | tf_op jit(solution)/shard_map/ppermute | solution.py:427
  10.9 2.9 %shard_map.91 = (f32[2,2,128,1024]{3,2,1,0:T(8,128)S(1)}, f32[2,2,128,1024]{3,2,1,0:T(8,128)S(1)}, bf16[2,2,256,1024]{3,2,1,0:T(8,128)(2,1)S(1)}, f32[2,2,128,10...) custom-call(bf16[256,4096]{1,0:T(8,128)(2,1)S(1)} %bitcast.8, ...), custom_call_target="tpu_custom_call" | custom-call | flops 3000000000 | tf_op jit(solution)/shard_map/pallas_call | solution.py:235
  13.8 6.1 %collective-permute-done.came_ref.refs_11_ = f32[272,256]{1,0:T(8,128)S(1)} collective-permute-done((f32[272,256]{1,0:T(8,128)S(1)}, f32[272,256]{1,0:T(8,128)S(1)}, u32[]{:S(2)}, u32[]{:S(2)}) %collective-permute-start) | collective-permute-done | bytes 278560 | tf_op jit(solution)/shard_map/ppermute | solution.py:427
  20.5 2.9 %shard_map.87 = (f32[2,2,128,1024]{3,2,1,0:T(8,128)S(1)}, f32[2,2,128,1024]{3,2,1,0:T(8,128)S(1)}, bf16[2,2,256,1024]{3,2,1,0:T(8,128)(2,1)S(1)}, f32[2,2,128,10...) custom-call(bf16[256,4096]{1,0:T(8,128)(2,1)S(1)} %bitcast.9, ...), custom_call_target="tpu_custom_call" | custom-call | flops 3000000000 | tf_op jit(solution)/shard_map/pallas_call | solution.py:235
  23.4 2.4 %collective-permute-done.4.came_ref.refs_11_ = f32[272,256]{1,0:T(8,128)S(1)} collective-permute-done((f32[272,256]{1,0:T(8,128)S(1)}, f32[272,256]{1,0:T(8,128)S(1)}, u32[]{:S(2)}, u32[]{:S(2)}) %collective-permute-start.4) | collective-permute-done | bytes 278560 | tf_op jit(solution)/shard_map/ppermute | solution.py:427
  26.5 2.8 %collective-permute-done.1.refs_12_ = f32[272,256]{1,0:T(8,128)S(1)} collective-permute-done((f32[272,256]{1,0:T(8,128)S(1)}, f32[272,256]{1,0:T(8,128)S(1)}, u32[]{:S(2)}, u32[]{:S(2)}) %collective-permute-start.1) | collective-permute-done | bytes 278560 | tf_op jit(solution)/shard_map/ppermute | solution.py:427
  29.3 5.4 %shard_map.89 = (f32[1024,128]{1,0:T(8,128)S(1)}, f32[1024,128]{1,0:T(8,128)S(1)}, f32[272,256]{1,0:T(8,128)S(1)}, f32[2,2,136,256]{3,2,1,0:T(8,128)S(1)}, f32[2,2,128,256]{3,2,1,0:T(8,128)S(1)}) custom-call(s32[1,8]{1,0:T(1,128)S(1)} %copy-done.9, bf16[256,4096]{1,0:T(8,128)(2,1)S(1)} %bitcast.10, bf16[256,512]{1,0:T(8,128)(2,1)S(1)} %bitcast.15, ...), custom_call_target="tpu_custom_call" | custom-call | flops 6000000000 | tf_op jit(solution)/shard_map/pallas_call | solution.py:235
  34.7 4.7 %collective-permute-start.2 = (f32[272,256]{1,0:T(8,128)S(1)}, f32[272,256]{1,0:T(8,128)S(1)}, u32[]{:S(2)}, u32[]{:S(2)}) collective-permute-start(f32[272,256]{1,0:T(8,128)S(1)} %get-tuple-element.75.own_ref), channel_id=1, source_target_pairs={{0,7},{1,0},{2,1},{3,2},{4,3},{5,4},{6,5},{7,6},{8,15},{9,8},{10,9... | collective-permute-start | bytes 835592 | tf_op jit(solution)/shard_map/ppermute | solution.py:427
  39.5 5.1 %shard_map.93 = (f32[1024,128]{1,0:T(8,128)S(1)}, f32[1024,128]{1,0:T(8,128)S(1)}, f32[272,256]{1,0:T(8,128)S(1)}, f32[2,2,136,256]{3,2,1,0:T(8,128)S(1)}, f32[2,2,128,256]{3,2,1,0:T(8,128)S(1)}) custom-call(s32[1,8]{1,0:T(1,128)S(1)} %copy-done.9, bf16[256,4096]{1,0:T(8,128)(2,1)S(1)} %bitcast.11, bf16[256,512]{1,0:T(8,128)(2,1)S(1)} %bitcast.16, ...), custom_call_target="tpu_custom_call" | custom-call | flops 6000000000 | tf_op jit(solution)/shard_map/pallas_call | solution.py:235
  45.8 3.6 %collective-permute-start.10 = (f32[272,256]{1,0:T(8,128)S(1)}, f32[272,256]{1,0:T(8,128)S(1)}, u32[]{:S(2)}, u32[]{:S(2)}) collective-permute-start(f32[272,256]{1,0:T(8,128)S(1)} %get-tuple-element.96.own_ref), channel_id=1, source_target_pairs={{0,7},{1,0},{2,1},{3,2},{4,3},{5,4},{6,5},{7,6},{8,15},{9,8},{10,9... | collective-permute-start | bytes 835592 | tf_op jit(solution)/shard_map/ppermute | solution.py:427
  53.1 4.5 %collective-permute-done.10.came_ref.refs_6_ = f32[272,256]{1,0:T(8,128)S(1)} collective-permute-done((f32[272,256]{1,0:T(8,128)S(1)}, f32[272,256]{1,0:T(8,128)S(1)}, u32[]{:S(2)}, u32[]{:S(2)}) %collective-permute-start.10) | collective-permute-done | bytes 278560 | tf_op jit(solution)/shard_map/ppermute | solution.py:427
  58.2 5.6 %collective-permute-done.11.refs_7_ = f32[272,256]{1,0:T(8,128)S(1)} collective-permute-done((f32[272,256]{1,0:T(8,128)S(1)}, f32[272,256]{1,0:T(8,128)S(1)}, u32[]{:S(2)}, u32[]{:S(2)}) %collective-permute-start.11) | collective-permute-done | bytes 278560 | tf_op jit(solution)/shard_map/ppermute | solution.py:427
  65.7 4.8 %collective-permute-start.15 = (f32[272,256]{1,0:T(8,128)S(1)}, f32[272,256]{1,0:T(8,128)S(1)}, u32[]{:S(2)}, u32[]{:S(2)}) collective-permute-start(f32[272,256]{1,0:T(8,128)S(1)} %shard_map.95), channel_id=1, source_target_pairs={{0,6},{1,7},{2,0},{3,1},{4,2},{5,3},{6,4},{7,5},{8,14},{9,15},{10,... | collective-permute-start | bytes 835592 | tf_op jit(solution)/shard_map/ppermute | solution.py:427
  71.2 3.8 %collective-permute-start.14 = (f32[128,128]{1,0:T(8,128)S(1)}, f32[128,128]{1,0:T(8,128)S(1)}, u32[]{:S(2)}, u32[]{:S(2)}) collective-permute-start(f32[128,128]{1,0:T(8,128)S(1)} %get-tuple-element.105), channel_id=1, source_target_pairs={{0,6},{1,7},{2,4},{3,5},{4,2},{5,3},{6,0},{7,1},{8,14},{9,15},{10,... | collective-permute-start | bytes 196616 | tf_op jit(solution)/shard_map/ppermute | solution.py:321
  76.5 2.5 %collective-permute-done.12.refs_1_ = f32[128,128]{1,0:T(8,128)S(1)} collective-permute-done((f32[128,128]{1,0:T(8,128)S(1)}, f32[128,128]{1,0:T(8,128)S(1)}, u32[]{:S(2)}, u32[]{:S(2)}) %collective-permute-start.12) | collective-permute-done | bytes 65568 | tf_op jit(solution)/shard_map/ppermute | solution.py:321
  84.5 2.2 %collective-permute-start.17 = (f32[192,128]{1,0:T(8,128)S(1)}, f32[192,128]{1,0:T(8,128)S(1)}, u32[]{:S(2)}, u32[]{:S(2)}) collective-permute-start(f32[192,128]{1,0:T(8,128)S(1)} %get-tuple-element.121), channel_id=1, source_target_pairs={{0,2},{1,3},{2,0},{3,1},{4,6},{5,7},{6,4},{7,5},{8,10},{9,11},{10,... | collective-permute-start | bytes 294920 | tf_op jit(solution)/shard_map/ppermute | solution.py:321
  90.1 2.3 %collective-permute-done.18.refs_2_ = f32[192,128]{1,0:T(8,128)S(1)} collective-permute-done((f32[192,128]{1,0:T(8,128)S(1)}, f32[192,128]{1,0:T(8,128)S(1)}, u32[]{:S(2)}, u32[]{:S(2)}) %collective-permute-start.18) | collective-permute-done | bytes 98336 | tf_op jit(solution)/shard_map/ppermute | solution.py:321
  92.4 4.9 %collective-permute-done.19.refs_3_ = f32[192,128]{1,0:T(8,128)S(1)} collective-permute-done((f32[192,128]{1,0:T(8,128)S(1)}, f32[192,128]{1,0:T(8,128)S(1)}, u32[]{:S(2)}, u32[]{:S(2)}) %collective-permute-start.19) | collective-permute-done | bytes 98336 | tf_op jit(solution)/shard_map/ppermute | solution.py:321
  97.3 2.1 %collective-permute-start.22 = (f32[576,128]{1,0:T(8,128)S(1)}, f32[576,128]{1,0:T(8,128)S(1)}, u32[]{:S(2)}, u32[]{:S(2)}) collective-permute-start(f32[576,128]{1,0:T(8,128)S(1)} %shard_map.104.refs_0_), channel_id=1, source_target_pairs={{0,17},{1,16},{2,19},{3,18},{4,21},{5,20},{6,23},{7,22},{8,25},{9,... | collective-permute-start | bytes 884744 | tf_op jit(solution)/shard_map/ppermute | solution.py:321
  101.3 6.9 %collective-permute-done.22.refs_3_ = f32[576,128]{1,0:T(8,128)S(1)} collective-permute-done((f32[576,128]{1,0:T(8,128)S(1)}, f32[576,128]{1,0:T(8,128)S(1)}, u32[]{:S(2)}, u32[]{:S(2)}) %collective-permute-start.22) | collective-permute-done | bytes 294944 | tf_op jit(solution)/shard_map/ppermute | solution.py:321
  108.2 4.5 %collective-permute-done.21.refs_2_ = f32[576,128]{1,0:T(8,128)S(1)} collective-permute-done((f32[576,128]{1,0:T(8,128)S(1)}, f32[576,128]{1,0:T(8,128)S(1)}, u32[]{:S(2)}, u32[]{:S(2)}) %collective-permute-start.21) | collective-permute-done | bytes 294944 | tf_op jit(solution)/shard_map/ppermute | solution.py:321
  114.0 3.3 %collective-permute-start.26 = (f32[64,128]{1,0:T(8,128)S(1)}, f32[64,128]{1,0:T(8,128)S(1)}, u32[]{:S(2)}, u32[]{:S(2)}) collective-permute-start(f32[64,128]{1,0:T(8,128)S(1)} %get-tuple-element.127.refs_0_), channel_id=1, source_target_pairs={{0,6},{1,7},{2,4},{3,5},{4,2},{5,3},{6,0},{7,1},{8,14},{9,15},{10,... | collective-permute-start | bytes 98312 | tf_op jit(solution)/shard_map/ppermute | solution.py:321
  119.8 2.3 %collective-permute-done.25.refs_2_ = f32[64,128]{1,0:T(8,128)S(1)} collective-permute-done((f32[64,128]{1,0:T(8,128)S(1)}, f32[64,128]{1,0:T(8,128)S(1)}, u32[]{:S(2)}, u32[]{:S(2)}) %collective-permute-start.25) | collective-permute-done | bytes 32800 | tf_op jit(solution)/shard_map/ppermute | solution.py:321
  (77 shorter events, 34.3 us)
Async XLA Ops:
  6.3 13.5 %collective-permute-start = (f32[272,256]{1,0:T(8,128)S(1)}, f32[272,256]{1,0:T(8,128)S(1)}, u32[]{:S(2)}, u32[]{:S(2)}) collective-permute-start(f32[272,256]{1,0:T(8,128)S(1)} %get-tuple-element.73.own_ref), channel_id=1, source_target_pairs={{0,1},{1,2},{2,3},{3,4},{4,5},{5,6},{6,7},{7,0},{8,9},{9,10},{10,1... | collective-permute-start | bytes 835592 | tf_op jit(solution)/shard_map/ppermute | solution.py:427
  9.3 16.5 %collective-permute-start.4 = (f32[272,256]{1,0:T(8,128)S(1)}, f32[272,256]{1,0:T(8,128)S(1)}, u32[]{:S(2)}, u32[]{:S(2)}) collective-permute-start(f32[272,256]{1,0:T(8,128)S(1)} %get-tuple-element.83.own_ref), channel_id=1, source_target_pairs={{0,1},{1,2},{2,3},{3,4},{4,5},{5,6},{6,7},{7,0},{8,9},{9,10},{10,1... | collective-permute-start | bytes 835592 | tf_op jit(solution)/shard_map/ppermute | solution.py:427
  20.4 8.9 %collective-permute-start.1 = (f32[272,256]{1,0:T(8,128)S(1)}, f32[272,256]{1,0:T(8,128)S(1)}, u32[]{:S(2)}, u32[]{:S(2)}) collective-permute-start(f32[272,256]{1,0:T(8,128)S(1)} %shard_map.88), channel_id=1, source_target_pairs={{0,2},{1,3},{2,4},{3,5},{4,6},{5,7},{6,0},{7,1},{8,10},{9,11},{10,... | collective-permute-start | bytes 835592 | tf_op jit(solution)/shard_map/ppermute | solution.py:427
  26.4 13.1 %collective-permute-start.5 = (f32[272,256]{1,0:T(8,128)S(1)}, f32[272,256]{1,0:T(8,128)S(1)}, u32[]{:S(2)}, u32[]{:S(2)}) collective-permute-start(f32[272,256]{1,0:T(8,128)S(1)} %shard_map.92), channel_id=1, source_target_pairs={{0,2},{1,3},{2,4},{3,5},{4,6},{5,7},{6,0},{7,1},{8,10},{9,11},{10,... | collective-permute-start | bytes 835592 | tf_op jit(solution)/shard_map/ppermute | solution.py:427
  34.7 9.9 %collective-permute-start.2 = (f32[272,256]{1,0:T(8,128)S(1)}, f32[272,256]{1,0:T(8,128)S(1)}, u32[]{:S(2)}, u32[]{:S(2)}) collective-permute-start(f32[272,256]{1,0:T(8,128)S(1)} %get-tuple-element.75.own_ref), channel_id=1, source_target_pairs={{0,7},{1,0},{2,1},{3,2},{4,3},{5,4},{6,5},{7,6},{8,15},{9,8},{10,9... | collective-permute-start | bytes 835592 | tf_op jit(solution)/shard_map/ppermute | solution.py:427
  39.5 5.8 %collective-permute-start.3 = (f32[1024,128]{1,0:T(8,128)S(1)}, f32[1024,128]{1,0:T(8,128)S(1)}, u32[]{:S(2)}, u32[]{:S(2)}) collective-permute-start(f32[1024,128]{1,0:T(8,128)S(1)} %get-tuple-element.76), channel_id=1, source_target_pairs={{0,8},{1,9},{2,10},{3,11},{4,12},{5,13},{6,14},{7,15},{8,0},{9,1},... | collective-permute-start | bytes 1572872 | tf_op jit(solution)/shard_map/ppermute | solution.py:321
  45.8 11.8 %collective-permute-start.10 = (f32[272,256]{1,0:T(8,128)S(1)}, f32[272,256]{1,0:T(8,128)S(1)}, u32[]{:S(2)}, u32[]{:S(2)}) collective-permute-start(f32[272,256]{1,0:T(8,128)S(1)} %get-tuple-element.96.own_ref), channel_id=1, source_target_pairs={{0,7},{1,0},{2,1},{3,2},{4,3},{5,4},{6,5},{7,6},{8,15},{9,8},{10,9... | collective-permute-start | bytes 835592 | tf_op jit(solution)/shard_map/ppermute | solution.py:427
  49.4 14.4 %collective-permute-start.11 = (f32[272,256]{1,0:T(8,128)S(1)}, f32[272,256]{1,0:T(8,128)S(1)}, u32[]{:S(2)}, u32[]{:S(2)}) collective-permute-start(f32[272,256]{1,0:T(8,128)S(1)} %shard_map.90), channel_id=1, source_target_pairs={{0,6},{1,7},{2,0},{3,1},{4,2},{5,3},{6,4},{7,5},{8,14},{9,15},{10,... | collective-permute-start | bytes 835592 | tf_op jit(solution)/shard_map/ppermute | solution.py:427
  49.6 14.3 %collective-permute-start.7 = (f32[512,128]{1,0:T(8,128)S(1)}, f32[512,128]{1,0:T(8,128)S(1)}, u32[]{:S(2)}, u32[]{:S(2)}) collective-permute-start(f32[512,128]{1,0:T(8,128)S(1)} %get-tuple-element.93), channel_id=1, source_target_pairs={{0,16},{1,17},{2,18},{3,19},{4,20},{5,21},{6,22},{7,23},{8,24},{9,... | collective-permute-start | bytes 786440 | tf_op jit(solution)/shard_map/ppermute | solution.py:321
  51.1 14.5 %collective-permute-start.8 = (f32[512,128]{1,0:T(8,128)S(1)}, f32[512,128]{1,0:T(8,128)S(1)}, u32[]{:S(2)}, u32[]{:S(2)}) collective-permute-start(f32[512,128]{1,0:T(8,128)S(1)} %get-tuple-element.94), channel_id=1, source_target_pairs={{0,1},{1,0},{2,3},{3,2},{4,5},{5,4},{6,7},{7,6},{8,9},{9,8},{10,11... | collective-permute-start | bytes 786440 | tf_op jit(solution)/shard_map/ppermute | solution.py:321
  51.8 13.9 %collective-permute-start.9 = (f32[512,128]{1,0:T(8,128)S(1)}, f32[512,128]{1,0:T(8,128)S(1)}, u32[]{:S(2)}, u32[]{:S(2)}) collective-permute-start(f32[512,128]{1,0:T(8,128)S(1)} %get-tuple-element.95), channel_id=1, source_target_pairs={{0,17},{1,16},{2,19},{3,18},{4,21},{5,20},{6,23},{7,22},{8,25},{9,... | collective-permute-start | bytes 786440 | tf_op jit(solution)/shard_map/ppermute | solution.py:321
  65.7 15.9 %collective-permute-start.15 = (f32[272,256]{1,0:T(8,128)S(1)}, f32[272,256]{1,0:T(8,128)S(1)}, u32[]{:S(2)}, u32[]{:S(2)}) collective-permute-start(f32[272,256]{1,0:T(8,128)S(1)} %shard_map.95), channel_id=1, source_target_pairs={{0,6},{1,7},{2,0},{3,1},{4,2},{5,3},{6,4},{7,5},{8,14},{9,15},{10,... | collective-permute-start | bytes 835592 | tf_op jit(solution)/shard_map/ppermute | solution.py:427
  70.5 8.4 %collective-permute-start.12 = (f32[128,128]{1,0:T(8,128)S(1)}, f32[128,128]{1,0:T(8,128)S(1)}, u32[]{:S(2)}, u32[]{:S(2)}) collective-permute-start(f32[128,128]{1,0:T(8,128)S(1)} %get-tuple-element.103), channel_id=1, source_target_pairs={{0,2},{1,3},{2,0},{3,1},{4,6},{5,7},{6,4},{7,5},{8,10},{9,11},{10,... | collective-permute-start | bytes 196616 | tf_op jit(solution)/shard_map/ppermute | solution.py:321
  70.6 9.5 %collective-permute-start.13 = (f32[128,128]{1,0:T(8,128)S(1)}, f32[128,128]{1,0:T(8,128)S(1)}, u32[]{:S(2)}, u32[]{:S(2)}) collective-permute-start(f32[128,128]{1,0:T(8,128)S(1)} %get-tuple-element.104), channel_id=1, source_target_pairs={{0,4},{1,5},{2,6},{3,7},{4,0},{5,1},{6,2},{7,3},{8,12},{9,13},{10,... | collective-permute-start | bytes 196616 | tf_op jit(solution)/shard_map/ppermute | solution.py:321
  71.2 10.3 %collective-permute-start.14 = (f32[128,128]{1,0:T(8,128)S(1)}, f32[128,128]{1,0:T(8,128)S(1)}, u32[]{:S(2)}, u32[]{:S(2)}) collective-permute-start(f32[128,128]{1,0:T(8,128)S(1)} %get-tuple-element.105), channel_id=1, source_target_pairs={{0,6},{1,7},{2,4},{3,5},{4,2},{5,3},{6,0},{7,1},{8,14},{9,15},{10,... | collective-permute-start | bytes 196616 | tf_op jit(solution)/shard_map/ppermute | solution.py:321
  84.5 5.6 %collective-permute-start.17 = (f32[192,128]{1,0:T(8,128)S(1)}, f32[192,128]{1,0:T(8,128)S(1)}, u32[]{:S(2)}, u32[]{:S(2)}) collective-permute-start(f32[192,128]{1,0:T(8,128)S(1)} %get-tuple-element.121), channel_id=1, source_target_pairs={{0,2},{1,3},{2,0},{3,1},{4,6},{5,7},{6,4},{7,5},{8,10},{9,11},{10,... | collective-permute-start | bytes 294920 | tf_op jit(solution)/shard_map/ppermute | solution.py:321
  86.7 5.6 %collective-permute-start.18 = (f32[192,128]{1,0:T(8,128)S(1)}, f32[192,128]{1,0:T(8,128)S(1)}, u32[]{:S(2)}, u32[]{:S(2)}) collective-permute-start(f32[192,128]{1,0:T(8,128)S(1)} %get-tuple-element.122), channel_id=1, source_target_pairs={{0,4},{1,5},{2,6},{3,7},{4,0},{5,1},{6,2},{7,3},{8,12},{9,13},{10,... | collective-permute-start | bytes 294920 | tf_op jit(solution)/shard_map/ppermute | solution.py:321
  88.8 8.4 %collective-permute-start.19 = (f32[192,128]{1,0:T(8,128)S(1)}, f32[192,128]{1,0:T(8,128)S(1)}, u32[]{:S(2)}, u32[]{:S(2)}) collective-permute-start(f32[192,128]{1,0:T(8,128)S(1)} %get-tuple-element.123), channel_id=1, source_target_pairs={{0,6},{1,7},{2,4},{3,5},{4,2},{5,3},{6,0},{7,1},{8,14},{9,15},{10,... | collective-permute-start | bytes 294920 | tf_op jit(solution)/shard_map/ppermute | solution.py:321
  97.3 11.0 %collective-permute-start.22 = (f32[576,128]{1,0:T(8,128)S(1)}, f32[576,128]{1,0:T(8,128)S(1)}, u32[]{:S(2)}, u32[]{:S(2)}) collective-permute-start(f32[576,128]{1,0:T(8,128)S(1)} %shard_map.104.refs_0_), channel_id=1, source_target_pairs={{0,17},{1,16},{2,19},{3,18},{4,21},{5,20},{6,23},{7,22},{8,25},{9,... | collective-permute-start | bytes 884744 | tf_op jit(solution)/shard_map/ppermute | solution.py:321
  99.4 13.4 %collective-permute-start.21 = (f32[576,128]{1,0:T(8,128)S(1)}, f32[576,128]{1,0:T(8,128)S(1)}, u32[]{:S(2)}, u32[]{:S(2)}) collective-permute-start(f32[576,128]{1,0:T(8,128)S(1)} %shard_map.104.refs_0_), channel_id=1, source_target_pairs={{0,1},{1,0},{2,3},{3,2},{4,5},{5,4},{6,7},{7,6},{8,9},{9,8},{10,11... | collective-permute-start | bytes 884744 | tf_op jit(solution)/shard_map/ppermute | solution.py:321
  99.9 13.9 %collective-permute-start.20 = (f32[576,128]{1,0:T(8,128)S(1)}, f32[576,128]{1,0:T(8,128)S(1)}, u32[]{:S(2)}, u32[]{:S(2)}) collective-permute-start(f32[576,128]{1,0:T(8,128)S(1)} %shard_map.104.refs_0_), channel_id=1, source_target_pairs={{0,16},{1,17},{2,18},{3,19},{4,20},{5,21},{6,22},{7,23},{8,24},{9,... | collective-permute-start | bytes 884744 | tf_op jit(solution)/shard_map/ppermute | solution.py:321
  113.9 10.7 %collective-permute-start.23 = (f32[2048,128]{1,0:T(8,128)S(1)}, f32[2048,128]{1,0:T(8,128)S(1)}, u32[]{:S(2)}, u32[]{:S(2)}) collective-permute-start(f32[2048,128]{1,0:T(8,128)S(1)} %get-tuple-element.126.own_ref), channel_id=1, source_target_pairs={{0,8},{1,9},{2,10},{3,11},{4,12},{5,13},{6,14},{7,15},{8,0},{9,1},... | collective-permute-start | bytes 3145736 | tf_op jit(solution)/shard_map/ppermute | solution.py:321
  114.0 5.8 %collective-permute-start.26 = (f32[64,128]{1,0:T(8,128)S(1)}, f32[64,128]{1,0:T(8,128)S(1)}, u32[]{:S(2)}, u32[]{:S(2)}) collective-permute-start(f32[64,128]{1,0:T(8,128)S(1)} %get-tuple-element.127.refs_0_), channel_id=1, source_target_pairs={{0,6},{1,7},{2,4},{3,5},{4,2},{5,3},{6,0},{7,1},{8,14},{9,15},{10,... | collective-permute-start | bytes 98312 | tf_op jit(solution)/shard_map/ppermute | solution.py:321
  117.3 4.8 %collective-permute-start.25 = (f32[64,128]{1,0:T(8,128)S(1)}, f32[64,128]{1,0:T(8,128)S(1)}, u32[]{:S(2)}, u32[]{:S(2)}) collective-permute-start(f32[64,128]{1,0:T(8,128)S(1)} %get-tuple-element.127.refs_0_), channel_id=1, source_target_pairs={{0,4},{1,5},{2,6},{3,7},{4,0},{5,1},{6,2},{7,3},{8,12},{9,13},{10,... | collective-permute-start | bytes 98312 | tf_op jit(solution)/shard_map/ppermute | solution.py:321
  (15 other events, 105.3 us)

commit v3 on v2

--- a/solution.py
+++ b/solution.py
@@ -56,7 +56,15 @@
     return jnp.broadcast_to(row, (PAD, row.shape[1]))
 
 
-def key_kernel(count, parts, spans_ref, k_ref, v_ref, w_ref, feat_ref, block_ref, *tail_refs):
+def key_kernel(count, parts, spans_hbm, k_hbm, v_hbm, w_hbm, feat_ref, block_ref, *rest):
+    tail_refs = rest[: len(parts)]
+    spans_ref, k_ref, v_ref, w_ref, sems = rest[len(parts) :]
+    pairs = [(spans_hbm, spans_ref), (k_hbm, k_ref), (w_hbm, w_ref), (v_hbm, v_ref)]
+    copies = [pltpu.make_async_copy(a, b, sems.at[n]) for n, (a, b) in enumerate(pairs)]
+    for copy in copies:
+        copy.start()
+    for copy in copies:
+        copy.wait()
     width = w_ref.shape[-1]
     first = lax.axis_index("seq") * count
     starts = [bounds(spans_ref, first + c)[0] for c in range(count)]
@@ -277,26 +285,6 @@
             at, base = at + size, base + rows
 
 
-def pack_kernel(stage, cut, x_ref, extra_ref, *outs):
-    own = x_ref.shape[0]
-    mine = index_in(stage)
-    size = extra_ref.shape[0] // (len(outs) if cut else 1)
-    for m, out in enumerate(outs):
-        start = pl.multiple_of((mine ^ m) * size, PAD) if cut else 0
-        out[:own] = x_ref[...]
-        out[own:] = extra_ref[pl.ds(start, size), :]
-
-
-def merge_kernel(stage, layout, *refs):
-    pieces = 1 << len(stage)
-    join_pieces_kernel(stage, layout, *refs[: pieces + 1])
-    own = sum(rows for _, rows in layout) // pieces
-    total = refs[0][own:]
-    for ref in refs[1:pieces]:
-        total = total + ref[own:]
-    refs[pieces + 1][...] = total
-
-
 def rows_of(rows, width):
     return jax.ShapeDtypeStruct((rows, width), F32)
 
@@ -343,9 +331,9 @@
             *came,
         )
 
-    def scatter(self, groups, stage):
+    def scatter(self, groups, stage, whole=WHOLE):
         rows = [g[0].shape[0] for g in groups]
-        if sum(rows) > WHOLE and min(rows) >> len(stage) >= PAD:
+        if sum(rows) > whole and min(rows) >> len(stage) >= PAD:
             out, layout = self.split(groups, stage)
         else:
             whole, layout = self.split(groups, [])
@@ -354,33 +342,6 @@
 
     def gather(self, x, stage, layout):
         return x if layout is None else self.join(x, stage, layout)
-
-    def gather_with(self, x, stage, layout, extra, last_stage):
-        if layout is None:
-            groups, extra_layout = self.scatter([[extra]], stage)
-            return x, self.split(groups, [])[0][0], extra_layout
-        pieces = 1 << len(stage)
-        rows, width = extra.shape
-        cut = not last_stage and rows // pieces >= PAD
-        size = rows // pieces if cut else rows
-        own = x.shape[0]
-        out = local_call(
-            functools.partial(pack_kernel, stage, cut),
-            [rows_of(own + size, width)] * (pieces if cut else 1),
-            0.4,
-            x,
-            extra,
-        )
-        out = out if cut else out * pieces
-        came = [out[0]] + [self.send(out[m], stage, m) for m in range(1, pieces)]
-        total = sum(r for _, r in layout)
-        x, extra = local_call(
-            functools.partial(merge_kernel, stage, layout),
-            [rows_of(total, width), rows_of(size, width)],
-            0.4,
-            *came,
-        )
-        return x, extra, [(1, rows)] if cut else None
 
 
 def assemble_kernel(heads, half, own_ref, came_ref, out_ref):
@@ -410,21 +371,27 @@
         k2, v2 = keys[0], values[0]
         parts = [(0, hk // 2), (hk // 2, hk)]
         array = jax.ShapeDtypeStruct
-        out = local_call(
+        out = pl.pallas_call(
             functools.partial(key_kernel, count, parts),
-            [array((hk, rows, feats), BF16), array((hk, count, tall, feats), F32)]
+            out_shape=[array((hk, rows, feats), BF16), array((hk, count, tall, feats), F32)]
             + [rows_of((hi - lo) * tall, feats) for lo, hi in parts],
-            3.0,
-            k2,
-            v2,
-            k_map,
-            spans=doc_spans,
-        )
+            in_specs=[pl.BlockSpec(memory_space=pl.ANY)] * 4,
+            scratch_shapes=[
+                pltpu.SMEM(doc_spans.shape, jnp.int32),
+                pltpu.VMEM(k2.shape, BF16),
+                pltpu.VMEM(v2.shape, BF16),
+                pltpu.VMEM(k_map.shape, BF16),
+                pltpu.SemaphoreType.DMA((4,)),
+            ],
+            compiler_params=pltpu.CompilerParams(vmem_limit_bytes=LIMIT),
+            cost_estimate=cost(3 * PER_MICRO, 0),
+        )(doc_spans, k2, v2, k_map)
         feat_k, blocks, tails = out[0], out[1], out[2:]
 
         def shift(own, hop, reverse):
-            step = n_seq - hop if reverse else hop
-            return lax.ppermute(own, "seq", [(i, (i + step) % n_seq) for i in range(n_seq)])
+            step = -hop if reverse else hop
+            ring = [(i, (i + step) % n_seq) for i in range(n_seq)]
+            return lax.ppermute(own, "seq", ring)
 
         def join(own, got, hop, reverse):
             return local_call(
@@ -496,10 +463,11 @@
         back_one = shift(first[2], 1, True)
         core_one = total.send(first[1], total.core, 1)
         second = late(parts[1], ready[1], came[1])
-        joined = join(first[2], back_one, 1, True)
-        joined, core_one, *second = lax.optimization_barrier((joined, core_one, *second))
+        core_one, back_one, *second = lax.optimization_barrier((core_one, back_one, *second))
         back_two = [shift(second[2], 1, True)]
         core_two = total.send(second[1], total.core, 1)
+        joined = join(first[2], back_one, 1, True)
+        joined, core_two = lax.optimization_barrier((joined, core_two))
         back_one = [back_one] + exchange(joined, True, 1)
         groups, layout = total.scatter([[first[0], core_one], [second[0], core_two]], total.stages[0])
         layouts = [layout]
@@ -511,20 +479,26 @@
             layouts.append(layout)
         x = total.split(groups, [])[0][0]
         x, back_two = lax.optimization_barrier((x, back_two))
+        for stage, layout in reversed(list(zip(total.stages[1:], layouts[1:]))):
+            x = total.gather(x, stage, layout)
         gk = [
             last(p, m[3], m[4], b)
             for p, m, b in zip(parts, (first, second), (back_one, back_two))
         ]
         out, core_layout = total.split([[g] for g in gk], total.core)
-        extra = total.split([[out[0], total.send(out[1], total.core, 1)]], [])[0][0]
+        extra = [[out[0], total.send(out[1], total.core, 1)]]
+        extra, layout = total.scatter(extra, total.stages[0], 2 * WHOLE)
+        extra_layouts = [layout]
         x, extra = lax.optimization_barrier((x, extra))
-        extra_layouts = []
-        for k in reversed(range(len(total.stages))):
-            x, extra, layout = total.gather_with(x, total.stages[k], layouts[k], extra, k == 0)
-            extra_layouts.append((total.stages[k], layout))
+        x = total.gather(x, total.stages[0], layouts[0])
+        for stage in total.stages[1:]:
+            extra, layout = total.scatter(extra, stage, 2 * WHOLE)
+            extra_layouts.append(layout)
+        extra = total.split(extra, [])[0][0]
+        for stage, layout in reversed(list(zip(total.stages, extra_layouts))):
+            extra = total.gather(extra, stage, layout)
+        x, extra = lax.optimization_barrier((x, extra))
         halves = [x, total.send(x, total.core, 1)]
-        for stage, layout in reversed(extra_layouts):
-            extra = total.gather(extra, stage, layout)
         grad_q = local_call(
             functools.partial(assemble_kernel, hk, group * hd // 2),
             rows_of(hq * hd, hd),

time: 126 us -> 118 us (0.937)
  waiting for transfers between devices: 54 us -> 38.5 us
  starting transfers between devices: 41.2 us -> 48 us
    ppermute x20 -> x23, waiting for transfers between devices: 32.6 us -> 24 us  [send(): return lax.ppermute(x, ('dp', 'seq'), perm)]
    ppermute x20 -> x23, starting transfers between devices: 23.4 us -> 30.4 us  [send(): return lax.ppermute(x, ('dp', 'seq'), perm)]
    ppermute x8, waiting for transfers between devices: 21.4 us -> 14.5 us  [shift(): return lax.ppermute(own, 'seq', ring)]
    pallas_call x0 -> x1, Pallas kernels: none -> 2.23 us  [shards(): pl.pallas_call(functools.partial(key_kernel, count, parts), out_shape=[ar...]
    pallas_call x23 -> x21, Pallas kernels: 26.5 us -> 24.3 us  [local_call(): pl.pallas_call(body, out_shape=out_shape, in_specs=[SMEM] * len(first) +...]
  transfers between devices with their start and end apart: 28 -> 31, of which waited for: 19 -> 16; matrix products, arithmetic and copies ran while one was open for 0% -> 0% of each run, Pallas kernels for 17% -> 18%
where the time goes in v3:
time: 118 us; the launch traced here: 117 us
  starting transfers between devices  48 us (41%)
  waiting for transfers between devices  38.5 us (33%)
  Pallas kernels  26.5 us (22%)
  local copies, waits for them, and re-layouts  3.48 us (3%)
    ppermute x23, starting transfers between devices, send(): return lax.ppermute(x, ('dp', 'seq'), perm)  30.4 us
    pallas_call x21, Pallas kernels, local_call(): pl.pallas_call(body, out_shape=out_shape, in_specs=[SMEM] * len(first) +...  24.3 us
    ppermute x23, waiting for transfers between devices, send(): return lax.ppermute(x, ('dp', 'seq'), perm)  24 us
    ppermute x8, starting transfers between devices, shift(): return lax.ppermute(own, 'seq', ring)  17.6 us
    ppermute x8, waiting for transfers between devices, shift(): return lax.ppermute(own, 'seq', ring)  14.5 us
    unnamed x22, local copies, waits for them, and re-layouts  3.48 us
  transfers between devices with their start and end apart: 31, of which 16 were waited for; matrix products, arithmetic and copies ran while one was open for 0% of the time, Pallas kernels for 18%

profile of v3, /device:TPU:0, one launch (start us, length us, event | category | flops | bytes accessed | tf_op | source)
XLA Modules:
  0.0 117.4 jit_solution(16359679705663062382)
XLA Ops:
  4.1 2.2 %shard_map.86 = (bf16[4,256,256]{2,1,0:T(8,128)(2,1)S(1)}, f32[4,2,136,256]{3,2,1,0:T(8,128)S(1)}, f32[272,256]{1,0:T(8,128)S(1)}, f32[272,256]{1,0:T(8,128)S(1)}) custom-call(s32[1,8]{1,0:T(1,128)S(1)} %copy-done.9, bf16[256,512]{1,0:T(8,128)(2,1)S(1)} %bitcast.19, bf16[256,512]{1,0:T(8,128)(2,1)S(1)} %bitcast.12, bf16[4,128,128]{2,1,0:T(8,128)(2,1)S(1)} %copy-done.7), custom_call_target="tpu_custom_call" | custom-call | flops 3000000000 | tf_op jit(solution)/shard_map/pallas_call | solution.py:374
  6.3 3.0 %collective-permute-start = (f32[272,256]{1,0:T(8,128)S(1)}, f32[272,256]{1,0:T(8,128)S(1)}, u32[]{:S(2)}, u32[]{:S(2)}) collective-permute-start(f32[272,256]{1,0:T(8,128)S(1)} %get-tuple-element.72.own_ref), channel_id=1, source_target_pairs={{0,1},{1,2},{2,3},{3,4},{4,5},{5,6},{6,7},{7,0},{8,9},{9,10},{10,1... | collective-permute-start | bytes 835592 | tf_op jit(solution)/shard_map/ppermute | solution.py:394
  10.9 2.9 %shard_map.90 = (f32[2,2,128,1024]{3,2,1,0:T(8,128)S(1)}, f32[2,2,128,1024]{3,2,1,0:T(8,128)S(1)}, bf16[2,2,256,1024]{3,2,1,0:T(8,128)(2,1)S(1)}, f32[2,2,128,10...) custom-call(bf16[256,4096]{1,0:T(8,128)(2,1)S(1)} %bitcast.8, ...), custom_call_target="tpu_custom_call" | custom-call | flops 3000000000 | tf_op jit(solution)/shard_map/pallas_call | solution.py:243
  13.8 6.1 %collective-permute-done.came_ref.refs_11_ = f32[272,256]{1,0:T(8,128)S(1)} collective-permute-done((f32[272,256]{1,0:T(8,128)S(1)}, f32[272,256]{1,0:T(8,128)S(1)}, u32[]{:S(2)}, u32[]{:S(2)}) %collective-permute-start) | collective-permute-done | bytes 278560 | tf_op jit(solution)/shard_map/ppermute | solution.py:394
  20.5 2.9 %shard_map.87 = (f32[2,2,128,1024]{3,2,1,0:T(8,128)S(1)}, f32[2,2,128,1024]{3,2,1,0:T(8,128)S(1)}, bf16[2,2,256,1024]{3,2,1,0:T(8,128)(2,1)S(1)}, f32[2,2,128,10...) custom-call(bf16[256,4096]{1,0:T(8,128)(2,1)S(1)} %bitcast.9, ...), custom_call_target="tpu_custom_call" | custom-call | flops 3000000000 | tf_op jit(solution)/shard_map/pallas_call | solution.py:243
  23.5 2.4 %collective-permute-done.4.came_ref.refs_11_ = f32[272,256]{1,0:T(8,128)S(1)} collective-permute-done((f32[272,256]{1,0:T(8,128)S(1)}, f32[272,256]{1,0:T(8,128)S(1)}, u32[]{:S(2)}, u32[]{:S(2)}) %collective-permute-start.4) | collective-permute-done | bytes 278560 | tf_op jit(solution)/shard_map/ppermute | solution.py:394
  26.5 2.8 %collective-permute-done.1.refs_12_ = f32[272,256]{1,0:T(8,128)S(1)} collective-permute-done((f32[272,256]{1,0:T(8,128)S(1)}, f32[272,256]{1,0:T(8,128)S(1)}, u32[]{:S(2)}, u32[]{:S(2)}) %collective-permute-start.1) | collective-permute-done | bytes 278560 | tf_op jit(solution)/shard_map/ppermute | solution.py:394
  29.3 5.4 %shard_map.89 = (f32[1024,128]{1,0:T(8,128)S(1)}, f32[1024,128]{1,0:T(8,128)S(1)}, f32[272,256]{1,0:T(8,128)S(1)}, f32[2,2,136,256]{3,2,1,0:T(8,128)S(1)}, f32[2,2,128,256]{3,2,1,0:T(8,128)S(1)}) custom-call(s32[1,8]{1,0:T(1,128)S(1)} %copy-done.9, bf16[256,4096]{1,0:T(8,128)(2,1)S(1)} %bitcast.10, bf16[256,512]{1,0:T(8,128)(2,1)S(1)} %bitcast.15, ...), custom_call_target="tpu_custom_call" | custom-call | flops 6000000000 | tf_op jit(solution)/shard_map/pallas_call | solution.py:243
  34.8 4.7 %collective-permute-start.3 = (f32[272,256]{1,0:T(8,128)S(1)}, f32[272,256]{1,0:T(8,128)S(1)}, u32[]{:S(2)}, u32[]{:S(2)}) collective-permute-start(f32[272,256]{1,0:T(8,128)S(1)} %get-tuple-element.75.own_ref), channel_id=1, source_target_pairs={{0,7},{1,0},{2,1},{3,2},{4,3},{5,4},{6,5},{7,6},{8,15},{9,8},{10,9... | collective-permute-start | bytes 835592 | tf_op jit(solution)/shard_map/ppermute | solution.py:394
  39.5 5.2 %shard_map.92 = (f32[1024,128]{1,0:T(8,128)S(1)}, f32[1024,128]{1,0:T(8,128)S(1)}, f32[272,256]{1,0:T(8,128)S(1)}, f32[2,2,136,256]{3,2,1,0:T(8,128)S(1)}, f32[2,2,128,256]{3,2,1,0:T(8,128)S(1)}) custom-call(s32[1,8]{1,0:T(1,128)S(1)} %copy-done.9, bf16[256,4096]{1,0:T(8,128)(2,1)S(1)} %bitcast.11, bf16[256,512]{1,0:T(8,128)(2,1)S(1)} %bitcast.16, ...), custom_call_target="tpu_custom_call" | custom-call | flops 6000000000 | tf_op jit(solution)/shard_map/pallas_call | solution.py:243
  45.3 3.5 %collective-permute-start.10 = (f32[272,256]{1,0:T(8,128)S(1)}, f32[272,256]{1,0:T(8,128)S(1)}, u32[]{:S(2)}, u32[]{:S(2)}) collective-permute-start(f32[272,256]{1,0:T(8,128)S(1)} %get-tuple-element.97.own_ref), channel_id=1, source_target_pairs={{0,7},{1,0},{2,1},{3,2},{4,3},{5,4},{6,5},{7,6},{8,15},{9,8},{10,9... | collective-permute-start | bytes 835592 | tf_op jit(solution)/shard_map/ppermute | solution.py:394
  51.1 1.8 %collective-permute-start.8 = (f32[512,128]{1,0:T(8,128)S(1)}, f32[512,128]{1,0:T(8,128)S(1)}, u32[]{:S(2)}, u32[]{:S(2)}) collective-permute-start(f32[512,128]{1,0:T(8,128)S(1)} %get-tuple-element.95), channel_id=1, source_target_pairs={{0,1},{1,0},{2,3},{3,2},{4,5},{5,4},{6,7},{7,6},{8,9},{9,8},{10,11... | collective-permute-start | bytes 786440 | tf_op jit(solution)/shard_map/ppermute | solution.py:309
  53.1 3.2 %collective-permute-done.10.came_ref.refs_6_ = f32[272,256]{1,0:T(8,128)S(1)} collective-permute-done((f32[272,256]{1,0:T(8,128)S(1)}, f32[272,256]{1,0:T(8,128)S(1)}, u32[]{:S(2)}, u32[]{:S(2)}) %collective-permute-start.10) | collective-permute-done | bytes 278560 | tf_op jit(solution)/shard_map/ppermute | solution.py:394
  56.9 1.8 %collective-permute-done.7.refs_1_ = f32[512,128]{1,0:T(8,128)S(1)} collective-permute-done((f32[512,128]{1,0:T(8,128)S(1)}, f32[512,128]{1,0:T(8,128)S(1)}, u32[]{:S(2)}, u32[]{:S(2)}) %collective-permute-start.7) | collective-permute-done | bytes 262176 | tf_op jit(solution)/shard_map/ppermute | solution.py:309
  58.8 6.3 %collective-permute-done.8.refs_2_ = f32[512,128]{1,0:T(8,128)S(1)} collective-permute-done((f32[512,128]{1,0:T(8,128)S(1)}, f32[512,128]{1,0:T(8,128)S(1)}, u32[]{:S(2)}, u32[]{:S(2)}) %collective-permute-start.8) | collective-permute-done | bytes 262176 | tf_op jit(solution)/shard_map/ppermute | solution.py:309
  65.1 4.7 %collective-permute-start.15 = (f32[272,256]{1,0:T(8,128)S(1)}, f32[272,256]{1,0:T(8,128)S(1)}, u32[]{:S(2)}, u32[]{:S(2)}) collective-permute-start(f32[272,256]{1,0:T(8,128)S(1)} %shard_map.95), channel_id=1, source_target_pairs={{0,6},{1,7},{2,0},{3,1},{4,2},{5,3},{6,4},{7,5},{8,14},{9,15},{10,... | collective-permute-start | bytes 835592 | tf_op jit(solution)/shard_map/ppermute | solution.py:394
  70.6 3.8 %collective-permute-start.14 = (f32[128,128]{1,0:T(8,128)S(1)}, f32[128,128]{1,0:T(8,128)S(1)}, u32[]{:S(2)}, u32[]{:S(2)}) collective-permute-start(f32[128,128]{1,0:T(8,128)S(1)} %get-tuple-element.106), channel_id=1, source_target_pairs={{0,6},{1,7},{2,4},{3,5},{4,2},{5,3},{6,0},{7,1},{8,14},{9,15},{10,... | collective-permute-start | bytes 196616 | tf_op jit(solution)/shard_map/ppermute | solution.py:309
  75.8 2.5 %collective-permute-done.12.refs_1_ = f32[128,128]{1,0:T(8,128)S(1)} collective-permute-done((f32[128,128]{1,0:T(8,128)S(1)}, f32[128,128]{1,0:T(8,128)S(1)}, u32[]{:S(2)}, u32[]{:S(2)}) %collective-permute-start.12) | collective-permute-done | bytes 65568 | tf_op jit(solution)/shard_map/ppermute | solution.py:309
  82.5 3.7 %collective-permute-start.18 = (f32[128,128]{1,0:T(8,128)S(1)}, f32[128,128]{1,0:T(8,128)S(1)}, u32[]{:S(2)}, u32[]{:S(2)}) collective-permute-start(f32[128,128]{1,0:T(8,128)S(1)} %shard_map.97.refs_0_), channel_id=1, source_target_pairs={{0,6},{1,7},{2,4},{3,5},{4,2},{5,3},{6,0},{7,1},{8,14},{9,15},{10,... | collective-permute-start | bytes 196616 | tf_op jit(solution)/shard_map/ppermute | solution.py:309
  86.2 2.1 %collective-permute-start.22 = (f32[256,128]{1,0:T(8,128)S(1)}, f32[256,128]{1,0:T(8,128)S(1)}, u32[]{:S(2)}, u32[]{:S(2)}) collective-permute-start(f32[256,128]{1,0:T(8,128)S(1)} %shard_map.102.refs_0_), channel_id=1, source_target_pairs={{0,17},{1,16},{2,19},{3,18},{4,21},{5,20},{6,23},{7,22},{8,25},{9,... | collective-permute-start | bytes 393224 | tf_op jit(solution)/shard_map/ppermute | solution.py:309
  92.1 4.2 %collective-permute-done.17.refs_2_ = f32[128,128]{1,0:T(8,128)S(1)} collective-permute-done((f32[128,128]{1,0:T(8,128)S(1)}, f32[128,128]{1,0:T(8,128)S(1)}, u32[]{:S(2)}, u32[]{:S(2)}) %collective-permute-start.17) | collective-permute-done | bytes 65568 | tf_op jit(solution)/shard_map/ppermute | solution.py:309
  103.6 5.6 %collective-permute-start.26 = (f32[256,128]{1,0:T(8,128)S(1)}, f32[256,128]{1,0:T(8,128)S(1)}, u32[]{:S(2)}, u32[]{:S(2)}) collective-permute-start(f32[256,128]{1,0:T(8,128)S(1)} %shard_map.104.refs_0_), channel_id=1, source_target_pairs={{0,2},{1,3},{2,0},{3,1},{4,6},{5,7},{6,4},{7,5},{8,10},{9,11},{10,... | collective-permute-start | bytes 393224 | tf_op jit(solution)/shard_map/ppermute | solution.py:309
  110.3 1.8 %collective-permute-done.26.refs_1_ = f32[256,128]{1,0:T(8,128)S(1)} collective-permute-done((f32[256,128]{1,0:T(8,128)S(1)}, f32[256,128]{1,0:T(8,128)S(1)}, u32[]{:S(2)}, u32[]{:S(2)}) %collective-permute-start.26) | collective-permute-done | bytes 131104 | tf_op jit(solution)/shard_map/ppermute | solution.py:309
  112.9 2.3 %collective-permute-done.30.refs_1_ = f32[256,128]{1,0:T(8,128)S(1)} collective-permute-done((f32[256,128]{1,0:T(8,128)S(1)}, f32[256,128]{1,0:T(8,128)S(1)}, u32[]{:S(2)}, u32[]{:S(2)}) %collective-permute-start.30) | collective-permute-done | bytes 131104 | tf_op jit(solution)/shard_map/ppermute | solution.py:309
  (82 shorter events, 31.3 us)
Async XLA Ops:
  6.3 13.5 %collective-permute-start = (f32[272,256]{1,0:T(8,128)S(1)}, f32[272,256]{1,0:T(8,128)S(1)}, u32[]{:S(2)}, u32[]{:S(2)}) collective-permute-start(f32[272,256]{1,0:T(8,128)S(1)} %get-tuple-element.72.own_ref), channel_id=1, source_target_pairs={{0,1},{1,2},{2,3},{3,4},{4,5},{5,6},{6,7},{7,0},{8,9},{9,10},{10,1... | collective-permute-start | bytes 835592 | tf_op jit(solution)/shard_map/ppermute | solution.py:394
  9.4 16.5 %collective-permute-start.4 = (f32[272,256]{1,0:T(8,128)S(1)}, f32[272,256]{1,0:T(8,128)S(1)}, u32[]{:S(2)}, u32[]{:S(2)}) collective-permute-start(f32[272,256]{1,0:T(8,128)S(1)} %get-tuple-element.82.own_ref), channel_id=1, source_target_pairs={{0,1},{1,2},{2,3},{3,4},{4,5},{5,6},{6,7},{7,0},{8,9},{9,10},{10,1... | collective-permute-start | bytes 835592 | tf_op jit(solution)/shard_map/ppermute | solution.py:394
  20.5 8.9 %collective-permute-start.1 = (f32[272,256]{1,0:T(8,128)S(1)}, f32[272,256]{1,0:T(8,128)S(1)}, u32[]{:S(2)}, u32[]{:S(2)}) collective-permute-start(f32[272,256]{1,0:T(8,128)S(1)} %shard_map.88), channel_id=1, source_target_pairs={{0,2},{1,3},{2,4},{3,5},{4,6},{5,7},{6,0},{7,1},{8,10},{9,11},{10,... | collective-permute-start | bytes 835592 | tf_op jit(solution)/shard_map/ppermute | solution.py:394
  26.4 13.1 %collective-permute-start.5 = (f32[272,256]{1,0:T(8,128)S(1)}, f32[272,256]{1,0:T(8,128)S(1)}, u32[]{:S(2)}, u32[]{:S(2)}) collective-permute-start(f32[272,256]{1,0:T(8,128)S(1)} %shard_map.91), channel_id=1, source_target_pairs={{0,2},{1,3},{2,4},{3,5},{4,6},{5,7},{6,0},{7,1},{8,10},{9,11},{10,... | collective-permute-start | bytes 835592 | tf_op jit(solution)/shard_map/ppermute | solution.py:394
  34.8 9.9 %collective-permute-start.3 = (f32[272,256]{1,0:T(8,128)S(1)}, f32[272,256]{1,0:T(8,128)S(1)}, u32[]{:S(2)}, u32[]{:S(2)}) collective-permute-start(f32[272,256]{1,0:T(8,128)S(1)} %get-tuple-element.75.own_ref), channel_id=1, source_target_pairs={{0,7},{1,0},{2,1},{3,2},{4,3},{5,4},{6,5},{7,6},{8,15},{9,8},{10,9... | collective-permute-start | bytes 835592 | tf_op jit(solution)/shard_map/ppermute | solution.py:394
  45.3 11.1 %collective-permute-start.10 = (f32[272,256]{1,0:T(8,128)S(1)}, f32[272,256]{1,0:T(8,128)S(1)}, u32[]{:S(2)}, u32[]{:S(2)}) collective-permute-start(f32[272,256]{1,0:T(8,128)S(1)} %get-tuple-element.97.own_ref), channel_id=1, source_target_pairs={{0,7},{1,0},{2,1},{3,2},{4,3},{5,4},{6,5},{7,6},{8,15},{9,8},{10,9... | collective-permute-start | bytes 835592 | tf_op jit(solution)/shard_map/ppermute | solution.py:394
  49.4 15.8 %collective-permute-start.11 = (f32[272,256]{1,0:T(8,128)S(1)}, f32[272,256]{1,0:T(8,128)S(1)}, u32[]{:S(2)}, u32[]{:S(2)}) collective-permute-start(f32[272,256]{1,0:T(8,128)S(1)} %shard_map.93), channel_id=1, source_target_pairs={{0,6},{1,7},{2,0},{3,1},{4,2},{5,3},{6,4},{7,5},{8,14},{9,15},{10,... | collective-permute-start | bytes 835592 | tf_op jit(solution)/shard_map/ppermute | solution.py:394
  49.6 9.2 %collective-permute-start.7 = (f32[512,128]{1,0:T(8,128)S(1)}, f32[512,128]{1,0:T(8,128)S(1)}, u32[]{:S(2)}, u32[]{:S(2)}) collective-permute-start(f32[512,128]{1,0:T(8,128)S(1)} %get-tuple-element.94), channel_id=1, source_target_pairs={{0,16},{1,17},{2,18},{3,19},{4,20},{5,21},{6,22},{7,23},{8,24},{9,... | collective-permute-start | bytes 786440 | tf_op jit(solution)/shard_map/ppermute | solution.py:309
  51.1 14.0 %collective-permute-start.8 = (f32[512,128]{1,0:T(8,128)S(1)}, f32[512,128]{1,0:T(8,128)S(1)}, u32[]{:S(2)}, u32[]{:S(2)}) collective-permute-start(f32[512,128]{1,0:T(8,128)S(1)} %get-tuple-element.95), channel_id=1, source_target_pairs={{0,1},{1,0},{2,3},{3,2},{4,5},{5,4},{6,7},{7,6},{8,9},{9,8},{10,11... | collective-permute-start | bytes 786440 | tf_op jit(solution)/shard_map/ppermute | solution.py:309
  52.9 12.2 %collective-permute-start.9 = (f32[512,128]{1,0:T(8,128)S(1)}, f32[512,128]{1,0:T(8,128)S(1)}, u32[]{:S(2)}, u32[]{:S(2)}) collective-permute-start(f32[512,128]{1,0:T(8,128)S(1)} %get-tuple-element.96), channel_id=1, source_target_pairs={{0,17},{1,16},{2,19},{3,18},{4,21},{5,20},{6,23},{7,22},{8,25},{9,... | collective-permute-start | bytes 786440 | tf_op jit(solution)/shard_map/ppermute | solution.py:309
  65.1 15.8 %collective-permute-start.15 = (f32[272,256]{1,0:T(8,128)S(1)}, f32[272,256]{1,0:T(8,128)S(1)}, u32[]{:S(2)}, u32[]{:S(2)}) collective-permute-start(f32[272,256]{1,0:T(8,128)S(1)} %shard_map.95), channel_id=1, source_target_pairs={{0,6},{1,7},{2,0},{3,1},{4,2},{5,3},{6,4},{7,5},{8,14},{9,15},{10,... | collective-permute-start | bytes 835592 | tf_op jit(solution)/shard_map/ppermute | solution.py:394
  69.9 8.4 %collective-permute-start.12 = (f32[128,128]{1,0:T(8,128)S(1)}, f32[128,128]{1,0:T(8,128)S(1)}, u32[]{:S(2)}, u32[]{:S(2)}) collective-permute-start(f32[128,128]{1,0:T(8,128)S(1)} %get-tuple-element.104), channel_id=1, source_target_pairs={{0,2},{1,3},{2,0},{3,1},{4,6},{5,7},{6,4},{7,5},{8,10},{9,11},{10,... | collective-permute-start | bytes 196616 | tf_op jit(solution)/shard_map/ppermute | solution.py:309
  70.0 9.5 %collective-permute-start.13 = (f32[128,128]{1,0:T(8,128)S(1)}, f32[128,128]{1,0:T(8,128)S(1)}, u32[]{:S(2)}, u32[]{:S(2)}) collective-permute-start(f32[128,128]{1,0:T(8,128)S(1)} %get-tuple-element.105), channel_id=1, source_target_pairs={{0,4},{1,5},{2,6},{3,7},{4,0},{5,1},{6,2},{7,3},{8,12},{9,13},{10,... | collective-permute-start | bytes 196616 | tf_op jit(solution)/shard_map/ppermute | solution.py:309
  70.6 10.3 %collective-permute-start.14 = (f32[128,128]{1,0:T(8,128)S(1)}, f32[128,128]{1,0:T(8,128)S(1)}, u32[]{:S(2)}, u32[]{:S(2)}) collective-permute-start(f32[128,128]{1,0:T(8,128)S(1)} %get-tuple-element.106), channel_id=1, source_target_pairs={{0,6},{1,7},{2,4},{3,5},{4,2},{5,3},{6,0},{7,1},{8,14},{9,15},{10,... | collective-permute-start | bytes 196616 | tf_op jit(solution)/shard_map/ppermute | solution.py:309
  82.5 9.4 %collective-permute-start.18 = (f32[128,128]{1,0:T(8,128)S(1)}, f32[128,128]{1,0:T(8,128)S(1)}, u32[]{:S(2)}, u32[]{:S(2)}) collective-permute-start(f32[128,128]{1,0:T(8,128)S(1)} %shard_map.97.refs_0_), channel_id=1, source_target_pairs={{0,6},{1,7},{2,4},{3,5},{4,2},{5,3},{6,0},{7,1},{8,14},{9,15},{10,... | collective-permute-start | bytes 196616 | tf_op jit(solution)/shard_map/ppermute | solution.py:309
  86.2 10.2 %collective-permute-start.22 = (f32[256,128]{1,0:T(8,128)S(1)}, f32[256,128]{1,0:T(8,128)S(1)}, u32[]{:S(2)}, u32[]{:S(2)}) collective-permute-start(f32[256,128]{1,0:T(8,128)S(1)} %shard_map.102.refs_0_), channel_id=1, source_target_pairs={{0,17},{1,16},{2,19},{3,18},{4,21},{5,20},{6,23},{7,22},{8,25},{9,... | collective-permute-start | bytes 393224 | tf_op jit(solution)/shard_map/ppermute | solution.py:309
  88.3 8.1 %collective-permute-start.21 = (f32[256,128]{1,0:T(8,128)S(1)}, f32[256,128]{1,0:T(8,128)S(1)}, u32[]{:S(2)}, u32[]{:S(2)}) collective-permute-start(f32[256,128]{1,0:T(8,128)S(1)} %shard_map.102.refs_0_), channel_id=1, source_target_pairs={{0,1},{1,0},{2,3},{3,2},{4,5},{5,4},{6,7},{7,6},{8,9},{9,8},{10,11... | collective-permute-start | bytes 393224 | tf_op jit(solution)/shard_map/ppermute | solution.py:309
  88.9 7.8 %collective-permute-start.20 = (f32[256,128]{1,0:T(8,128)S(1)}, f32[256,128]{1,0:T(8,128)S(1)}, u32[]{:S(2)}, u32[]{:S(2)}) collective-permute-start(f32[256,128]{1,0:T(8,128)S(1)} %shard_map.102.refs_0_), channel_id=1, source_target_pairs={{0,16},{1,17},{2,18},{3,19},{4,20},{5,21},{6,22},{7,23},{8,24},{9,... | collective-permute-start | bytes 393224 | tf_op jit(solution)/shard_map/ppermute | solution.py:309
  96.7 6.9 %collective-permute-start.28 = (f32[256,128]{1,0:T(8,128)S(1)}, f32[256,128]{1,0:T(8,128)S(1)}, u32[]{:S(2)}, u32[]{:S(2)}) collective-permute-start(f32[256,128]{1,0:T(8,128)S(1)} %shard_map.104.refs_0_), channel_id=1, source_target_pairs={{0,6},{1,7},{2,4},{3,5},{4,2},{5,3},{6,0},{7,1},{8,14},{9,15},{10,... | collective-permute-start | bytes 393224 | tf_op jit(solution)/shard_map/ppermute | solution.py:309
  98.2 14.0 %collective-permute-start.25 = (f32[512,128]{1,0:T(8,128)S(1)}, f32[512,128]{1,0:T(8,128)S(1)}, u32[]{:S(2)}, u32[]{:S(2)}) collective-permute-start(f32[512,128]{1,0:T(8,128)S(1)} %shard_map.98.refs_0_), channel_id=1, source_target_pairs={{0,17},{1,16},{2,19},{3,18},{4,21},{5,20},{6,23},{7,22},{8,25},{9,... | collective-permute-start | bytes 786440 | tf_op jit(solution)/shard_map/ppermute | solution.py:309
  99.6 12.6 %collective-permute-start.24 = (f32[512,128]{1,0:T(8,128)S(1)}, f32[512,128]{1,0:T(8,128)S(1)}, u32[]{:S(2)}, u32[]{:S(2)}) collective-permute-start(f32[512,128]{1,0:T(8,128)S(1)} %shard_map.98.refs_0_), channel_id=1, source_target_pairs={{0,1},{1,0},{2,3},{3,2},{4,5},{5,4},{6,7},{7,6},{8,9},{9,8},{10,11... | collective-permute-start | bytes 786440 | tf_op jit(solution)/shard_map/ppermute | solution.py:309
  100.3 11.9 %collective-permute-start.23 = (f32[512,128]{1,0:T(8,128)S(1)}, f32[512,128]{1,0:T(8,128)S(1)}, u32[]{:S(2)}, u32[]{:S(2)}) collective-permute-start(f32[512,128]{1,0:T(8,128)S(1)} %shard_map.98.refs_0_), channel_id=1, source_target_pairs={{0,16},{1,17},{2,18},{3,19},{4,20},{5,21},{6,22},{7,23},{8,24},{9,... | collective-permute-start | bytes 786440 | tf_op jit(solution)/shard_map/ppermute | solution.py:309
  101.7 8.6 %collective-permute-start.27 = (f32[256,128]{1,0:T(8,128)S(1)}, f32[256,128]{1,0:T(8,128)S(1)}, u32[]{:S(2)}, u32[]{:S(2)}) collective-permute-start(f32[256,128]{1,0:T(8,128)S(1)} %shard_map.104.refs_0_), channel_id=1, source_target_pairs={{0,4},{1,5},{2,6},{3,7},{4,0},{5,1},{6,2},{7,3},{8,12},{9,13},{10,... | collective-permute-start | bytes 393224 | tf_op jit(solution)/shard_map/ppermute | solution.py:309
  103.6 8.6 %collective-permute-start.26 = (f32[256,128]{1,0:T(8,128)S(1)}, f32[256,128]{1,0:T(8,128)S(1)}, u32[]{:S(2)}, u32[]{:S(2)}) collective-permute-start(f32[256,128]{1,0:T(8,128)S(1)} %shard_map.104.refs_0_), channel_id=1, source_target_pairs={{0,2},{1,3},{2,0},{3,1},{4,6},{5,7},{6,4},{7,5},{8,10},{9,11},{10,... | collective-permute-start | bytes 393224 | tf_op jit(solution)/shard_map/ppermute | solution.py:309
  (18 other events, 117.4 us)

commit v4 on v3

--- a/solution.py
+++ b/solution.py
@@ -460,33 +460,35 @@
         came = [exchange(t, False) for t in tails]
         ready = [early(p) for p in parts]
         first = late(parts[0], ready[0], came[0])
-        back_one = shift(first[2], 1, True)
+        back_one = [shift(first[2], 1, True)]
         core_one = total.send(first[1], total.core, 1)
         second = late(parts[1], ready[1], came[1])
-        core_one, back_one, *second = lax.optimization_barrier((core_one, back_one, *second))
+        core_one, *second = lax.optimization_barrier((core_one, *second))
         back_two = [shift(second[2], 1, True)]
         core_two = total.send(second[1], total.core, 1)
-        joined = join(first[2], back_one, 1, True)
-        joined, core_two = lax.optimization_barrier((joined, core_two))
-        back_one = [back_one] + exchange(joined, True, 1)
         groups, layout = total.scatter([[first[0], core_one], [second[0], core_two]], total.stages[0])
         layouts = [layout]
-        joined = join(second[2], back_two[0], 1, True)
-        groups, joined, back_one = lax.optimization_barrier((groups, joined, back_one))
-        back_two += exchange(joined, True, 1)
+        ends = [
+            join(own[2], back[0], 1, True) if hops > 1 else back[0]
+            for own, back in ((first, back_one), (second, back_two))
+        ]
+        if hops > 1:
+            back_two += exchange(ends[1], True, 1)
+            back_one += exchange(ends[0], True, 1)
+        groups, ends = lax.optimization_barrier((groups, ends))
         for stage in total.stages[1:]:
             groups, layout = total.scatter(groups, stage)
             layouts.append(layout)
         x = total.split(groups, [])[0][0]
-        x, back_two = lax.optimization_barrier((x, back_two))
-        for stage, layout in reversed(list(zip(total.stages[1:], layouts[1:]))):
-            x = total.gather(x, stage, layout)
         gk = [
             last(p, m[3], m[4], b)
             for p, m, b in zip(parts, (first, second), (back_one, back_two))
         ]
         out, core_layout = total.split([[g] for g in gk], total.core)
         extra = [[out[0], total.send(out[1], total.core, 1)]]
+        x, extra = lax.optimization_barrier((x, extra))
+        for stage, layout in reversed(list(zip(total.stages[1:], layouts[1:]))):
+            x = total.gather(x, stage, layout)
         extra, layout = total.scatter(extra, total.stages[0], 2 * WHOLE)
         extra_layouts = [layout]
         x, extra = lax.optimization_barrier((x, extra))

time: 118 us -> 110 us (0.932)
  starting transfers between devices: 48 us -> 38.2 us
  waiting for transfers between devices: 38.5 us -> 40.4 us
    ppermute x8, starting transfers between devices: 17.6 us -> 10.5 us  [shift(): return lax.ppermute(own, 'seq', ring)]
    ppermute x8, waiting for transfers between devices: 14.5 us -> 20.9 us  [shift(): return lax.ppermute(own, 'seq', ring)]
    ppermute x23, waiting for transfers between devices: 24 us -> 19.4 us  [send(): return lax.ppermute(x, ('dp', 'seq'), perm)]
    ppermute x23, starting transfers between devices: 30.4 us -> 27.8 us  [send(): return lax.ppermute(x, ('dp', 'seq'), perm)]
    unnamed x22 -> x20, local copies, waits for them, and re-layouts: 3.48 us -> 3.48 us
  transfers between devices with their start and end apart: 31 -> 31, of which waited for: 16 -> 15; matrix products, arithmetic and copies ran while one was open for 0% -> 0% of each run, Pallas kernels for 18% -> 21%
where the time goes in v4:
time: 110 us; the launch traced here: 109 us
  waiting for transfers between devices  40.4 us (37%)
  starting transfers between devices  38.2 us (35%)
  Pallas kernels  26.5 us (24%)
  local copies, waits for them, and re-layouts  3.48 us (3%)
    ppermute x23, starting transfers between devices, send(): return lax.ppermute(x, ('dp', 'seq'), perm)  27.8 us
    pallas_call x21, Pallas kernels, local_call(): pl.pallas_call(body, out_shape=out_shape, in_specs=[SMEM] * len(first) +...  24.2 us
    ppermute x8, waiting for transfers between devices, shift(): return lax.ppermute(own, 'seq', ring)  20.9 us
    ppermute x23, waiting for transfers between devices, send(): return lax.ppermute(x, ('dp', 'seq'), perm)  19.4 us
    ppermute x8, starting transfers between devices, shift(): return lax.ppermute(own, 'seq', ring)  10.5 us
    unnamed x20, local copies, waits for them, and re-layouts  3.48 us
    pallas_call x1, Pallas kernels, shards(): pl.pallas_call(functools.partial(key_kernel, count, parts), out_shape=[ar...  2.23 us
  transfers between devices with their start and end apart: 31, of which 15 were waited for; matrix products, arithmetic and copies ran while one was open for 0% of the time, Pallas kernels for 21%

profile of v4, /device:TPU:0, one launch (start us, length us, event | category | flops | bytes accessed | tf_op | source)
XLA Modules:
  0.0 109.5 jit_solution(7450284191007459548)
XLA Ops:
  4.1 2.2 %shard_map.86 = (bf16[4,256,256]{2,1,0:T(8,128)(2,1)S(1)}, f32[4,2,136,256]{3,2,1,0:T(8,128)S(1)}, f32[272,256]{1,0:T(8,128)S(1)}, f32[272,256]{1,0:T(8,128)S(1)}) custom-call(s32[1,8]{1,0:T(1,128)S(1)} %copy-done.9, bf16[256,512]{1,0:T(8,128)(2,1)S(1)} %bitcast.19, bf16[256,512]{1,0:T(8,128)(2,1)S(1)} %bitcast.12, bf16[4,128,128]{2,1,0:T(8,128)(2,1)S(1)} %copy-done.7), custom_call_target="tpu_custom_call" | custom-call | flops 3000000000 | tf_op jit(solution)/shard_map/pallas_call | solution.py:374
  6.3 3.0 %collective-permute-start = (f32[272,256]{1,0:T(8,128)S(1)}, f32[272,256]{1,0:T(8,128)S(1)}, u32[]{:S(2)}, u32[]{:S(2)}) collective-permute-start(f32[272,256]{1,0:T(8,128)S(1)} %get-tuple-element.66.own_ref), channel_id=1, source_target_pairs={{0,1},{1,2},{2,3},{3,4},{4,5},{5,6},{6,7},{7,0},{8,9},{9,10},{10,1... | collective-permute-start | bytes 835592 | tf_op jit(solution)/shard_map/ppermute | solution.py:394
  10.9 2.9 %shard_map.90 = (f32[2,2,128,1024]{3,2,1,0:T(8,128)S(1)}, f32[2,2,128,1024]{3,2,1,0:T(8,128)S(1)}, bf16[2,2,256,1024]{3,2,1,0:T(8,128)(2,1)S(1)}, f32[2,2,128,10...) custom-call(bf16[256,4096]{1,0:T(8,128)(2,1)S(1)} %bitcast.8, ...), custom_call_target="tpu_custom_call" | custom-call | flops 3000000000 | tf_op jit(solution)/shard_map/pallas_call | solution.py:243
  13.8 6.1 %collective-permute-done.came_ref.refs_11_ = f32[272,256]{1,0:T(8,128)S(1)} collective-permute-done((f32[272,256]{1,0:T(8,128)S(1)}, f32[272,256]{1,0:T(8,128)S(1)}, u32[]{:S(2)}, u32[]{:S(2)}) %collective-permute-start) | collective-permute-done | bytes 278560 | tf_op jit(solution)/shard_map/ppermute | solution.py:394
  20.5 2.9 %shard_map.87 = (f32[2,2,128,1024]{3,2,1,0:T(8,128)S(1)}, f32[2,2,128,1024]{3,2,1,0:T(8,128)S(1)}, bf16[2,2,256,1024]{3,2,1,0:T(8,128)(2,1)S(1)}, f32[2,2,128,10...) custom-call(bf16[256,4096]{1,0:T(8,128)(2,1)S(1)} %bitcast.9, ...), custom_call_target="tpu_custom_call" | custom-call | flops 3000000000 | tf_op jit(solution)/shard_map/pallas_call | solution.py:243
  23.5 2.4 %collective-permute-done.3.came_ref.refs_11_ = f32[272,256]{1,0:T(8,128)S(1)} collective-permute-done((f32[272,256]{1,0:T(8,128)S(1)}, f32[272,256]{1,0:T(8,128)S(1)}, u32[]{:S(2)}, u32[]{:S(2)}) %collective-permute-start.3) | collective-permute-done | bytes 278560 | tf_op jit(solution)/shard_map/ppermute | solution.py:394
  26.5 2.8 %collective-permute-done.1.refs_12_ = f32[272,256]{1,0:T(8,128)S(1)} collective-permute-done((f32[272,256]{1,0:T(8,128)S(1)}, f32[272,256]{1,0:T(8,128)S(1)}, u32[]{:S(2)}, u32[]{:S(2)}) %collective-permute-start.1) | collective-permute-done | bytes 278560 | tf_op jit(solution)/shard_map/ppermute | solution.py:394
  29.3 5.4 %shard_map.89 = (f32[1024,128]{1,0:T(8,128)S(1)}, f32[1024,128]{1,0:T(8,128)S(1)}, f32[272,256]{1,0:T(8,128)S(1)}, f32[2,2,136,256]{3,2,1,0:T(8,128)S(1)}, f32[2,2,128,256]{3,2,1,0:T(8,128)S(1)}) custom-call(s32[1,8]{1,0:T(1,128)S(1)} %copy-done.9, bf16[256,4096]{1,0:T(8,128)(2,1)S(1)} %bitcast.10, bf16[256,512]{1,0:T(8,128)(2,1)S(1)} %bitcast.15, ...), custom_call_target="tpu_custom_call" | custom-call | flops 6000000000 | tf_op jit(solution)/shard_map/pallas_call | solution.py:243
  34.8 4.7 %collective-permute-start.9 = (f32[272,256]{1,0:T(8,128)S(1)}, f32[272,256]{1,0:T(8,128)S(1)}, u32[]{:S(2)}, u32[]{:S(2)}) collective-permute-start(f32[272,256]{1,0:T(8,128)S(1)} %get-tuple-element.88.own_ref), channel_id=1, source_target_pairs={{0,7},{1,0},{2,1},{3,2},{4,3},{5,4},{6,5},{7,6},{8,15},{9,8},{10,9... | collective-permute-start | bytes 835592 | tf_op jit(solution)/shard_map/ppermute | solution.py:394
  39.5 5.1 %shard_map.92 = (f32[1024,128]{1,0:T(8,128)S(1)}, f32[1024,128]{1,0:T(8,128)S(1)}, f32[272,256]{1,0:T(8,128)S(1)}, f32[2,2,136,256]{3,2,1,0:T(8,128)S(1)}, f32[2,2,128,256]{3,2,1,0:T(8,128)S(1)}) custom-call(s32[1,8]{1,0:T(1,128)S(1)} %copy-done.9, bf16[256,4096]{1,0:T(8,128)(2,1)S(1)} %bitcast.11, bf16[256,512]{1,0:T(8,128)(2,1)S(1)} %bitcast.16, ...), custom_call_target="tpu_custom_call" | custom-call | flops 6000000000 | tf_op jit(solution)/shard_map/pallas_call | solution.py:243
  46.4 7.4 %collective-permute-done.10.came_ref.refs_6_ = f32[272,256]{1,0:T(8,128)S(1)} collective-permute-done((f32[272,256]{1,0:T(8,128)S(1)}, f32[272,256]{1,0:T(8,128)S(1)}, u32[]{:S(2)}, u32[]{:S(2)}) %collective-permute-start.10) | collective-permute-done | bytes 278560 | tf_op jit(solution)/shard_map/ppermute | solution.py:394
  55.1 1.6 %collective-permute-start.6 = (f32[512,128]{1,0:T(8,128)S(1)}, f32[512,128]{1,0:T(8,128)S(1)}, u32[]{:S(2)}, u32[]{:S(2)}) collective-permute-start(f32[512,128]{1,0:T(8,128)S(1)} %get-tuple-element.85), channel_id=1, source_target_pairs={{0,16},{1,17},{2,18},{3,19},{4,20},{5,21},{6,22},{7,23},{8,24},{9,... | collective-permute-start | bytes 786440 | tf_op jit(solution)/shard_map/ppermute | solution.py:309
  56.6 3.7 %collective-permute-start.7 = (f32[512,128]{1,0:T(8,128)S(1)}, f32[512,128]{1,0:T(8,128)S(1)}, u32[]{:S(2)}, u32[]{:S(2)}) collective-permute-start(f32[512,128]{1,0:T(8,128)S(1)} %get-tuple-element.86), channel_id=1, source_target_pairs={{0,1},{1,0},{2,3},{3,2},{4,5},{5,4},{6,7},{7,6},{8,9},{9,8},{10,11... | collective-permute-start | bytes 786440 | tf_op jit(solution)/shard_map/ppermute | solution.py:309
  61.9 2.2 %collective-permute-done.15.refs_7_ = f32[272,256]{1,0:T(8,128)S(1)} collective-permute-done((f32[272,256]{1,0:T(8,128)S(1)}, f32[272,256]{1,0:T(8,128)S(1)}, u32[]{:S(2)}, u32[]{:S(2)}) %collective-permute-start.15) | collective-permute-done | bytes 278560 | tf_op jit(solution)/shard_map/ppermute | solution.py:394
  65.7 4.3 %collective-permute-done.7.refs_2_ = f32[512,128]{1,0:T(8,128)S(1)} collective-permute-done((f32[512,128]{1,0:T(8,128)S(1)}, f32[512,128]{1,0:T(8,128)S(1)}, u32[]{:S(2)}, u32[]{:S(2)}) %collective-permute-start.7) | collective-permute-done | bytes 262176 | tf_op jit(solution)/shard_map/ppermute | solution.py:309
  71.7 3.5 %collective-permute-start.13 = (f32[128,128]{1,0:T(8,128)S(1)}, f32[128,128]{1,0:T(8,128)S(1)}, u32[]{:S(2)}, u32[]{:S(2)}) collective-permute-start(f32[128,128]{1,0:T(8,128)S(1)} %get-tuple-element.97), channel_id=1, source_target_pairs={{0,6},{1,7},{2,4},{3,5},{4,2},{5,3},{6,0},{7,1},{8,14},{9,15},{10,... | collective-permute-start | bytes 196616 | tf_op jit(solution)/shard_map/ppermute | solution.py:309
  76.5 1.8 %collective-permute-done.13.refs_3_ = f32[128,128]{1,0:T(8,128)S(1)} collective-permute-done((f32[128,128]{1,0:T(8,128)S(1)}, f32[128,128]{1,0:T(8,128)S(1)}, u32[]{:S(2)}, u32[]{:S(2)}) %collective-permute-start.13) | collective-permute-done | bytes 65568 | tf_op jit(solution)/shard_map/ppermute | solution.py:309
  78.3 3.1 %collective-permute-start.19 = (f32[128,128]{1,0:T(8,128)S(1)}, f32[128,128]{1,0:T(8,128)S(1)}, u32[]{:S(2)}, u32[]{:S(2)}) collective-permute-start(f32[128,128]{1,0:T(8,128)S(1)} %shard_map.97.refs_0_), channel_id=1, source_target_pairs={{0,6},{1,7},{2,4},{3,5},{4,2},{5,3},{6,0},{7,1},{8,14},{9,15},{10,... | collective-permute-start | bytes 196616 | tf_op jit(solution)/shard_map/ppermute | solution.py:309
  81.4 2.0 %collective-permute-start.22 = (f32[256,128]{1,0:T(8,128)S(1)}, f32[256,128]{1,0:T(8,128)S(1)}, u32[]{:S(2)}, u32[]{:S(2)}) collective-permute-start(f32[256,128]{1,0:T(8,128)S(1)} %shard_map.102.refs_0_), channel_id=1, source_target_pairs={{0,17},{1,16},{2,19},{3,18},{4,21},{5,20},{6,23},{7,22},{8,25},{9,... | collective-permute-start | bytes 393224 | tf_op jit(solution)/shard_map/ppermute | solution.py:309
  86.3 3.8 %collective-permute-done.18.refs_2_ = f32[128,128]{1,0:T(8,128)S(1)} collective-permute-done((f32[128,128]{1,0:T(8,128)S(1)}, f32[128,128]{1,0:T(8,128)S(1)}, u32[]{:S(2)}, u32[]{:S(2)}) %collective-permute-start.18) | collective-permute-done | bytes 65568 | tf_op jit(solution)/shard_map/ppermute | solution.py:309
  90.2 3.7 %collective-permute-start.28 = (f32[256,128]{1,0:T(8,128)S(1)}, f32[256,128]{1,0:T(8,128)S(1)}, u32[]{:S(2)}, u32[]{:S(2)}) collective-permute-start(f32[256,128]{1,0:T(8,128)S(1)} %shard_map.104.refs_0_), channel_id=1, source_target_pairs={{0,6},{1,7},{2,4},{3,5},{4,2},{5,3},{6,0},{7,1},{8,14},{9,15},{10,... | collective-permute-start | bytes 393224 | tf_op jit(solution)/shard_map/ppermute | solution.py:309
  97.5 1.6 %collective-permute-start.26 = (f32[256,128]{1,0:T(8,128)S(1)}, f32[256,128]{1,0:T(8,128)S(1)}, u32[]{:S(2)}, u32[]{:S(2)}) collective-permute-start(f32[256,128]{1,0:T(8,128)S(1)} %shard_map.104.refs_0_), channel_id=1, source_target_pairs={{0,2},{1,3},{2,0},{3,1},{4,6},{5,7},{6,4},{7,5},{8,10},{9,11},{10,... | collective-permute-start | bytes 393224 | tf_op jit(solution)/shard_map/ppermute | solution.py:309
  99.1 4.6 %collective-permute-done.27.refs_2_ = f32[256,128]{1,0:T(8,128)S(1)} collective-permute-done((f32[256,128]{1,0:T(8,128)S(1)}, f32[256,128]{1,0:T(8,128)S(1)}, u32[]{:S(2)}, u32[]{:S(2)}) %collective-permute-start.27) | collective-permute-done | bytes 131104 | tf_op jit(solution)/shard_map/ppermute | solution.py:309
  105.0 2.3 %collective-permute-done.30.refs_1_ = f32[256,128]{1,0:T(8,128)S(1)} collective-permute-done((f32[256,128]{1,0:T(8,128)S(1)}, f32[256,128]{1,0:T(8,128)S(1)}, u32[]{:S(2)}, u32[]{:S(2)}) %collective-permute-start.30) | collective-permute-done | bytes 131104 | tf_op jit(solution)/shard_map/ppermute | solution.py:309
  (80 shorter events, 25.2 us)
Async XLA Ops:
  6.3 13.5 %collective-permute-start = (f32[272,256]{1,0:T(8,128)S(1)}, f32[272,256]{1,0:T(8,128)S(1)}, u32[]{:S(2)}, u32[]{:S(2)}) collective-permute-start(f32[272,256]{1,0:T(8,128)S(1)} %get-tuple-element.66.own_ref), channel_id=1, source_target_pairs={{0,1},{1,2},{2,3},{3,4},{4,5},{5,6},{6,7},{7,0},{8,9},{9,10},{10,1... | collective-permute-start | bytes 835592 | tf_op jit(solution)/shard_map/ppermute | solution.py:394
  9.4 16.5 %collective-permute-start.3 = (f32[272,256]{1,0:T(8,128)S(1)}, f32[272,256]{1,0:T(8,128)S(1)}, u32[]{:S(2)}, u32[]{:S(2)}) collective-permute-start(f32[272,256]{1,0:T(8,128)S(1)} %get-tuple-element.75.own_ref), channel_id=1, source_target_pairs={{0,1},{1,2},{2,3},{3,4},{4,5},{5,6},{6,7},{7,0},{8,9},{9,10},{10,1... | collective-permute-start | bytes 835592 | tf_op jit(solution)/shard_map/ppermute | solution.py:394
  20.5 8.9 %collective-permute-start.1 = (f32[272,256]{1,0:T(8,128)S(1)}, f32[272,256]{1,0:T(8,128)S(1)}, u32[]{:S(2)}, u32[]{:S(2)}) collective-permute-start(f32[272,256]{1,0:T(8,128)S(1)} %shard_map.88), channel_id=1, source_target_pairs={{0,2},{1,3},{2,4},{3,5},{4,6},{5,7},{6,0},{7,1},{8,10},{9,11},{10,... | collective-permute-start | bytes 835592 | tf_op jit(solution)/shard_map/ppermute | solution.py:394
  26.4 13.1 %collective-permute-start.4 = (f32[272,256]{1,0:T(8,128)S(1)}, f32[272,256]{1,0:T(8,128)S(1)}, u32[]{:S(2)}, u32[]{:S(2)}) collective-permute-start(f32[272,256]{1,0:T(8,128)S(1)} %shard_map.91), channel_id=1, source_target_pairs={{0,2},{1,3},{2,4},{3,5},{4,6},{5,7},{6,0},{7,1},{8,10},{9,11},{10,... | collective-permute-start | bytes 835592 | tf_op jit(solution)/shard_map/ppermute | solution.py:394
  34.8 10.5 %collective-permute-start.9 = (f32[272,256]{1,0:T(8,128)S(1)}, f32[272,256]{1,0:T(8,128)S(1)}, u32[]{:S(2)}, u32[]{:S(2)}) collective-permute-start(f32[272,256]{1,0:T(8,128)S(1)} %get-tuple-element.88.own_ref), channel_id=1, source_target_pairs={{0,7},{1,0},{2,1},{3,2},{4,3},{5,4},{6,5},{7,6},{8,15},{9,8},{10,9... | collective-permute-start | bytes 835592 | tf_op jit(solution)/shard_map/ppermute | solution.py:394
  44.7 10.3 %collective-permute-start.5 = (f32[1024,128]{1,0:T(8,128)S(1)}, f32[1024,128]{1,0:T(8,128)S(1)}, u32[]{:S(2)}, u32[]{:S(2)}) collective-permute-start(f32[1024,128]{1,0:T(8,128)S(1)} %get-tuple-element.83), channel_id=1, source_target_pairs={{0,8},{1,9},{2,10},{3,11},{4,12},{5,13},{6,14},{7,15},{8,0},{9,1},... | collective-permute-start | bytes 1572872 | tf_op jit(solution)/shard_map/ppermute | solution.py:309
  45.2 8.6 %collective-permute-start.10 = (f32[272,256]{1,0:T(8,128)S(1)}, f32[272,256]{1,0:T(8,128)S(1)}, u32[]{:S(2)}, u32[]{:S(2)}) collective-permute-start(f32[272,256]{1,0:T(8,128)S(1)} %get-tuple-element.89.own_ref), channel_id=1, source_target_pairs={{0,7},{1,0},{2,1},{3,2},{4,3},{5,4},{6,5},{7,6},{8,15},{9,8},{10,9... | collective-permute-start | bytes 835592 | tf_op jit(solution)/shard_map/ppermute | solution.py:394
  45.9 14.4 %collective-permute-start.14 = (f32[272,256]{1,0:T(8,128)S(1)}, f32[272,256]{1,0:T(8,128)S(1)}, u32[]{:S(2)}, u32[]{:S(2)}) collective-permute-start(f32[272,256]{1,0:T(8,128)S(1)} %shard_map.94), channel_id=1, source_target_pairs={{0,6},{1,7},{2,0},{3,1},{4,2},{5,3},{6,4},{7,5},{8,14},{9,15},{10,... | collective-permute-start | bytes 835592 | tf_op jit(solution)/shard_map/ppermute | solution.py:394
  54.5 9.6 %collective-permute-start.15 = (f32[272,256]{1,0:T(8,128)S(1)}, f32[272,256]{1,0:T(8,128)S(1)}, u32[]{:S(2)}, u32[]{:S(2)}) collective-permute-start(f32[272,256]{1,0:T(8,128)S(1)} %shard_map.95), channel_id=1, source_target_pairs={{0,6},{1,7},{2,0},{3,1},{4,2},{5,3},{6,4},{7,5},{8,14},{9,15},{10,... | collective-permute-start | bytes 835592 | tf_op jit(solution)/shard_map/ppermute | solution.py:394
  55.1 10.6 %collective-permute-start.6 = (f32[512,128]{1,0:T(8,128)S(1)}, f32[512,128]{1,0:T(8,128)S(1)}, u32[]{:S(2)}, u32[]{:S(2)}) collective-permute-start(f32[512,128]{1,0:T(8,128)S(1)} %get-tuple-element.85), channel_id=1, source_target_pairs={{0,16},{1,17},{2,18},{3,19},{4,20},{5,21},{6,22},{7,23},{8,24},{9,... | collective-permute-start | bytes 786440 | tf_op jit(solution)/shard_map/ppermute | solution.py:309
  56.6 13.3 %collective-permute-start.7 = (f32[512,128]{1,0:T(8,128)S(1)}, f32[512,128]{1,0:T(8,128)S(1)}, u32[]{:S(2)}, u32[]{:S(2)}) collective-permute-start(f32[512,128]{1,0:T(8,128)S(1)} %get-tuple-element.86), channel_id=1, source_target_pairs={{0,1},{1,0},{2,3},{3,2},{4,5},{5,4},{6,7},{7,6},{8,9},{9,8},{10,11... | collective-permute-start | bytes 786440 | tf_op jit(solution)/shard_map/ppermute | solution.py:309
  60.4 10.3 %collective-permute-start.8 = (f32[512,128]{1,0:T(8,128)S(1)}, f32[512,128]{1,0:T(8,128)S(1)}, u32[]{:S(2)}, u32[]{:S(2)}) collective-permute-start(f32[512,128]{1,0:T(8,128)S(1)} %get-tuple-element.87), channel_id=1, source_target_pairs={{0,17},{1,16},{2,19},{3,18},{4,21},{5,20},{6,23},{7,22},{8,25},{9,... | collective-permute-start | bytes 786440 | tf_op jit(solution)/shard_map/ppermute | solution.py:309
  65.6 12.7 %collective-permute-start.16 = (f32[256,128]{1,0:T(8,128)S(1)}, f32[256,128]{1,0:T(8,128)S(1)}, u32[]{:S(2)}, u32[]{:S(2)}) collective-permute-start(f32[256,128]{1,0:T(8,128)S(1)} %get-tuple-element.103), channel_id=1, source_target_pairs={{0,8},{1,9},{2,10},{3,11},{4,12},{5,13},{6,14},{7,15},{8,0},{9,1},... | collective-permute-start | bytes 393224 | tf_op jit(solution)/shard_map/ppermute | solution.py:309
  71.7 6.6 %collective-permute-start.13 = (f32[128,128]{1,0:T(8,128)S(1)}, f32[128,128]{1,0:T(8,128)S(1)}, u32[]{:S(2)}, u32[]{:S(2)}) collective-permute-start(f32[128,128]{1,0:T(8,128)S(1)} %get-tuple-element.97), channel_id=1, source_target_pairs={{0,6},{1,7},{2,4},{3,5},{4,2},{5,3},{6,0},{7,1},{8,14},{9,15},{10,... | collective-permute-start | bytes 196616 | tf_op jit(solution)/shard_map/ppermute | solution.py:309
  78.3 6.7 %collective-permute-start.19 = (f32[128,128]{1,0:T(8,128)S(1)}, f32[128,128]{1,0:T(8,128)S(1)}, u32[]{:S(2)}, u32[]{:S(2)}) collective-permute-start(f32[128,128]{1,0:T(8,128)S(1)} %shard_map.97.refs_0_), channel_id=1, source_target_pairs={{0,6},{1,7},{2,4},{3,5},{4,2},{5,3},{6,0},{7,1},{8,14},{9,15},{10,... | collective-permute-start | bytes 196616 | tf_op jit(solution)/shard_map/ppermute | solution.py:309
  81.4 8.8 %collective-permute-start.22 = (f32[256,128]{1,0:T(8,128)S(1)}, f32[256,128]{1,0:T(8,128)S(1)}, u32[]{:S(2)}, u32[]{:S(2)}) collective-permute-start(f32[256,128]{1,0:T(8,128)S(1)} %shard_map.102.refs_0_), channel_id=1, source_target_pairs={{0,17},{1,16},{2,19},{3,18},{4,21},{5,20},{6,23},{7,22},{8,25},{9,... | collective-permute-start | bytes 393224 | tf_op jit(solution)/shard_map/ppermute | solution.py:309
  83.4 6.8 %collective-permute-start.21 = (f32[256,128]{1,0:T(8,128)S(1)}, f32[256,128]{1,0:T(8,128)S(1)}, u32[]{:S(2)}, u32[]{:S(2)}) collective-permute-start(f32[256,128]{1,0:T(8,128)S(1)} %shard_map.102.refs_0_), channel_id=1, source_target_pairs={{0,1},{1,0},{2,3},{3,2},{4,5},{5,4},{6,7},{7,6},{8,9},{9,8},{10,11... | collective-permute-start | bytes 393224 | tf_op jit(solution)/shard_map/ppermute | solution.py:309
  84.4 5.8 %collective-permute-start.20 = (f32[256,128]{1,0:T(8,128)S(1)}, f32[256,128]{1,0:T(8,128)S(1)}, u32[]{:S(2)}, u32[]{:S(2)}) collective-permute-start(f32[256,128]{1,0:T(8,128)S(1)} %shard_map.102.refs_0_), channel_id=1, source_target_pairs={{0,16},{1,17},{2,18},{3,19},{4,20},{5,21},{6,22},{7,23},{8,24},{9,... | collective-permute-start | bytes 393224 | tf_op jit(solution)/shard_map/ppermute | solution.py:309
  90.2 7.2 %collective-permute-start.28 = (f32[256,128]{1,0:T(8,128)S(1)}, f32[256,128]{1,0:T(8,128)S(1)}, u32[]{:S(2)}, u32[]{:S(2)}) collective-permute-start(f32[256,128]{1,0:T(8,128)S(1)} %shard_map.104.refs_0_), channel_id=1, source_target_pairs={{0,6},{1,7},{2,4},{3,5},{4,2},{5,3},{6,0},{7,1},{8,14},{9,15},{10,... | collective-permute-start | bytes 393224 | tf_op jit(solution)/shard_map/ppermute | solution.py:309
  93.9 9.9 %collective-permute-start.25 = (f32[512,128]{1,0:T(8,128)S(1)}, f32[512,128]{1,0:T(8,128)S(1)}, u32[]{:S(2)}, u32[]{:S(2)}) collective-permute-start(f32[512,128]{1,0:T(8,128)S(1)} %shard_map.101.refs_0_), channel_id=1, source_target_pairs={{0,17},{1,16},{2,19},{3,18},{4,21},{5,20},{6,23},{7,22},{8,25},{9,... | collective-permute-start | bytes 786440 | tf_op jit(solution)/shard_map/ppermute | solution.py:309
  95.4 8.6 %collective-permute-start.24 = (f32[512,128]{1,0:T(8,128)S(1)}, f32[512,128]{1,0:T(8,128)S(1)}, u32[]{:S(2)}, u32[]{:S(2)}) collective-permute-start(f32[512,128]{1,0:T(8,128)S(1)} %shard_map.101.refs_0_), channel_id=1, source_target_pairs={{0,1},{1,0},{2,3},{3,2},{4,5},{5,4},{6,7},{7,6},{8,9},{9,8},{10,11... | collective-permute-start | bytes 786440 | tf_op jit(solution)/shard_map/ppermute | solution.py:309
  96.9 7.4 %collective-permute-start.23 = (f32[512,128]{1,0:T(8,128)S(1)}, f32[512,128]{1,0:T(8,128)S(1)}, u32[]{:S(2)}, u32[]{:S(2)}) collective-permute-start(f32[512,128]{1,0:T(8,128)S(1)} %shard_map.101.refs_0_), channel_id=1, source_target_pairs={{0,16},{1,17},{2,18},{3,19},{4,20},{5,21},{6,22},{7,23},{8,24},{9,... | collective-permute-start | bytes 786440 | tf_op jit(solution)/shard_map/ppermute | solution.py:309
  97.4 6.3 %collective-permute-start.27 = (f32[256,128]{1,0:T(8,128)S(1)}, f32[256,128]{1,0:T(8,128)S(1)}, u32[]{:S(2)}, u32[]{:S(2)}) collective-permute-start(f32[256,128]{1,0:T(8,128)S(1)} %shard_map.104.refs_0_), channel_id=1, source_target_pairs={{0,4},{1,5},{2,6},{3,7},{4,0},{5,1},{6,2},{7,3},{8,12},{9,13},{10,... | collective-permute-start | bytes 393224 | tf_op jit(solution)/shard_map/ppermute | solution.py:309
  97.5 6.4 %collective-permute-start.26 = (f32[256,128]{1,0:T(8,128)S(1)}, f32[256,128]{1,0:T(8,128)S(1)}, u32[]{:S(2)}, u32[]{:S(2)}) collective-permute-start(f32[256,128]{1,0:T(8,128)S(1)} %shard_map.104.refs_0_), channel_id=1, source_target_pairs={{0,2},{1,3},{2,0},{3,1},{4,6},{5,7},{6,4},{7,5},{8,10},{9,11},{10,... | collective-permute-start | bytes 393224 | tf_op jit(solution)/shard_map/ppermute | solution.py:309
  (17 other events, 93.0 us)

commit v5 on v4

--- a/solution.py
+++ b/solution.py
@@ -56,28 +56,24 @@
     return jnp.broadcast_to(row, (PAD, row.shape[1]))
 
 
-def key_kernel(count, parts, spans_hbm, k_hbm, v_hbm, w_hbm, feat_ref, block_ref, *rest):
-    tail_refs = rest[: len(parts)]
-    spans_ref, k_ref, v_ref, w_ref, sems = rest[len(parts) :]
-    pairs = [(spans_hbm, spans_ref), (k_hbm, k_ref), (w_hbm, w_ref), (v_hbm, v_ref)]
-    copies = [pltpu.make_async_copy(a, b, sems.at[n]) for n, (a, b) in enumerate(pairs)]
-    for copy in copies:
-        copy.start()
-    for copy in copies:
-        copy.wait()
-    width = w_ref.shape[-1]
+def key_kernel(count, parts, width, spans_ref, packed_ref, feat_ref, block_ref, *tail_refs):
+    total = parts[-1][1] * width
+    stack = packed_ref.shape[0] // width
     first = lax.axis_index("seq") * count
     starts = [bounds(spans_ref, first + c)[0] for c in range(count)]
     for (lo, hi), tail_ref in zip(parts, tail_refs):
         for i in range(lo, hi):
             cols = slice(i * width, (i + 1) * width)
-            up, low = soft_pair(dot(k_ref[:, cols], w_ref[i], NN), -1)
+            at = 2 * total + i // stack * width
+            weight = packed_ref[i % stack * width : (i % stack + 1) * width, at : at + width]
+            up, low = soft_pair(dot(packed_ref[:, cols], weight, NN), -1)
             feat = jnp.concatenate([up, low], axis=-1).astype(BF16)
             feat_ref[i] = feat
             tail = None
             for c in range(count):
                 rows = slice(c * SPAN, (c + 1) * SPAN)
-                state = dot(v_ref[rows, cols], feat[rows], TN)
+                vals = packed_ref[rows, total + i * width : total + (i + 1) * width]
+                state = dot(vals, feat[rows], TN)
                 norm = jnp.sum(feat[rows].astype(F32), axis=0, keepdims=True)
                 both = jnp.concatenate([state, tall_rows(norm)], axis=0)
                 block_ref[i, c] = both
@@ -344,7 +340,8 @@
         return x if layout is None else self.join(x, stage, layout)
 
 
-def assemble_kernel(heads, half, own_ref, came_ref, out_ref):
+def assemble_kernel(heads, half, stage, layout, own_ref, came_ref, key_own, key_came, out_ref, key_ref):
+    join_pieces_kernel(stage, layout, key_own, key_came, key_ref)
     mine = lax.axis_index("dp") & 1
     for side, ref in enumerate((own_ref, came_ref)):
         for i in range(heads):
@@ -371,21 +368,17 @@
         k2, v2 = keys[0], values[0]
         parts = [(0, hk // 2), (hk // 2, hk)]
         array = jax.ShapeDtypeStruct
-        out = pl.pallas_call(
-            functools.partial(key_kernel, count, parts),
-            out_shape=[array((hk, rows, feats), BF16), array((hk, count, tall, feats), F32)]
+        stack = rows // hd
+        weights = jnp.pad(k_map, ((0, -hk % stack), (0, 0), (0, 0)))
+        weights = [weights[i : i + stack].reshape(rows, hd) for i in range(0, hk, stack)]
+        out = local_call(
+            functools.partial(key_kernel, count, parts, hd),
+            [array((hk, rows, feats), BF16), array((hk, count, tall, feats), F32)]
             + [rows_of((hi - lo) * tall, feats) for lo, hi in parts],
-            in_specs=[pl.BlockSpec(memory_space=pl.ANY)] * 4,
-            scratch_shapes=[
-                pltpu.SMEM(doc_spans.shape, jnp.int32),
-                pltpu.VMEM(k2.shape, BF16),
-                pltpu.VMEM(v2.shape, BF16),
-                pltpu.VMEM(k_map.shape, BF16),
-                pltpu.SemaphoreType.DMA((4,)),
-            ],
-            compiler_params=pltpu.CompilerParams(vmem_limit_bytes=LIMIT),
-            cost_estimate=cost(3 * PER_MICRO, 0),
-        )(doc_spans, k2, v2, k_map)
+            3.0,
+            jnp.concatenate([k2, v2] + weights, axis=1),
+            spans=doc_spans,
+        )
         feat_k, blocks, tails = out[0], out[1], out[2:]
 
         def shift(own, hop, reverse):
@@ -417,7 +410,7 @@
                 functools.partial(early_kernel, part, count, group),
                 [wide(hd, F32), wide(hd, F32), wide(feats, BF16), wide(hd, F32), wide(PAD, F32)]
                 + [wide(hd, BF16)],
-                3.0,
+                1.5,
                 q2,
                 t2,
                 v2,
@@ -432,7 +425,7 @@
                 [rows_of(heads * group * hd // 2, hd)] * 2
                 + [rows_of(heads * tall, feats)]
                 + [array((heads, count, tall, feats), F32), array((heads, count, SPAN, feats), F32)],
-                6.0,
+                6,
                 q2,
                 v2,
                 feat_k,
@@ -446,7 +439,7 @@
             return local_call(
                 functools.partial(last_kernel, part, count, hops),
                 rows_of((part[1] - part[0]) * hd, hd),
-                1.5,
+                0.5,
                 k2,
                 v2,
                 k_map,
@@ -486,13 +479,11 @@
         ]
         out, core_layout = total.split([[g] for g in gk], total.core)
         extra = [[out[0], total.send(out[1], total.core, 1)]]
-        x, extra = lax.optimization_barrier((x, extra))
-        for stage, layout in reversed(list(zip(total.stages[1:], layouts[1:]))):
-            x = total.gather(x, stage, layout)
         extra, layout = total.scatter(extra, total.stages[0], 2 * WHOLE)
         extra_layouts = [layout]
         x, extra = lax.optimization_barrier((x, extra))
-        x = total.gather(x, total.stages[0], layouts[0])
+        for stage, layout in reversed(list(zip(total.stages, layouts))):
+            x = total.gather(x, stage, layout)
         for stage in total.stages[1:]:
             extra, layout = total.scatter(extra, stage, 2 * WHOLE)
             extra_layouts.append(layout)
@@ -500,14 +491,13 @@
         for stage, layout in reversed(list(zip(total.stages, extra_layouts))):
             extra = total.gather(extra, stage, layout)
         x, extra = lax.optimization_barrier((x, extra))
-        halves = [x, total.send(x, total.core, 1)]
-        grad_q = local_call(
-            functools.partial(assemble_kernel, hk, group * hd // 2),
-            rows_of(hq * hd, hd),
+        halves = [x, total.send(x, total.core, 1), extra, total.send(extra, total.core, 1)]
+        grad_q, grad_k = local_call(
+            functools.partial(assemble_kernel, hk, group * hd // 2, total.core, core_layout),
+            [rows_of(hq * hd, hd), rows_of(hk * hd, hd)],
             1.0,
             *halves,
         )
-        grad_k = total.join(extra, total.core, core_layout)
         return grad_q.reshape(hq, hd, hd), grad_k.reshape(hk, hd, hd)
 
     in_specs = (

time: 110 us -> 106 us (0.964)
  waiting for transfers between devices: 40.4 us -> 36.3 us
  starting transfers between devices: 38.2 us -> 40.6 us
  local copies, waits for them, and re-layouts: 3.48 us -> 1.56 us
    unnamed x20 -> x14, local copies, waits for them, and re-layouts: 3.48 us -> 0.68 us
    ppermute x23, waiting for transfers between devices: 19.4 us -> 16.9 us  [send(): return lax.ppermute(x, ('dp', 'seq'), perm)]
    pallas_call x1 -> x0, Pallas kernels: 2.23 us -> none  [shards(): pl.pallas_call(functools.partial(key_kernel, count, parts), out_shape=[ar...]
    ppermute x8, starting transfers between devices: 10.5 us -> 12 us  [shift(): return lax.ppermute(own, 'seq', ring)]
    ppermute x8, waiting for transfers between devices: 20.9 us -> 19.4 us  [shift(): return lax.ppermute(own, 'seq', ring)]
    pallas_call x21, Pallas kernels: 24.2 us -> 25.5 us  [local_call(): pl.pallas_call(body, out_shape=out_shape, in_specs=[SMEM] * len(first) +...]
  transfers between devices with their start and end apart: 31 -> 31, of which waited for: 15 -> 12; matrix products, arithmetic and copies ran while one was open for 0% -> 0% of each run, Pallas kernels for 21% -> 20%
where the time goes in v5:
time: 106 us
  starting transfers between devices  40.6 us (38%)
  waiting for transfers between devices  36.3 us (34%)
  Pallas kernels  25.5 us (24%)
  local copies, waits for them, and re-layouts  1.56 us (1%)
  other arithmetic  1.08 us (1%)
    ppermute x23, starting transfers between devices, send(): return lax.ppermute(x, ('dp', 'seq'), perm)  28.6 us
    pallas_call x21, Pallas kernels, local_call(): pl.pallas_call(body, out_shape=out_shape, in_specs=[SMEM] * len(first) +...  25.5 us
    ppermute x8, waiting for transfers between devices, shift(): return lax.ppermute(own, 'seq', ring)  19.4 us
    ppermute x23, waiting for transfers between devices, send(): return lax.ppermute(x, ('dp', 'seq'), perm)  16.9 us
    ppermute x8, starting transfers between devices, shift(): return lax.ppermute(own, 'seq', ring)  12 us
  transfers between devices with their start and end apart: 31, of which 12 were waited for; matrix products, arithmetic and copies ran while one was open for 0% of the time, Pallas kernels for 20%

profile of v5, /device:TPU:0, one launch (start us, length us, event | category | flops | bytes accessed | tf_op | source)
XLA Modules:
  0.0 106.0 jit_solution(10514109269521380996)
XLA Ops:
  3.3 2.2 %shard_map.86 = (bf16[4,256,256]{2,1,0:T(8,128)(2,1)S(1)}, f32[4,2,136,256]{3,2,1,0:T(8,128)S(1)}, f32[272,256]{1,0:T(8,128)S(1)}, f32[272,256]{1,0:T(8,128)S(1)}) custom-call(s32[1,8]{1,0:T(1,128)S(1)} %copy-done.6, bf16[256,1280]{1,0:T(8,128)(2,1)S(1)} %pad_maximum_fusion.packed_ref), custom_call_target="tpu_custom_call" | custom-call | flops 3000000000 | tf_op jit(solution)/shard_map/pallas_call | solution.py:239
  5.5 3.0 %collective-permute-start = (f32[272,256]{1,0:T(8,128)S(1)}, f32[272,256]{1,0:T(8,128)S(1)}, u32[]{:S(2)}, u32[]{:S(2)}) collective-permute-start(f32[272,256]{1,0:T(8,128)S(1)} %get-tuple-element.65.own_ref), channel_id=1, source_target_pairs={{0,1},{1,2},{2,3},{3,4},{4,5},{5,6},{6,7},{7,0},{8,9},{9,10},{10,1... | collective-permute-start | bytes 835592 | tf_op jit(solution)/shard_map/ppermute | solution.py:387
  10.0 9.0 %collective-permute-done.came_ref.refs_11_ = f32[272,256]{1,0:T(8,128)S(1)} collective-permute-done((f32[272,256]{1,0:T(8,128)S(1)}, f32[272,256]{1,0:T(8,128)S(1)}, u32[]{:S(2)}, u32[]{:S(2)}) %collective-permute-start) | collective-permute-done | bytes 278560 | tf_op jit(solution)/shard_map/ppermute | solution.py:387
  19.7 2.9 %shard_map.90 = (f32[2,2,128,1024]{3,2,1,0:T(8,128)S(1)}, f32[2,2,128,1024]{3,2,1,0:T(8,128)S(1)}, bf16[2,2,256,1024]{3,2,1,0:T(8,128)(2,1)S(1)}, f32[2,2,128,10...) custom-call(bf16[256,4096]{1,0:T(8,128)(2,1)S(1)} %bitcast.10, ...), custom_call_target="tpu_custom_call" | custom-call | flops 1500000000 | tf_op jit(solution)/shard_map/pallas_call | solution.py:239
  22.6 2.9 %shard_map.87 = (f32[2,2,128,1024]{3,2,1,0:T(8,128)S(1)}, f32[2,2,128,1024]{3,2,1,0:T(8,128)S(1)}, bf16[2,2,256,1024]{3,2,1,0:T(8,128)(2,1)S(1)}, f32[2,2,128,10...) custom-call(bf16[256,4096]{1,0:T(8,128)(2,1)S(1)} %bitcast.11, ...), custom_call_target="tpu_custom_call" | custom-call | flops 1500000000 | tf_op jit(solution)/shard_map/pallas_call | solution.py:239
  26.1 1.6 %collective-permute-start.4 = (f32[272,256]{1,0:T(8,128)S(1)}, f32[272,256]{1,0:T(8,128)S(1)}, u32[]{:S(2)}, u32[]{:S(2)}) collective-permute-start(f32[272,256]{1,0:T(8,128)S(1)} %shard_map.91), channel_id=1, source_target_pairs={{0,2},{1,3},{2,4},{3,5},{4,6},{5,7},{6,0},{7,1},{8,10},{9,11},{10,... | collective-permute-start | bytes 835592 | tf_op jit(solution)/shard_map/ppermute | solution.py:387
  28.5 5.2 %shard_map.89 = (f32[1024,128]{1,0:T(8,128)S(1)}, f32[1024,128]{1,0:T(8,128)S(1)}, f32[272,256]{1,0:T(8,128)S(1)}, f32[2,2,136,256]{3,2,1,0:T(8,128)S(1)}, f32[2,2,128,256]{3,2,1,0:T(8,128)S(1)}) custom-call(s32[1,8]{1,0:T(1,128)S(1)} %copy-done.6, bf16[256,4096]{1,0:T(8,128)(2,1)S(1)} %bitcast.12, bf16[256,512]{1,0:T(8,128)(2,1)S(1)} %bitcast.17, ...), custom_call_target="tpu_custom_call" | custom-call | flops 6000000000 | tf_op jit(solution)/shard_map/pallas_call | solution.py:239
  33.6 4.7 %collective-permute-start.9 = (f32[272,256]{1,0:T(8,128)S(1)}, f32[272,256]{1,0:T(8,128)S(1)}, u32[]{:S(2)}, u32[]{:S(2)}) collective-permute-start(f32[272,256]{1,0:T(8,128)S(1)} %get-tuple-element.87.own_ref), channel_id=1, source_target_pairs={{0,7},{1,0},{2,1},{3,2},{4,3},{5,4},{6,5},{7,6},{8,15},{9,8},{10,9... | collective-permute-start | bytes 835592 | tf_op jit(solution)/shard_map/ppermute | solution.py:387
  38.3 5.1 %shard_map.92 = (f32[1024,128]{1,0:T(8,128)S(1)}, f32[1024,128]{1,0:T(8,128)S(1)}, f32[272,256]{1,0:T(8,128)S(1)}, f32[2,2,136,256]{3,2,1,0:T(8,128)S(1)}, f32[2,2,128,256]{3,2,1,0:T(8,128)S(1)}) custom-call(s32[1,8]{1,0:T(1,128)S(1)} %copy-done.6, bf16[256,4096]{1,0:T(8,128)(2,1)S(1)} %bitcast.13, bf16[256,512]{1,0:T(8,128)(2,1)S(1)} %bitcast.18, ...), custom_call_target="tpu_custom_call" | custom-call | flops 6000000000 | tf_op jit(solution)/shard_map/pallas_call | solution.py:239
  45.3 7.4 %collective-permute-done.10.came_ref.refs_6_ = f32[272,256]{1,0:T(8,128)S(1)} collective-permute-done((f32[272,256]{1,0:T(8,128)S(1)}, f32[272,256]{1,0:T(8,128)S(1)}, u32[]{:S(2)}, u32[]{:S(2)}) %collective-permute-start.10) | collective-permute-done | bytes 278560 | tf_op jit(solution)/shard_map/ppermute | solution.py:387
  55.5 3.7 %collective-permute-start.7 = (f32[512,128]{1,0:T(8,128)S(1)}, f32[512,128]{1,0:T(8,128)S(1)}, u32[]{:S(2)}, u32[]{:S(2)}) collective-permute-start(f32[512,128]{1,0:T(8,128)S(1)} %get-tuple-element.85), channel_id=1, source_target_pairs={{0,1},{1,0},{2,3},{3,2},{4,5},{5,4},{6,7},{7,6},{8,9},{9,8},{10,11... | collective-permute-start | bytes 786440 | tf_op jit(solution)/shard_map/ppermute | solution.py:305
  60.7 2.2 %collective-permute-done.15.refs_7_ = f32[272,256]{1,0:T(8,128)S(1)} collective-permute-done((f32[272,256]{1,0:T(8,128)S(1)}, f32[272,256]{1,0:T(8,128)S(1)}, u32[]{:S(2)}, u32[]{:S(2)}) %collective-permute-start.15) | collective-permute-done | bytes 278560 | tf_op jit(solution)/shard_map/ppermute | solution.py:387
  64.5 4.3 %collective-permute-done.7.refs_2_ = f32[512,128]{1,0:T(8,128)S(1)} collective-permute-done((f32[512,128]{1,0:T(8,128)S(1)}, f32[512,128]{1,0:T(8,128)S(1)}, u32[]{:S(2)}, u32[]{:S(2)}) %collective-permute-start.7) | collective-permute-done | bytes 262176 | tf_op jit(solution)/shard_map/ppermute | solution.py:305
  69.7 1.8 %collective-permute-start.19 = (f32[256,128]{1,0:T(8,128)S(1)}, f32[256,128]{1,0:T(8,128)S(1)}, u32[]{:S(2)}, u32[]{:S(2)}) collective-permute-start(f32[256,128]{1,0:T(8,128)S(1)} %shard_map.101.refs_0_), channel_id=1, source_target_pairs={{0,17},{1,16},{2,19},{3,18},{4,21},{5,20},{6,23},{7,22},{8,25},{9,... | collective-permute-start | bytes 393224 | tf_op jit(solution)/shard_map/ppermute | solution.py:305
  74.1 3.5 %collective-permute-start.13 = (f32[128,128]{1,0:T(8,128)S(1)}, f32[128,128]{1,0:T(8,128)S(1)}, u32[]{:S(2)}, u32[]{:S(2)}) collective-permute-start(f32[128,128]{1,0:T(8,128)S(1)} %get-tuple-element.96), channel_id=1, source_target_pairs={{0,6},{1,7},{2,4},{3,5},{4,2},{5,3},{6,0},{7,1},{8,14},{9,15},{10,... | collective-permute-start | bytes 196616 | tf_op jit(solution)/shard_map/ppermute | solution.py:305
  78.4 2.2 %collective-permute-done.13.refs_3_ = f32[128,128]{1,0:T(8,128)S(1)} collective-permute-done((f32[128,128]{1,0:T(8,128)S(1)}, f32[128,128]{1,0:T(8,128)S(1)}, u32[]{:S(2)}, u32[]{:S(2)}) %collective-permute-start.13) | collective-permute-done | bytes 65568 | tf_op jit(solution)/shard_map/ppermute | solution.py:305
  80.7 3.1 %collective-permute-start.22 = (f32[128,128]{1,0:T(8,128)S(1)}, f32[128,128]{1,0:T(8,128)S(1)}, u32[]{:S(2)}, u32[]{:S(2)}) collective-permute-start(f32[128,128]{1,0:T(8,128)S(1)} %shard_map.97.refs_0_), channel_id=1, source_target_pairs={{0,6},{1,7},{2,4},{3,5},{4,2},{5,3},{6,0},{7,1},{8,14},{9,15},{10,... | collective-permute-start | bytes 196616 | tf_op jit(solution)/shard_map/ppermute | solution.py:305
  85.2 3.1 %collective-permute-start.28 = (f32[256,128]{1,0:T(8,128)S(1)}, f32[256,128]{1,0:T(8,128)S(1)}, u32[]{:S(2)}, u32[]{:S(2)}) collective-permute-start(f32[256,128]{1,0:T(8,128)S(1)} %shard_map.104.refs_0_), channel_id=1, source_target_pairs={{0,6},{1,7},{2,4},{3,5},{4,2},{5,3},{6,0},{7,1},{8,14},{9,15},{10,... | collective-permute-start | bytes 393224 | tf_op jit(solution)/shard_map/ppermute | solution.py:305
  89.2 1.8 %collective-permute-start.25 = (f32[512,128]{1,0:T(8,128)S(1)}, f32[512,128]{1,0:T(8,128)S(1)}, u32[]{:S(2)}, u32[]{:S(2)}) collective-permute-start(f32[512,128]{1,0:T(8,128)S(1)} %shard_map.102.refs_0_), channel_id=1, source_target_pairs={{0,17},{1,16},{2,19},{3,18},{4,21},{5,20},{6,23},{7,22},{8,25},{9,... | collective-permute-start | bytes 786440 | tf_op jit(solution)/shard_map/ppermute | solution.py:305
  91.0 1.7 %collective-permute-start.24 = (f32[512,128]{1,0:T(8,128)S(1)}, f32[512,128]{1,0:T(8,128)S(1)}, u32[]{:S(2)}, u32[]{:S(2)}) collective-permute-start(f32[512,128]{1,0:T(8,128)S(1)} %shard_map.102.refs_0_), channel_id=1, source_target_pairs={{0,1},{1,0},{2,3},{3,2},{4,5},{5,4},{6,7},{7,6},{8,9},{9,8},{10,11... | collective-permute-start | bytes 786440 | tf_op jit(solution)/shard_map/ppermute | solution.py:305
  92.7 2.5 %collective-permute-start.27 = (f32[256,128]{1,0:T(8,128)S(1)}, f32[256,128]{1,0:T(8,128)S(1)}, u32[]{:S(2)}, u32[]{:S(2)}) collective-permute-start(f32[256,128]{1,0:T(8,128)S(1)} %shard_map.104.refs_0_), channel_id=1, source_target_pairs={{0,4},{1,5},{2,6},{3,7},{4,0},{5,1},{6,2},{7,3},{8,12},{9,13},{10,... | collective-permute-start | bytes 393224 | tf_op jit(solution)/shard_map/ppermute | solution.py:305
  95.7 4.3 %collective-permute-done.27.refs_2_ = f32[256,128]{1,0:T(8,128)S(1)} collective-permute-done((f32[256,128]{1,0:T(8,128)S(1)}, f32[256,128]{1,0:T(8,128)S(1)}, u32[]{:S(2)}, u32[]{:S(2)}) %collective-permute-start.27) | collective-permute-done | bytes 131104 | tf_op jit(solution)/shard_map/ppermute | solution.py:305
  102.0 2.3 %collective-permute-done.30.key_came = f32[256,128]{1,0:T(8,128)S(1)} collective-permute-done((f32[256,128]{1,0:T(8,128)S(1)}, f32[256,128]{1,0:T(8,128)S(1)}, u32[]{:S(2)}, u32[]{:S(2)}) %collective-permute-start.30) | collective-permute-done | bytes 131104 | tf_op jit(solution)/shard_map/ppermute | solution.py:305
  104.4 1.6 %shard_map.106 = (f32[4096,128]{1,0:T(8,128)}, f32[512,128]{1,0:T(8,128)}) custom-call(f32[2048,128]{1,0:T(8,128)S(1)} %shard_map.103.own_ref, f32[2048,128]{1,0:T(8,128)S(1)} %collective-permute-done.29.came_ref, f32[256,128]{1,0:T(8,128)S(1)} %shard_map.105.key_own, f32[256,128]{1,0:T(8,128)S(1)} %collective-permute-done.30.key_came), custom_call_target="tpu_custom_call" | custom-call | flops 1000000000 | tf_op jit(solution)/shard_map/pallas_call | solution.py:239
  (75 shorter events, 22.8 us)
Async XLA Ops:
  5.5 13.5 %collective-permute-start = (f32[272,256]{1,0:T(8,128)S(1)}, f32[272,256]{1,0:T(8,128)S(1)}, u32[]{:S(2)}, u32[]{:S(2)}) collective-permute-start(f32[272,256]{1,0:T(8,128)S(1)} %get-tuple-element.65.own_ref), channel_id=1, source_target_pairs={{0,1},{1,2},{2,3},{3,4},{4,5},{5,6},{6,7},{7,0},{8,9},{9,10},{10,1... | collective-permute-start | bytes 835592 | tf_op jit(solution)/shard_map/ppermute | solution.py:387
  8.5 17.0 %collective-permute-start.3 = (f32[272,256]{1,0:T(8,128)S(1)}, f32[272,256]{1,0:T(8,128)S(1)}, u32[]{:S(2)}, u32[]{:S(2)}) collective-permute-start(f32[272,256]{1,0:T(8,128)S(1)} %get-tuple-element.74.own_ref), channel_id=1, source_target_pairs={{0,1},{1,2},{2,3},{3,4},{4,5},{5,6},{6,7},{7,0},{8,9},{9,10},{10,1... | collective-permute-start | bytes 835592 | tf_op jit(solution)/shard_map/ppermute | solution.py:387
  19.6 8.9 %collective-permute-start.1 = (f32[272,256]{1,0:T(8,128)S(1)}, f32[272,256]{1,0:T(8,128)S(1)}, u32[]{:S(2)}, u32[]{:S(2)}) collective-permute-start(f32[272,256]{1,0:T(8,128)S(1)} %shard_map.88), channel_id=1, source_target_pairs={{0,2},{1,3},{2,4},{3,5},{4,6},{5,7},{6,0},{7,1},{8,10},{9,11},{10,... | collective-permute-start | bytes 835592 | tf_op jit(solution)/shard_map/ppermute | solution.py:387
  26.1 12.2 %collective-permute-start.4 = (f32[272,256]{1,0:T(8,128)S(1)}, f32[272,256]{1,0:T(8,128)S(1)}, u32[]{:S(2)}, u32[]{:S(2)}) collective-permute-start(f32[272,256]{1,0:T(8,128)S(1)} %shard_map.91), channel_id=1, source_target_pairs={{0,2},{1,3},{2,4},{3,5},{4,6},{5,7},{6,0},{7,1},{8,10},{9,11},{10,... | collective-permute-start | bytes 835592 | tf_op jit(solution)/shard_map/ppermute | solution.py:387
  33.6 10.5 %collective-permute-start.9 = (f32[272,256]{1,0:T(8,128)S(1)}, f32[272,256]{1,0:T(8,128)S(1)}, u32[]{:S(2)}, u32[]{:S(2)}) collective-permute-start(f32[272,256]{1,0:T(8,128)S(1)} %get-tuple-element.87.own_ref), channel_id=1, source_target_pairs={{0,7},{1,0},{2,1},{3,2},{4,3},{5,4},{6,5},{7,6},{8,15},{9,8},{10,9... | collective-permute-start | bytes 835592 | tf_op jit(solution)/shard_map/ppermute | solution.py:387
  43.5 10.3 %collective-permute-start.5 = (f32[1024,128]{1,0:T(8,128)S(1)}, f32[1024,128]{1,0:T(8,128)S(1)}, u32[]{:S(2)}, u32[]{:S(2)}) collective-permute-start(f32[1024,128]{1,0:T(8,128)S(1)} %get-tuple-element.82), channel_id=1, source_target_pairs={{0,8},{1,9},{2,10},{3,11},{4,12},{5,13},{6,14},{7,15},{8,0},{9,1},... | collective-permute-start | bytes 1572872 | tf_op jit(solution)/shard_map/ppermute | solution.py:305
  44.1 8.6 %collective-permute-start.10 = (f32[272,256]{1,0:T(8,128)S(1)}, f32[272,256]{1,0:T(8,128)S(1)}, u32[]{:S(2)}, u32[]{:S(2)}) collective-permute-start(f32[272,256]{1,0:T(8,128)S(1)} %get-tuple-element.88.own_ref), channel_id=1, source_target_pairs={{0,7},{1,0},{2,1},{3,2},{4,3},{5,4},{6,5},{7,6},{8,15},{9,8},{10,9... | collective-permute-start | bytes 835592 | tf_op jit(solution)/shard_map/ppermute | solution.py:387
  44.8 14.4 %collective-permute-start.14 = (f32[272,256]{1,0:T(8,128)S(1)}, f32[272,256]{1,0:T(8,128)S(1)}, u32[]{:S(2)}, u32[]{:S(2)}) collective-permute-start(f32[272,256]{1,0:T(8,128)S(1)} %shard_map.94), channel_id=1, source_target_pairs={{0,6},{1,7},{2,0},{3,1},{4,2},{5,3},{6,4},{7,5},{8,14},{9,15},{10,... | collective-permute-start | bytes 835592 | tf_op jit(solution)/shard_map/ppermute | solution.py:387
  53.3 9.6 %collective-permute-start.15 = (f32[272,256]{1,0:T(8,128)S(1)}, f32[272,256]{1,0:T(8,128)S(1)}, u32[]{:S(2)}, u32[]{:S(2)}) collective-permute-start(f32[272,256]{1,0:T(8,128)S(1)} %shard_map.95), channel_id=1, source_target_pairs={{0,6},{1,7},{2,0},{3,1},{4,2},{5,3},{6,4},{7,5},{8,14},{9,15},{10,... | collective-permute-start | bytes 835592 | tf_op jit(solution)/shard_map/ppermute | solution.py:387
  53.9 10.6 %collective-permute-start.6 = (f32[512,128]{1,0:T(8,128)S(1)}, f32[512,128]{1,0:T(8,128)S(1)}, u32[]{:S(2)}, u32[]{:S(2)}) collective-permute-start(f32[512,128]{1,0:T(8,128)S(1)} %get-tuple-element.84), channel_id=1, source_target_pairs={{0,16},{1,17},{2,18},{3,19},{4,20},{5,21},{6,22},{7,23},{8,24},{9,... | collective-permute-start | bytes 786440 | tf_op jit(solution)/shard_map/ppermute | solution.py:305
  55.5 13.3 %collective-permute-start.7 = (f32[512,128]{1,0:T(8,128)S(1)}, f32[512,128]{1,0:T(8,128)S(1)}, u32[]{:S(2)}, u32[]{:S(2)}) collective-permute-start(f32[512,128]{1,0:T(8,128)S(1)} %get-tuple-element.85), channel_id=1, source_target_pairs={{0,1},{1,0},{2,3},{3,2},{4,5},{5,4},{6,7},{7,6},{8,9},{9,8},{10,11... | collective-permute-start | bytes 786440 | tf_op jit(solution)/shard_map/ppermute | solution.py:305
  59.2 10.3 %collective-permute-start.8 = (f32[512,128]{1,0:T(8,128)S(1)}, f32[512,128]{1,0:T(8,128)S(1)}, u32[]{:S(2)}, u32[]{:S(2)}) collective-permute-start(f32[512,128]{1,0:T(8,128)S(1)} %get-tuple-element.86), channel_id=1, source_target_pairs={{0,17},{1,16},{2,19},{3,18},{4,21},{5,20},{6,23},{7,22},{8,25},{9,... | collective-permute-start | bytes 786440 | tf_op jit(solution)/shard_map/ppermute | solution.py:305
  69.7 11.0 %collective-permute-start.19 = (f32[256,128]{1,0:T(8,128)S(1)}, f32[256,128]{1,0:T(8,128)S(1)}, u32[]{:S(2)}, u32[]{:S(2)}) collective-permute-start(f32[256,128]{1,0:T(8,128)S(1)} %shard_map.101.refs_0_), channel_id=1, source_target_pairs={{0,17},{1,16},{2,19},{3,18},{4,21},{5,20},{6,23},{7,22},{8,25},{9,... | collective-permute-start | bytes 393224 | tf_op jit(solution)/shard_map/ppermute | solution.py:305
  71.5 9.2 %collective-permute-start.18 = (f32[256,128]{1,0:T(8,128)S(1)}, f32[256,128]{1,0:T(8,128)S(1)}, u32[]{:S(2)}, u32[]{:S(2)}) collective-permute-start(f32[256,128]{1,0:T(8,128)S(1)} %shard_map.101.refs_0_), channel_id=1, source_target_pairs={{0,1},{1,0},{2,3},{3,2},{4,5},{5,4},{6,7},{7,6},{8,9},{9,8},{10,11... | collective-permute-start | bytes 393224 | tf_op jit(solution)/shard_map/ppermute | solution.py:305
  72.7 8.0 %collective-permute-start.17 = (f32[256,128]{1,0:T(8,128)S(1)}, f32[256,128]{1,0:T(8,128)S(1)}, u32[]{:S(2)}, u32[]{:S(2)}) collective-permute-start(f32[256,128]{1,0:T(8,128)S(1)} %shard_map.101.refs_0_), channel_id=1, source_target_pairs={{0,16},{1,17},{2,18},{3,19},{4,20},{5,21},{6,22},{7,23},{8,24},{9,... | collective-permute-start | bytes 393224 | tf_op jit(solution)/shard_map/ppermute | solution.py:305
  74.1 6.5 %collective-permute-start.13 = (f32[128,128]{1,0:T(8,128)S(1)}, f32[128,128]{1,0:T(8,128)S(1)}, u32[]{:S(2)}, u32[]{:S(2)}) collective-permute-start(f32[128,128]{1,0:T(8,128)S(1)} %get-tuple-element.96), channel_id=1, source_target_pairs={{0,6},{1,7},{2,4},{3,5},{4,2},{5,3},{6,0},{7,1},{8,14},{9,15},{10,... | collective-permute-start | bytes 196616 | tf_op jit(solution)/shard_map/ppermute | solution.py:305
  80.7 7.6 %collective-permute-start.22 = (f32[128,128]{1,0:T(8,128)S(1)}, f32[128,128]{1,0:T(8,128)S(1)}, u32[]{:S(2)}, u32[]{:S(2)}) collective-permute-start(f32[128,128]{1,0:T(8,128)S(1)} %shard_map.97.refs_0_), channel_id=1, source_target_pairs={{0,6},{1,7},{2,4},{3,5},{4,2},{5,3},{6,0},{7,1},{8,14},{9,15},{10,... | collective-permute-start | bytes 196616 | tf_op jit(solution)/shard_map/ppermute | solution.py:305
  83.8 5.3 %collective-permute-start.21 = (f32[128,128]{1,0:T(8,128)S(1)}, f32[128,128]{1,0:T(8,128)S(1)}, u32[]{:S(2)}, u32[]{:S(2)}) collective-permute-start(f32[128,128]{1,0:T(8,128)S(1)} %shard_map.97.refs_0_), channel_id=1, source_target_pairs={{0,4},{1,5},{2,6},{3,7},{4,0},{5,1},{6,2},{7,3},{8,12},{9,13},{10,... | collective-permute-start | bytes 196616 | tf_op jit(solution)/shard_map/ppermute | solution.py:305
  85.2 10.0 %collective-permute-start.28 = (f32[256,128]{1,0:T(8,128)S(1)}, f32[256,128]{1,0:T(8,128)S(1)}, u32[]{:S(2)}, u32[]{:S(2)}) collective-permute-start(f32[256,128]{1,0:T(8,128)S(1)} %shard_map.104.refs_0_), channel_id=1, source_target_pairs={{0,6},{1,7},{2,4},{3,5},{4,2},{5,3},{6,0},{7,1},{8,14},{9,15},{10,... | collective-permute-start | bytes 393224 | tf_op jit(solution)/shard_map/ppermute | solution.py:305
  89.2 12.2 %collective-permute-start.25 = (f32[512,128]{1,0:T(8,128)S(1)}, f32[512,128]{1,0:T(8,128)S(1)}, u32[]{:S(2)}, u32[]{:S(2)}) collective-permute-start(f32[512,128]{1,0:T(8,128)S(1)} %shard_map.102.refs_0_), channel_id=1, source_target_pairs={{0,17},{1,16},{2,19},{3,18},{4,21},{5,20},{6,23},{7,22},{8,25},{9,... | collective-permute-start | bytes 786440 | tf_op jit(solution)/shard_map/ppermute | solution.py:305
  91.0 10.4 %collective-permute-start.24 = (f32[512,128]{1,0:T(8,128)S(1)}, f32[512,128]{1,0:T(8,128)S(1)}, u32[]{:S(2)}, u32[]{:S(2)}) collective-permute-start(f32[512,128]{1,0:T(8,128)S(1)} %shard_map.102.refs_0_), channel_id=1, source_target_pairs={{0,1},{1,0},{2,3},{3,2},{4,5},{5,4},{6,7},{7,6},{8,9},{9,8},{10,11... | collective-permute-start | bytes 786440 | tf_op jit(solution)/shard_map/ppermute | solution.py:305
  92.7 8.6 %collective-permute-start.23 = (f32[512,128]{1,0:T(8,128)S(1)}, f32[512,128]{1,0:T(8,128)S(1)}, u32[]{:S(2)}, u32[]{:S(2)}) collective-permute-start(f32[512,128]{1,0:T(8,128)S(1)} %shard_map.102.refs_0_), channel_id=1, source_target_pairs={{0,16},{1,17},{2,18},{3,19},{4,20},{5,21},{6,22},{7,23},{8,24},{9,... | collective-permute-start | bytes 786440 | tf_op jit(solution)/shard_map/ppermute | solution.py:305
  92.7 7.3 %collective-permute-start.27 = (f32[256,128]{1,0:T(8,128)S(1)}, f32[256,128]{1,0:T(8,128)S(1)}, u32[]{:S(2)}, u32[]{:S(2)}) collective-permute-start(f32[256,128]{1,0:T(8,128)S(1)} %shard_map.104.refs_0_), channel_id=1, source_target_pairs={{0,4},{1,5},{2,6},{3,7},{4,0},{5,1},{6,2},{7,3},{8,12},{9,13},{10,... | collective-permute-start | bytes 393224 | tf_op jit(solution)/shard_map/ppermute | solution.py:305
  95.2 6.1 %collective-permute-start.26 = (f32[256,128]{1,0:T(8,128)S(1)}, f32[256,128]{1,0:T(8,128)S(1)}, u32[]{:S(2)}, u32[]{:S(2)}) collective-permute-start(f32[256,128]{1,0:T(8,128)S(1)} %shard_map.104.refs_0_), channel_id=1, source_target_pairs={{0,2},{1,3},{2,0},{3,1},{4,6},{5,7},{6,4},{7,5},{8,10},{9,11},{10,... | collective-permute-start | bytes 393224 | tf_op jit(solution)/shard_map/ppermute | solution.py:305
  (14 other events, 124.3 us)

commit v6 on v5

--- a/solution.py
+++ b/solution.py
@@ -150,7 +150,7 @@
                 state = some if state is None else state + some
             for e in range(c):
                 state = state + flag(start <= first + e) * block_ref[i, e]
-            state = state.astype(BF16)
+            state = jnp.concatenate([state, state[SPAN:]], axis=0).astype(BF16)
             feat_k = feat_k_ref[i, rows]
             feat = feat_ref[k, c]
             across = dot(state, feat, NN)
@@ -169,8 +169,10 @@
             rest = d_denom - high.astype(F32)
             mid = rest.astype(BF16)
             low = (rest - mid.astype(F32)).astype(BF16)
-            fill = jnp.zeros((2 * PAD - 3, high.shape[1]), BF16)
-            left = jnp.concatenate([d_numer, pairs, high, mid, low, fill], axis=0)
+            three = [high.astype(F32), mid.astype(F32), low.astype(F32)]
+            three.append(jnp.zeros((2 * PAD - 3, high.shape[1]), F32))
+            three = jnp.concatenate(three, axis=0).astype(BF16)
+            left = jnp.concatenate([d_numer, pairs, three], axis=0)
             crossed = dot(left, feat, NT)
             at = 2 * SPAN
             norm_row = crossed[at : at + 1] + crossed[at + 1 : at + 2] + crossed[at + 2 : at + 3]

time: 106 us -> 106 us (level)
  no operation moved by 1% of the time
where the time goes in v6:
time: 106 us
  starting transfers between devices  40.5 us (38%)
  waiting for transfers between devices  36.3 us (34%)
  Pallas kernels  25.4 us (24%)
  local copies, waits for them, and re-layouts  1.56 us (1%)
  other arithmetic  1.08 us (1%)
    ppermute x23, starting transfers between devices, send(): return lax.ppermute(x, ('dp', 'seq'), perm)  28.6 us
    pallas_call x21, Pallas kernels, local_call(): pl.pallas_call(body, out_shape=out_shape, in_specs=[SMEM] * len(first) +...  25.4 us
    ppermute x8, waiting for transfers between devices, shift(): return lax.ppermute(own, 'seq', ring)  19.4 us
    ppermute x23, waiting for transfers between devices, send(): return lax.ppermute(x, ('dp', 'seq'), perm)  16.9 us
    ppermute x8, starting transfers between devices, shift(): return lax.ppermute(own, 'seq', ring)  12 us
  transfers between devices with their start and end apart: 31, of which 12 were waited for; matrix products, arithmetic and copies ran while one was open for 0% of the time, Pallas kernels for 20%

profile of v6, /device:TPU:0, one launch (start us, length us, event | category | flops | bytes accessed | tf_op | source)
XLA Modules:
  0.0 105.9 jit_solution(12027316282644789905)
XLA Ops:
  3.3 2.2 %shard_map.86 = (bf16[4,256,256]{2,1,0:T(8,128)(2,1)S(1)}, f32[4,2,136,256]{3,2,1,0:T(8,128)S(1)}, f32[272,256]{1,0:T(8,128)S(1)}, f32[272,256]{1,0:T(8,128)S(1)}) custom-call(s32[1,8]{1,0:T(1,128)S(1)} %copy-done.6, bf16[256,1280]{1,0:T(8,128)(2,1)S(1)} %pad_maximum_fusion.packed_ref), custom_call_target="tpu_custom_call" | custom-call | flops 3000000000 | tf_op jit(solution)/shard_map/pallas_call | solution.py:241
  5.5 3.0 %collective-permute-start = (f32[272,256]{1,0:T(8,128)S(1)}, f32[272,256]{1,0:T(8,128)S(1)}, u32[]{:S(2)}, u32[]{:S(2)}) collective-permute-start(f32[272,256]{1,0:T(8,128)S(1)} %get-tuple-element.65.own_ref), channel_id=1, source_target_pairs={{0,1},{1,2},{2,3},{3,4},{4,5},{5,6},{6,7},{7,0},{8,9},{9,10},{10,1... | collective-permute-start | bytes 835592 | tf_op jit(solution)/shard_map/ppermute | solution.py:389
  10.0 9.0 %collective-permute-done.came_ref.refs_11_ = f32[272,256]{1,0:T(8,128)S(1)} collective-permute-done((f32[272,256]{1,0:T(8,128)S(1)}, f32[272,256]{1,0:T(8,128)S(1)}, u32[]{:S(2)}, u32[]{:S(2)}) %collective-permute-start) | collective-permute-done | bytes 278560 | tf_op jit(solution)/shard_map/ppermute | solution.py:389
  19.7 2.9 %shard_map.90 = (f32[2,2,128,1024]{3,2,1,0:T(8,128)S(1)}, f32[2,2,128,1024]{3,2,1,0:T(8,128)S(1)}, bf16[2,2,256,1024]{3,2,1,0:T(8,128)(2,1)S(1)}, f32[2,2,128,10...) custom-call(bf16[256,4096]{1,0:T(8,128)(2,1)S(1)} %bitcast.10, ...), custom_call_target="tpu_custom_call" | custom-call | flops 1500000000 | tf_op jit(solution)/shard_map/pallas_call | solution.py:241
  22.6 2.9 %shard_map.87 = (f32[2,2,128,1024]{3,2,1,0:T(8,128)S(1)}, f32[2,2,128,1024]{3,2,1,0:T(8,128)S(1)}, bf16[2,2,256,1024]{3,2,1,0:T(8,128)(2,1)S(1)}, f32[2,2,128,10...) custom-call(bf16[256,4096]{1,0:T(8,128)(2,1)S(1)} %bitcast.11, ...), custom_call_target="tpu_custom_call" | custom-call | flops 1500000000 | tf_op jit(solution)/shard_map/pallas_call | solution.py:241
  26.1 1.6 %collective-permute-start.4 = (f32[272,256]{1,0:T(8,128)S(1)}, f32[272,256]{1,0:T(8,128)S(1)}, u32[]{:S(2)}, u32[]{:S(2)}) collective-permute-start(f32[272,256]{1,0:T(8,128)S(1)} %shard_map.91), channel_id=1, source_target_pairs={{0,2},{1,3},{2,4},{3,5},{4,6},{5,7},{6,0},{7,1},{8,10},{9,11},{10,... | collective-permute-start | bytes 835592 | tf_op jit(solution)/shard_map/ppermute | solution.py:389
  28.5 5.1 %shard_map.89 = (f32[1024,128]{1,0:T(8,128)S(1)}, f32[1024,128]{1,0:T(8,128)S(1)}, f32[272,256]{1,0:T(8,128)S(1)}, f32[2,2,136,256]{3,2,1,0:T(8,128)S(1)}, f32[2,2,128,256]{3,2,1,0:T(8,128)S(1)}) custom-call(s32[1,8]{1,0:T(1,128)S(1)} %copy-done.6, bf16[256,4096]{1,0:T(8,128)(2,1)S(1)} %bitcast.12, bf16[256,512]{1,0:T(8,128)(2,1)S(1)} %bitcast.17, ...), custom_call_target="tpu_custom_call" | custom-call | flops 6000000000 | tf_op jit(solution)/shard_map/pallas_call | solution.py:241
  33.6 4.7 %collective-permute-start.9 = (f32[272,256]{1,0:T(8,128)S(1)}, f32[272,256]{1,0:T(8,128)S(1)}, u32[]{:S(2)}, u32[]{:S(2)}) collective-permute-start(f32[272,256]{1,0:T(8,128)S(1)} %get-tuple-element.87.own_ref), channel_id=1, source_target_pairs={{0,7},{1,0},{2,1},{3,2},{4,3},{5,4},{6,5},{7,6},{8,15},{9,8},{10,9... | collective-permute-start | bytes 835592 | tf_op jit(solution)/shard_map/ppermute | solution.py:389
  38.3 5.1 %shard_map.92 = (f32[1024,128]{1,0:T(8,128)S(1)}, f32[1024,128]{1,0:T(8,128)S(1)}, f32[272,256]{1,0:T(8,128)S(1)}, f32[2,2,136,256]{3,2,1,0:T(8,128)S(1)}, f32[2,2,128,256]{3,2,1,0:T(8,128)S(1)}) custom-call(s32[1,8]{1,0:T(1,128)S(1)} %copy-done.6, bf16[256,4096]{1,0:T(8,128)(2,1)S(1)} %bitcast.13, bf16[256,512]{1,0:T(8,128)(2,1)S(1)} %bitcast.18, ...), custom_call_target="tpu_custom_call" | custom-call | flops 6000000000 | tf_op jit(solution)/shard_map/pallas_call | solution.py:241
  45.2 7.4 %collective-permute-done.10.came_ref.refs_6_ = f32[272,256]{1,0:T(8,128)S(1)} collective-permute-done((f32[272,256]{1,0:T(8,128)S(1)}, f32[272,256]{1,0:T(8,128)S(1)}, u32[]{:S(2)}, u32[]{:S(2)}) %collective-permute-start.10) | collective-permute-done | bytes 278560 | tf_op jit(solution)/shard_map/ppermute | solution.py:389
  55.4 3.8 %collective-permute-start.7 = (f32[512,128]{1,0:T(8,128)S(1)}, f32[512,128]{1,0:T(8,128)S(1)}, u32[]{:S(2)}, u32[]{:S(2)}) collective-permute-start(f32[512,128]{1,0:T(8,128)S(1)} %get-tuple-element.85), channel_id=1, source_target_pairs={{0,1},{1,0},{2,3},{3,2},{4,5},{5,4},{6,7},{7,6},{8,9},{9,8},{10,11... | collective-permute-start | bytes 786440 | tf_op jit(solution)/shard_map/ppermute | solution.py:307
  60.6 2.2 %collective-permute-done.15.refs_7_ = f32[272,256]{1,0:T(8,128)S(1)} collective-permute-done((f32[272,256]{1,0:T(8,128)S(1)}, f32[272,256]{1,0:T(8,128)S(1)}, u32[]{:S(2)}, u32[]{:S(2)}) %collective-permute-start.15) | collective-permute-done | bytes 278560 | tf_op jit(solution)/shard_map/ppermute | solution.py:389
  64.4 4.3 %collective-permute-done.7.refs_2_ = f32[512,128]{1,0:T(8,128)S(1)} collective-permute-done((f32[512,128]{1,0:T(8,128)S(1)}, f32[512,128]{1,0:T(8,128)S(1)}, u32[]{:S(2)}, u32[]{:S(2)}) %collective-permute-start.7) | collective-permute-done | bytes 262176 | tf_op jit(solution)/shard_map/ppermute | solution.py:307
  69.6 1.8 %collective-permute-start.19 = (f32[256,128]{1,0:T(8,128)S(1)}, f32[256,128]{1,0:T(8,128)S(1)}, u32[]{:S(2)}, u32[]{:S(2)}) collective-permute-start(f32[256,128]{1,0:T(8,128)S(1)} %shard_map.101.refs_0_), channel_id=1, source_target_pairs={{0,17},{1,16},{2,19},{3,18},{4,21},{5,20},{6,23},{7,22},{8,25},{9,... | collective-permute-start | bytes 393224 | tf_op jit(solution)/shard_map/ppermute | solution.py:307
  74.0 3.5 %collective-permute-start.13 = (f32[128,128]{1,0:T(8,128)S(1)}, f32[128,128]{1,0:T(8,128)S(1)}, u32[]{:S(2)}, u32[]{:S(2)}) collective-permute-start(f32[128,128]{1,0:T(8,128)S(1)} %get-tuple-element.96), channel_id=1, source_target_pairs={{0,6},{1,7},{2,4},{3,5},{4,2},{5,3},{6,0},{7,1},{8,14},{9,15},{10,... | collective-permute-start | bytes 196616 | tf_op jit(solution)/shard_map/ppermute | solution.py:307
  78.4 2.2 %collective-permute-done.13.refs_3_ = f32[128,128]{1,0:T(8,128)S(1)} collective-permute-done((f32[128,128]{1,0:T(8,128)S(1)}, f32[128,128]{1,0:T(8,128)S(1)}, u32[]{:S(2)}, u32[]{:S(2)}) %collective-permute-start.13) | collective-permute-done | bytes 65568 | tf_op jit(solution)/shard_map/ppermute | solution.py:307
  80.6 3.1 %collective-permute-start.22 = (f32[128,128]{1,0:T(8,128)S(1)}, f32[128,128]{1,0:T(8,128)S(1)}, u32[]{:S(2)}, u32[]{:S(2)}) collective-permute-start(f32[128,128]{1,0:T(8,128)S(1)} %shard_map.97.refs_0_), channel_id=1, source_target_pairs={{0,6},{1,7},{2,4},{3,5},{4,2},{5,3},{6,0},{7,1},{8,14},{9,15},{10,... | collective-permute-start | bytes 196616 | tf_op jit(solution)/shard_map/ppermute | solution.py:307
  85.1 3.1 %collective-permute-start.28 = (f32[256,128]{1,0:T(8,128)S(1)}, f32[256,128]{1,0:T(8,128)S(1)}, u32[]{:S(2)}, u32[]{:S(2)}) collective-permute-start(f32[256,128]{1,0:T(8,128)S(1)} %shard_map.104.refs_0_), channel_id=1, source_target_pairs={{0,6},{1,7},{2,4},{3,5},{4,2},{5,3},{6,0},{7,1},{8,14},{9,15},{10,... | collective-permute-start | bytes 393224 | tf_op jit(solution)/shard_map/ppermute | solution.py:307
  89.1 1.8 %collective-permute-start.25 = (f32[512,128]{1,0:T(8,128)S(1)}, f32[512,128]{1,0:T(8,128)S(1)}, u32[]{:S(2)}, u32[]{:S(2)}) collective-permute-start(f32[512,128]{1,0:T(8,128)S(1)} %shard_map.102.refs_0_), channel_id=1, source_target_pairs={{0,17},{1,16},{2,19},{3,18},{4,21},{5,20},{6,23},{7,22},{8,25},{9,... | collective-permute-start | bytes 786440 | tf_op jit(solution)/shard_map/ppermute | solution.py:307
  90.9 1.8 %collective-permute-start.24 = (f32[512,128]{1,0:T(8,128)S(1)}, f32[512,128]{1,0:T(8,128)S(1)}, u32[]{:S(2)}, u32[]{:S(2)}) collective-permute-start(f32[512,128]{1,0:T(8,128)S(1)} %shard_map.102.refs_0_), channel_id=1, source_target_pairs={{0,1},{1,0},{2,3},{3,2},{4,5},{5,4},{6,7},{7,6},{8,9},{9,8},{10,11... | collective-permute-start | bytes 786440 | tf_op jit(solution)/shard_map/ppermute | solution.py:307
  92.7 2.5 %collective-permute-start.27 = (f32[256,128]{1,0:T(8,128)S(1)}, f32[256,128]{1,0:T(8,128)S(1)}, u32[]{:S(2)}, u32[]{:S(2)}) collective-permute-start(f32[256,128]{1,0:T(8,128)S(1)} %shard_map.104.refs_0_), channel_id=1, source_target_pairs={{0,4},{1,5},{2,6},{3,7},{4,0},{5,1},{6,2},{7,3},{8,12},{9,13},{10,... | collective-permute-start | bytes 393224 | tf_op jit(solution)/shard_map/ppermute | solution.py:307
  95.6 4.3 %collective-permute-done.27.refs_2_ = f32[256,128]{1,0:T(8,128)S(1)} collective-permute-done((f32[256,128]{1,0:T(8,128)S(1)}, f32[256,128]{1,0:T(8,128)S(1)}, u32[]{:S(2)}, u32[]{:S(2)}) %collective-permute-start.27) | collective-permute-done | bytes 131104 | tf_op jit(solution)/shard_map/ppermute | solution.py:307
  102.0 2.3 %collective-permute-done.30.key_came = f32[256,128]{1,0:T(8,128)S(1)} collective-permute-done((f32[256,128]{1,0:T(8,128)S(1)}, f32[256,128]{1,0:T(8,128)S(1)}, u32[]{:S(2)}, u32[]{:S(2)}) %collective-permute-start.30) | collective-permute-done | bytes 131104 | tf_op jit(solution)/shard_map/ppermute | solution.py:307
  104.3 1.6 %shard_map.106 = (f32[4096,128]{1,0:T(8,128)}, f32[512,128]{1,0:T(8,128)}) custom-call(f32[2048,128]{1,0:T(8,128)S(1)} %shard_map.103.own_ref, f32[2048,128]{1,0:T(8,128)S(1)} %collective-permute-done.29.came_ref, f32[256,128]{1,0:T(8,128)S(1)} %shard_map.105.key_own, f32[256,128]{1,0:T(8,128)S(1)} %collective-permute-done.30.key_came), custom_call_target="tpu_custom_call" | custom-call | flops 1000000000 | tf_op jit(solution)/shard_map/pallas_call | solution.py:241
  (75 shorter events, 22.8 us)
Async XLA Ops:
  5.5 13.5 %collective-permute-start = (f32[272,256]{1,0:T(8,128)S(1)}, f32[272,256]{1,0:T(8,128)S(1)}, u32[]{:S(2)}, u32[]{:S(2)}) collective-permute-start(f32[272,256]{1,0:T(8,128)S(1)} %get-tuple-element.65.own_ref), channel_id=1, source_target_pairs={{0,1},{1,2},{2,3},{3,4},{4,5},{5,6},{6,7},{7,0},{8,9},{9,10},{10,1... | collective-permute-start | bytes 835592 | tf_op jit(solution)/shard_map/ppermute | solution.py:389
  8.5 17.0 %collective-permute-start.3 = (f32[272,256]{1,0:T(8,128)S(1)}, f32[272,256]{1,0:T(8,128)S(1)}, u32[]{:S(2)}, u32[]{:S(2)}) collective-permute-start(f32[272,256]{1,0:T(8,128)S(1)} %get-tuple-element.74.own_ref), channel_id=1, source_target_pairs={{0,1},{1,2},{2,3},{3,4},{4,5},{5,6},{6,7},{7,0},{8,9},{9,10},{10,1... | collective-permute-start | bytes 835592 | tf_op jit(solution)/shard_map/ppermute | solution.py:389
  19.6 8.9 %collective-permute-start.1 = (f32[272,256]{1,0:T(8,128)S(1)}, f32[272,256]{1,0:T(8,128)S(1)}, u32[]{:S(2)}, u32[]{:S(2)}) collective-permute-start(f32[272,256]{1,0:T(8,128)S(1)} %shard_map.88), channel_id=1, source_target_pairs={{0,2},{1,3},{2,4},{3,5},{4,6},{5,7},{6,0},{7,1},{8,10},{9,11},{10,... | collective-permute-start | bytes 835592 | tf_op jit(solution)/shard_map/ppermute | solution.py:389
  26.1 12.2 %collective-permute-start.4 = (f32[272,256]{1,0:T(8,128)S(1)}, f32[272,256]{1,0:T(8,128)S(1)}, u32[]{:S(2)}, u32[]{:S(2)}) collective-permute-start(f32[272,256]{1,0:T(8,128)S(1)} %shard_map.91), channel_id=1, source_target_pairs={{0,2},{1,3},{2,4},{3,5},{4,6},{5,7},{6,0},{7,1},{8,10},{9,11},{10,... | collective-permute-start | bytes 835592 | tf_op jit(solution)/shard_map/ppermute | solution.py:389
  33.6 10.5 %collective-permute-start.9 = (f32[272,256]{1,0:T(8,128)S(1)}, f32[272,256]{1,0:T(8,128)S(1)}, u32[]{:S(2)}, u32[]{:S(2)}) collective-permute-start(f32[272,256]{1,0:T(8,128)S(1)} %get-tuple-element.87.own_ref), channel_id=1, source_target_pairs={{0,7},{1,0},{2,1},{3,2},{4,3},{5,4},{6,5},{7,6},{8,15},{9,8},{10,9... | collective-permute-start | bytes 835592 | tf_op jit(solution)/shard_map/ppermute | solution.py:389
  43.4 10.3 %collective-permute-start.5 = (f32[1024,128]{1,0:T(8,128)S(1)}, f32[1024,128]{1,0:T(8,128)S(1)}, u32[]{:S(2)}, u32[]{:S(2)}) collective-permute-start(f32[1024,128]{1,0:T(8,128)S(1)} %get-tuple-element.82), channel_id=1, source_target_pairs={{0,8},{1,9},{2,10},{3,11},{4,12},{5,13},{6,14},{7,15},{8,0},{9,1},... | collective-permute-start | bytes 1572872 | tf_op jit(solution)/shard_map/ppermute | solution.py:307
  44.0 8.6 %collective-permute-start.10 = (f32[272,256]{1,0:T(8,128)S(1)}, f32[272,256]{1,0:T(8,128)S(1)}, u32[]{:S(2)}, u32[]{:S(2)}) collective-permute-start(f32[272,256]{1,0:T(8,128)S(1)} %get-tuple-element.88.own_ref), channel_id=1, source_target_pairs={{0,7},{1,0},{2,1},{3,2},{4,3},{5,4},{6,5},{7,6},{8,15},{9,8},{10,9... | collective-permute-start | bytes 835592 | tf_op jit(solution)/shard_map/ppermute | solution.py:389
  44.7 14.5 %collective-permute-start.14 = (f32[272,256]{1,0:T(8,128)S(1)}, f32[272,256]{1,0:T(8,128)S(1)}, u32[]{:S(2)}, u32[]{:S(2)}) collective-permute-start(f32[272,256]{1,0:T(8,128)S(1)} %shard_map.94), channel_id=1, source_target_pairs={{0,6},{1,7},{2,0},{3,1},{4,2},{5,3},{6,4},{7,5},{8,14},{9,15},{10,... | collective-permute-start | bytes 835592 | tf_op jit(solution)/shard_map/ppermute | solution.py:389
  53.2 9.6 %collective-permute-start.15 = (f32[272,256]{1,0:T(8,128)S(1)}, f32[272,256]{1,0:T(8,128)S(1)}, u32[]{:S(2)}, u32[]{:S(2)}) collective-permute-start(f32[272,256]{1,0:T(8,128)S(1)} %shard_map.95), channel_id=1, source_target_pairs={{0,6},{1,7},{2,0},{3,1},{4,2},{5,3},{6,4},{7,5},{8,14},{9,15},{10,... | collective-permute-start | bytes 835592 | tf_op jit(solution)/shard_map/ppermute | solution.py:389
  53.8 10.6 %collective-permute-start.6 = (f32[512,128]{1,0:T(8,128)S(1)}, f32[512,128]{1,0:T(8,128)S(1)}, u32[]{:S(2)}, u32[]{:S(2)}) collective-permute-start(f32[512,128]{1,0:T(8,128)S(1)} %get-tuple-element.84), channel_id=1, source_target_pairs={{0,16},{1,17},{2,18},{3,19},{4,20},{5,21},{6,22},{7,23},{8,24},{9,... | collective-permute-start | bytes 786440 | tf_op jit(solution)/shard_map/ppermute | solution.py:307
  55.4 13.3 %collective-permute-start.7 = (f32[512,128]{1,0:T(8,128)S(1)}, f32[512,128]{1,0:T(8,128)S(1)}, u32[]{:S(2)}, u32[]{:S(2)}) collective-permute-start(f32[512,128]{1,0:T(8,128)S(1)} %get-tuple-element.85), channel_id=1, source_target_pairs={{0,1},{1,0},{2,3},{3,2},{4,5},{5,4},{6,7},{7,6},{8,9},{9,8},{10,11... | collective-permute-start | bytes 786440 | tf_op jit(solution)/shard_map/ppermute | solution.py:307
  59.1 10.3 %collective-permute-start.8 = (f32[512,128]{1,0:T(8,128)S(1)}, f32[512,128]{1,0:T(8,128)S(1)}, u32[]{:S(2)}, u32[]{:S(2)}) collective-permute-start(f32[512,128]{1,0:T(8,128)S(1)} %get-tuple-element.86), channel_id=1, source_target_pairs={{0,17},{1,16},{2,19},{3,18},{4,21},{5,20},{6,23},{7,22},{8,25},{9,... | collective-permute-start | bytes 786440 | tf_op jit(solution)/shard_map/ppermute | solution.py:307
  69.6 11.0 %collective-permute-start.19 = (f32[256,128]{1,0:T(8,128)S(1)}, f32[256,128]{1,0:T(8,128)S(1)}, u32[]{:S(2)}, u32[]{:S(2)}) collective-permute-start(f32[256,128]{1,0:T(8,128)S(1)} %shard_map.101.refs_0_), channel_id=1, source_target_pairs={{0,17},{1,16},{2,19},{3,18},{4,21},{5,20},{6,23},{7,22},{8,25},{9,... | collective-permute-start | bytes 393224 | tf_op jit(solution)/shard_map/ppermute | solution.py:307
  71.4 9.2 %collective-permute-start.18 = (f32[256,128]{1,0:T(8,128)S(1)}, f32[256,128]{1,0:T(8,128)S(1)}, u32[]{:S(2)}, u32[]{:S(2)}) collective-permute-start(f32[256,128]{1,0:T(8,128)S(1)} %shard_map.101.refs_0_), channel_id=1, source_target_pairs={{0,1},{1,0},{2,3},{3,2},{4,5},{5,4},{6,7},{7,6},{8,9},{9,8},{10,11... | collective-permute-start | bytes 393224 | tf_op jit(solution)/shard_map/ppermute | solution.py:307
  72.6 8.0 %collective-permute-start.17 = (f32[256,128]{1,0:T(8,128)S(1)}, f32[256,128]{1,0:T(8,128)S(1)}, u32[]{:S(2)}, u32[]{:S(2)}) collective-permute-start(f32[256,128]{1,0:T(8,128)S(1)} %shard_map.101.refs_0_), channel_id=1, source_target_pairs={{0,16},{1,17},{2,18},{3,19},{4,20},{5,21},{6,22},{7,23},{8,24},{9,... | collective-permute-start | bytes 393224 | tf_op jit(solution)/shard_map/ppermute | solution.py:307
  74.0 6.5 %collective-permute-start.13 = (f32[128,128]{1,0:T(8,128)S(1)}, f32[128,128]{1,0:T(8,128)S(1)}, u32[]{:S(2)}, u32[]{:S(2)}) collective-permute-start(f32[128,128]{1,0:T(8,128)S(1)} %get-tuple-element.96), channel_id=1, source_target_pairs={{0,6},{1,7},{2,4},{3,5},{4,2},{5,3},{6,0},{7,1},{8,14},{9,15},{10,... | collective-permute-start | bytes 196616 | tf_op jit(solution)/shard_map/ppermute | solution.py:307
  80.6 7.6 %collective-permute-start.22 = (f32[128,128]{1,0:T(8,128)S(1)}, f32[128,128]{1,0:T(8,128)S(1)}, u32[]{:S(2)}, u32[]{:S(2)}) collective-permute-start(f32[128,128]{1,0:T(8,128)S(1)} %shard_map.97.refs_0_), channel_id=1, source_target_pairs={{0,6},{1,7},{2,4},{3,5},{4,2},{5,3},{6,0},{7,1},{8,14},{9,15},{10,... | collective-permute-start | bytes 196616 | tf_op jit(solution)/shard_map/ppermute | solution.py:307
  83.7 5.3 %collective-permute-start.21 = (f32[128,128]{1,0:T(8,128)S(1)}, f32[128,128]{1,0:T(8,128)S(1)}, u32[]{:S(2)}, u32[]{:S(2)}) collective-permute-start(f32[128,128]{1,0:T(8,128)S(1)} %shard_map.97.refs_0_), channel_id=1, source_target_pairs={{0,4},{1,5},{2,6},{3,7},{4,0},{5,1},{6,2},{7,3},{8,12},{9,13},{10,... | collective-permute-start | bytes 196616 | tf_op jit(solution)/shard_map/ppermute | solution.py:307
  85.1 10.0 %collective-permute-start.28 = (f32[256,128]{1,0:T(8,128)S(1)}, f32[256,128]{1,0:T(8,128)S(1)}, u32[]{:S(2)}, u32[]{:S(2)}) collective-permute-start(f32[256,128]{1,0:T(8,128)S(1)} %shard_map.104.refs_0_), channel_id=1, source_target_pairs={{0,6},{1,7},{2,4},{3,5},{4,2},{5,3},{6,0},{7,1},{8,14},{9,15},{10,... | collective-permute-start | bytes 393224 | tf_op jit(solution)/shard_map/ppermute | solution.py:307
  89.1 12.2 %collective-permute-start.25 = (f32[512,128]{1,0:T(8,128)S(1)}, f32[512,128]{1,0:T(8,128)S(1)}, u32[]{:S(2)}, u32[]{:S(2)}) collective-permute-start(f32[512,128]{1,0:T(8,128)S(1)} %shard_map.102.refs_0_), channel_id=1, source_target_pairs={{0,17},{1,16},{2,19},{3,18},{4,21},{5,20},{6,23},{7,22},{8,25},{9,... | collective-permute-start | bytes 786440 | tf_op jit(solution)/shard_map/ppermute | solution.py:307
  90.9 10.4 %collective-permute-start.24 = (f32[512,128]{1,0:T(8,128)S(1)}, f32[512,128]{1,0:T(8,128)S(1)}, u32[]{:S(2)}, u32[]{:S(2)}) collective-permute-start(f32[512,128]{1,0:T(8,128)S(1)} %shard_map.102.refs_0_), channel_id=1, source_target_pairs={{0,1},{1,0},{2,3},{3,2},{4,5},{5,4},{6,7},{7,6},{8,9},{9,8},{10,11... | collective-permute-start | bytes 786440 | tf_op jit(solution)/shard_map/ppermute | solution.py:307
  92.6 8.6 %collective-permute-start.23 = (f32[512,128]{1,0:T(8,128)S(1)}, f32[512,128]{1,0:T(8,128)S(1)}, u32[]{:S(2)}, u32[]{:S(2)}) collective-permute-start(f32[512,128]{1,0:T(8,128)S(1)} %shard_map.102.refs_0_), channel_id=1, source_target_pairs={{0,16},{1,17},{2,18},{3,19},{4,20},{5,21},{6,22},{7,23},{8,24},{9,... | collective-permute-start | bytes 786440 | tf_op jit(solution)/shard_map/ppermute | solution.py:307
  92.7 7.3 %collective-permute-start.27 = (f32[256,128]{1,0:T(8,128)S(1)}, f32[256,128]{1,0:T(8,128)S(1)}, u32[]{:S(2)}, u32[]{:S(2)}) collective-permute-start(f32[256,128]{1,0:T(8,128)S(1)} %shard_map.104.refs_0_), channel_id=1, source_target_pairs={{0,4},{1,5},{2,6},{3,7},{4,0},{5,1},{6,2},{7,3},{8,12},{9,13},{10,... | collective-permute-start | bytes 393224 | tf_op jit(solution)/shard_map/ppermute | solution.py:307
  95.1 6.1 %collective-permute-start.26 = (f32[256,128]{1,0:T(8,128)S(1)}, f32[256,128]{1,0:T(8,128)S(1)}, u32[]{:S(2)}, u32[]{:S(2)}) collective-permute-start(f32[256,128]{1,0:T(8,128)S(1)} %shard_map.104.refs_0_), channel_id=1, source_target_pairs={{0,2},{1,3},{2,0},{3,1},{4,6},{5,7},{6,4},{7,5},{8,10},{9,11},{10,... | collective-permute-start | bytes 393224 | tf_op jit(solution)/shard_map/ppermute | solution.py:307
  (14 other events, 124.3 us)

commit v7 on v6

--- a/solution.py
+++ b/solution.py
@@ -314,7 +314,7 @@
         out = local_call(
             functools.partial(split_kernel, stage, layout),
             [rows_of(size, width)] * pieces,
-            0.4,
+            0.15,
             *[a for g in groups for a in g],
         )
         return out, layout
@@ -325,7 +325,7 @@
         return local_call(
             functools.partial(join_pieces_kernel, stage, layout),
             rows_of(total, x.shape[1]),
-            0.4,
+            0.15,
             *came,
         )
 
@@ -342,13 +342,29 @@
         return x if layout is None else self.join(x, stage, layout)
 
 
-def assemble_kernel(heads, half, stage, layout, own_ref, came_ref, key_own, key_came, out_ref, key_ref):
-    join_pieces_kernel(stage, layout, key_own, key_came, key_ref)
-    mine = lax.axis_index("dp") & 1
-    for side, ref in enumerate((own_ref, came_ref)):
-        for i in range(heads):
-            start = pl.multiple_of((2 * i + (mine ^ side)) * half, PAD)
-            out_ref[pl.ds(start, half), :] = ref[i * half : (i + 1) * half]
+def after(x, *others):
+    return lax.optimization_barrier((x, others))[0]
+
+
+def assemble_kernel(parts, half, stage, core, key_layout, *refs):
+    pieces = 1 << len(stage)
+    sides = (refs[:pieces], refs[pieces : 2 * pieces])
+    key_own, key_came, out_ref, key_ref = refs[2 * pieces :]
+    join_pieces_kernel(core, key_layout, key_own, key_came, key_ref)
+    mine = index_in(stage)
+    mine_core = index_in(core)
+    for side, held in enumerate(sides):
+        for m, ref in enumerate(held):
+            at = 0
+            for low, high in parts:
+                size = (high - low) * half // pieces
+                step = math.gcd(size, half)
+                for k in range(0, size, step):
+                    flat = (mine ^ m) * size + k
+                    head = low + lax.div(flat, jnp.int32(half))
+                    row = (2 * head + (mine_core ^ side)) * half + lax.rem(flat, jnp.int32(half))
+                    out_ref[pl.ds(pl.multiple_of(row, PAD), step), :] = ref[at + k : at + k + step]
+                at += size
 
 
 def solution(mesh):
@@ -484,21 +500,27 @@
         extra, layout = total.scatter(extra, total.stages[0], 2 * WHOLE)
         extra_layouts = [layout]
         x, extra = lax.optimization_barrier((x, extra))
-        for stage, layout in reversed(list(zip(total.stages, layouts))):
+        for stage, layout in reversed(list(zip(total.stages[1:], layouts[1:]))):
             x = total.gather(x, stage, layout)
+        own = [x] + [total.send(x, total.stages[0], m) for m in range(1, 1 << len(total.stages[0]))]
         for stage in total.stages[1:]:
             extra, layout = total.scatter(extra, stage, 2 * WHOLE)
             extra_layouts.append(layout)
         extra = total.split(extra, [])[0][0]
         for stage, layout in reversed(list(zip(total.stages, extra_layouts))):
             extra = total.gather(extra, stage, layout)
-        x, extra = lax.optimization_barrier((x, extra))
-        halves = [x, total.send(x, total.core, 1), extra, total.send(extra, total.core, 1)]
+        own, extra = lax.optimization_barrier((own, extra))
+        other = [total.send(piece, total.core, 1) for piece in own]
         grad_q, grad_k = local_call(
-            functools.partial(assemble_kernel, hk, group * hd // 2, total.core, core_layout),
+            functools.partial(
+                assemble_kernel, parts, group * hd // 2, total.stages[0], total.core, core_layout
+            ),
             [rows_of(hq * hd, hd), rows_of(hk * hd, hd)],
             1.0,
-            *halves,
+            *own,
+            *other,
+            extra,
+            total.send(extra, total.core, 1),
         )
         return grad_q.reshape(hq, hd, hd), grad_k.reshape(hk, hd, hd)
 

time: 106 us -> 106 us (level)
    ppermute x23 -> x26, starting transfers between devices: 28.6 us -> 29.2 us  [send(): return lax.ppermute(x, ('dp', 'seq'), perm)]
    ppermute x23 -> x26, waiting for transfers between devices: 16.9 us -> 16.3 us  [send(): return lax.ppermute(x, ('dp', 'seq'), perm)]
    pallas_call x21 -> x20, Pallas kernels: 25.4 us -> 25.3 us  [local_call(): pl.pallas_call(body, out_shape=out_shape, in_specs=[SMEM] * len(first) +...]
  transfers between devices with their start and end apart: 31 -> 34, of which waited for: 12 -> 12; matrix products, arithmetic and copies ran while one was open for 0% -> 0% of each run, Pallas kernels for 20% -> 20%
where the time goes in v7:
time: 106 us
  starting transfers between devices  41.1 us (39%)
  waiting for transfers between devices  35.7 us (34%)
  Pallas kernels  25.3 us (24%)
  local copies, waits for them, and re-layouts  1.56 us (1%)
  other arithmetic  1.08 us (1%)
    ppermute x26, starting transfers between devices, send(): return lax.ppermute(x, ('dp', 'seq'), perm)  29.2 us
    pallas_call x20, Pallas kernels, local_call(): pl.pallas_call(body, out_shape=out_shape, in_specs=[SMEM] * len(first) +...  25.3 us
    ppermute x8, waiting for transfers between devices, shift(): return lax.ppermute(own, 'seq', ring)  19.4 us
    ppermute x26, waiting for transfers between devices, send(): return lax.ppermute(x, ('dp', 'seq'), perm)  16.3 us
    ppermute x8, starting transfers between devices, shift(): return lax.ppermute(own, 'seq', ring)  12 us
  transfers between devices with their start and end apart: 34, of which 12 were waited for; matrix products, arithmetic and copies ran while one was open for 0% of the time, Pallas kernels for 20%

profile of v7, /device:TPU:0, one launch (start us, length us, event | category | flops | bytes accessed | tf_op | source)
XLA Modules:
  0.0 105.8 jit_solution(7697941784534473414)
XLA Ops:
  3.3 2.2 %shard_map.86 = (bf16[4,256,256]{2,1,0:T(8,128)(2,1)S(1)}, f32[4,2,136,256]{3,2,1,0:T(8,128)S(1)}, f32[272,256]{1,0:T(8,128)S(1)}, f32[272,256]{1,0:T(8,128)S(1)}) custom-call(s32[1,8]{1,0:T(1,128)S(1)} %copy-done.6, bf16[256,1280]{1,0:T(8,128)(2,1)S(1)} %pad_maximum_fusion.packed_ref), custom_call_target="tpu_custom_call" | custom-call | flops 3000000000 | tf_op jit(solution)/shard_map/pallas_call | solution.py:241
  5.5 3.0 %collective-permute-start = (f32[272,256]{1,0:T(8,128)S(1)}, f32[272,256]{1,0:T(8,128)S(1)}, u32[]{:S(2)}, u32[]{:S(2)}) collective-permute-start(f32[272,256]{1,0:T(8,128)S(1)} %get-tuple-element.68.own_ref), channel_id=1, source_target_pairs={{0,1},{1,2},{2,3},{3,4},{4,5},{5,6},{6,7},{7,0},{8,9},{9,10},{10,1... | collective-permute-start | bytes 835592 | tf_op jit(solution)/shard_map/ppermute | solution.py:405
  10.0 9.0 %collective-permute-done.came_ref.refs_11_ = f32[272,256]{1,0:T(8,128)S(1)} collective-permute-done((f32[272,256]{1,0:T(8,128)S(1)}, f32[272,256]{1,0:T(8,128)S(1)}, u32[]{:S(2)}, u32[]{:S(2)}) %collective-permute-start) | collective-permute-done | bytes 278560 | tf_op jit(solution)/shard_map/ppermute | solution.py:405
  19.7 2.9 %shard_map.90 = (f32[2,2,128,1024]{3,2,1,0:T(8,128)S(1)}, f32[2,2,128,1024]{3,2,1,0:T(8,128)S(1)}, bf16[2,2,256,1024]{3,2,1,0:T(8,128)(2,1)S(1)}, f32[2,2,128,10...) custom-call(bf16[256,4096]{1,0:T(8,128)(2,1)S(1)} %bitcast.10, ...), custom_call_target="tpu_custom_call" | custom-call | flops 1500000000 | tf_op jit(solution)/shard_map/pallas_call | solution.py:241
  22.6 2.9 %shard_map.87 = (f32[2,2,128,1024]{3,2,1,0:T(8,128)S(1)}, f32[2,2,128,1024]{3,2,1,0:T(8,128)S(1)}, bf16[2,2,256,1024]{3,2,1,0:T(8,128)(2,1)S(1)}, f32[2,2,128,10...) custom-call(bf16[256,4096]{1,0:T(8,128)(2,1)S(1)} %bitcast.11, ...), custom_call_target="tpu_custom_call" | custom-call | flops 1500000000 | tf_op jit(solution)/shard_map/pallas_call | solution.py:241
  26.1 1.6 %collective-permute-start.4 = (f32[272,256]{1,0:T(8,128)S(1)}, f32[272,256]{1,0:T(8,128)S(1)}, u32[]{:S(2)}, u32[]{:S(2)}) collective-permute-start(f32[272,256]{1,0:T(8,128)S(1)} %shard_map.91), channel_id=1, source_target_pairs={{0,2},{1,3},{2,4},{3,5},{4,6},{5,7},{6,0},{7,1},{8,10},{9,11},{10,... | collective-permute-start | bytes 835592 | tf_op jit(solution)/shard_map/ppermute | solution.py:405
  28.5 5.1 %shard_map.89 = (f32[1024,128]{1,0:T(8,128)S(1)}, f32[1024,128]{1,0:T(8,128)S(1)}, f32[272,256]{1,0:T(8,128)S(1)}, f32[2,2,136,256]{3,2,1,0:T(8,128)S(1)}, f32[2,2,128,256]{3,2,1,0:T(8,128)S(1)}) custom-call(s32[1,8]{1,0:T(1,128)S(1)} %copy-done.6, bf16[256,4096]{1,0:T(8,128)(2,1)S(1)} %bitcast.12, bf16[256,512]{1,0:T(8,128)(2,1)S(1)} %bitcast.17, ...), custom_call_target="tpu_custom_call" | custom-call | flops 6000000000 | tf_op jit(solution)/shard_map/pallas_call | solution.py:241
  33.6 4.7 %collective-permute-start.9 = (f32[272,256]{1,0:T(8,128)S(1)}, f32[272,256]{1,0:T(8,128)S(1)}, u32[]{:S(2)}, u32[]{:S(2)}) collective-permute-start(f32[272,256]{1,0:T(8,128)S(1)} %get-tuple-element.90.own_ref), channel_id=1, source_target_pairs={{0,7},{1,0},{2,1},{3,2},{4,3},{5,4},{6,5},{7,6},{8,15},{9,8},{10,9... | collective-permute-start | bytes 835592 | tf_op jit(solution)/shard_map/ppermute | solution.py:405
  38.3 5.1 %shard_map.92 = (f32[1024,128]{1,0:T(8,128)S(1)}, f32[1024,128]{1,0:T(8,128)S(1)}, f32[272,256]{1,0:T(8,128)S(1)}, f32[2,2,136,256]{3,2,1,0:T(8,128)S(1)}, f32[2,2,128,256]{3,2,1,0:T(8,128)S(1)}) custom-call(s32[1,8]{1,0:T(1,128)S(1)} %copy-done.6, bf16[256,4096]{1,0:T(8,128)(2,1)S(1)} %bitcast.13, bf16[256,512]{1,0:T(8,128)(2,1)S(1)} %bitcast.18, ...), custom_call_target="tpu_custom_call" | custom-call | flops 6000000000 | tf_op jit(solution)/shard_map/pallas_call | solution.py:241
  45.2 7.4 %collective-permute-done.10.came_ref.refs_6_ = f32[272,256]{1,0:T(8,128)S(1)} collective-permute-done((f32[272,256]{1,0:T(8,128)S(1)}, f32[272,256]{1,0:T(8,128)S(1)}, u32[]{:S(2)}, u32[]{:S(2)}) %collective-permute-start.10) | collective-permute-done | bytes 278560 | tf_op jit(solution)/shard_map/ppermute | solution.py:405
  55.4 3.8 %collective-permute-start.7 = (f32[512,128]{1,0:T(8,128)S(1)}, f32[512,128]{1,0:T(8,128)S(1)}, u32[]{:S(2)}, u32[]{:S(2)}) collective-permute-start(f32[512,128]{1,0:T(8,128)S(1)} %get-tuple-element.88), channel_id=1, source_target_pairs={{0,1},{1,0},{2,3},{3,2},{4,5},{5,4},{6,7},{7,6},{8,9},{9,8},{10,11... | collective-permute-start | bytes 786440 | tf_op jit(solution)/shard_map/ppermute | solution.py:307
  60.6 2.2 %collective-permute-done.15.refs_7_ = f32[272,256]{1,0:T(8,128)S(1)} collective-permute-done((f32[272,256]{1,0:T(8,128)S(1)}, f32[272,256]{1,0:T(8,128)S(1)}, u32[]{:S(2)}, u32[]{:S(2)}) %collective-permute-start.15) | collective-permute-done | bytes 278560 | tf_op jit(solution)/shard_map/ppermute | solution.py:405
  64.4 4.3 %collective-permute-done.7.refs_2_ = f32[512,128]{1,0:T(8,128)S(1)} collective-permute-done((f32[512,128]{1,0:T(8,128)S(1)}, f32[512,128]{1,0:T(8,128)S(1)}, u32[]{:S(2)}, u32[]{:S(2)}) %collective-permute-start.7) | collective-permute-done | bytes 262176 | tf_op jit(solution)/shard_map/ppermute | solution.py:307
  69.6 1.8 %collective-permute-start.19 = (f32[256,128]{1,0:T(8,128)S(1)}, f32[256,128]{1,0:T(8,128)S(1)}, u32[]{:S(2)}, u32[]{:S(2)}) collective-permute-start(f32[256,128]{1,0:T(8,128)S(1)} %shard_map.101.refs_0_), channel_id=1, source_target_pairs={{0,17},{1,16},{2,19},{3,18},{4,21},{5,20},{6,23},{7,22},{8,25},{9,... | collective-permute-start | bytes 393224 | tf_op jit(solution)/shard_map/ppermute | solution.py:307
  74.0 3.5 %collective-permute-start.13 = (f32[128,128]{1,0:T(8,128)S(1)}, f32[128,128]{1,0:T(8,128)S(1)}, u32[]{:S(2)}, u32[]{:S(2)}) collective-permute-start(f32[128,128]{1,0:T(8,128)S(1)} %get-tuple-element.99), channel_id=1, source_target_pairs={{0,6},{1,7},{2,4},{3,5},{4,2},{5,3},{6,0},{7,1},{8,14},{9,15},{10,... | collective-permute-start | bytes 196616 | tf_op jit(solution)/shard_map/ppermute | solution.py:307
  78.4 2.2 %collective-permute-done.13.refs_3_ = f32[128,128]{1,0:T(8,128)S(1)} collective-permute-done((f32[128,128]{1,0:T(8,128)S(1)}, f32[128,128]{1,0:T(8,128)S(1)}, u32[]{:S(2)}, u32[]{:S(2)}) %collective-permute-start.13) | collective-permute-done | bytes 65568 | tf_op jit(solution)/shard_map/ppermute | solution.py:307
  80.6 3.1 %collective-permute-start.22 = (f32[128,128]{1,0:T(8,128)S(1)}, f32[128,128]{1,0:T(8,128)S(1)}, u32[]{:S(2)}, u32[]{:S(2)}) collective-permute-start(f32[128,128]{1,0:T(8,128)S(1)} %shard_map.97.refs_0_), channel_id=1, source_target_pairs={{0,6},{1,7},{2,4},{3,5},{4,2},{5,3},{6,0},{7,1},{8,14},{9,15},{10,... | collective-permute-start | bytes 196616 | tf_op jit(solution)/shard_map/ppermute | solution.py:307
  85.1 3.1 %collective-permute-start.28 = (f32[256,128]{1,0:T(8,128)S(1)}, f32[256,128]{1,0:T(8,128)S(1)}, u32[]{:S(2)}, u32[]{:S(2)}) collective-permute-start(f32[256,128]{1,0:T(8,128)S(1)} %shard_map.103.refs_0_), channel_id=1, source_target_pairs={{0,6},{1,7},{2,4},{3,5},{4,2},{5,3},{6,0},{7,1},{8,14},{9,15},{10,... | collective-permute-start | bytes 393224 | tf_op jit(solution)/shard_map/ppermute | solution.py:307
  89.1 1.8 %collective-permute-start.25 = (f32[512,128]{1,0:T(8,128)S(1)}, f32[512,128]{1,0:T(8,128)S(1)}, u32[]{:S(2)}, u32[]{:S(2)}) collective-permute-start(f32[512,128]{1,0:T(8,128)S(1)} %shard_map.102.refs_0_), channel_id=1, source_target_pairs={{0,17},{1,16},{2,19},{3,18},{4,21},{5,20},{6,23},{7,22},{8,25},{9,... | collective-permute-start | bytes 786440 | tf_op jit(solution)/shard_map/ppermute | solution.py:307
  90.9 1.8 %collective-permute-start.24 = (f32[512,128]{1,0:T(8,128)S(1)}, f32[512,128]{1,0:T(8,128)S(1)}, u32[]{:S(2)}, u32[]{:S(2)}) collective-permute-start(f32[512,128]{1,0:T(8,128)S(1)} %shard_map.102.refs_0_), channel_id=1, source_target_pairs={{0,1},{1,0},{2,3},{3,2},{4,5},{5,4},{6,7},{7,6},{8,9},{9,8},{10,11... | collective-permute-start | bytes 786440 | tf_op jit(solution)/shard_map/ppermute | solution.py:307
  92.7 2.5 %collective-permute-start.27 = (f32[256,128]{1,0:T(8,128)S(1)}, f32[256,128]{1,0:T(8,128)S(1)}, u32[]{:S(2)}, u32[]{:S(2)}) collective-permute-start(f32[256,128]{1,0:T(8,128)S(1)} %shard_map.103.refs_0_), channel_id=1, source_target_pairs={{0,4},{1,5},{2,6},{3,7},{4,0},{5,1},{6,2},{7,3},{8,12},{9,13},{10,... | collective-permute-start | bytes 393224 | tf_op jit(solution)/shard_map/ppermute | solution.py:307
  95.6 4.3 %collective-permute-done.27.refs_2_ = f32[256,128]{1,0:T(8,128)S(1)} collective-permute-done((f32[256,128]{1,0:T(8,128)S(1)}, f32[256,128]{1,0:T(8,128)S(1)}, u32[]{:S(2)}, u32[]{:S(2)}) %collective-permute-start.27) | collective-permute-done | bytes 131104 | tf_op jit(solution)/shard_map/ppermute | solution.py:307
  102.5 1.7 %collective-permute-done.33.refs_9_ = f32[256,128]{1,0:T(8,128)S(1)} collective-permute-done((f32[256,128]{1,0:T(8,128)S(1)}, f32[256,128]{1,0:T(8,128)S(1)}, u32[]{:S(2)}, u32[]{:S(2)}) %collective-permute-start.33) | collective-permute-done | bytes 131104 | tf_op jit(solution)/shard_map/ppermute | solution.py:307
  104.2 1.6 %shard_map.105 = (f32[4096,128]{1,0:T(8,128)}, f32[512,128]{1,0:T(8,128)}) custom-call(f32[512,128]{1,0:T(8,128)S(1)} %shard_map.102.refs_0_, f32[512,128]{1,0:T(8,128)S(1)} %collective-permute-done.23.refs_1_, f32[512,128]{1,0:T(8,128)S(1)} %collective-permute-done.24.refs_2_, f32[512,128]{1,0:T(8,128)S(1)} %collective-permute-done.25.refs_3_, ...), custom_call_target="tpu_custom_call" | custom-call | flops 1000000000 | tf_op jit(solution)/shard_map/pallas_call | solution.py:241
  (80 shorter events, 23.3 us)
Async XLA Ops:
  5.5 13.5 %collective-permute-start = (f32[272,256]{1,0:T(8,128)S(1)}, f32[272,256]{1,0:T(8,128)S(1)}, u32[]{:S(2)}, u32[]{:S(2)}) collective-permute-start(f32[272,256]{1,0:T(8,128)S(1)} %get-tuple-element.68.own_ref), channel_id=1, source_target_pairs={{0,1},{1,2},{2,3},{3,4},{4,5},{5,6},{6,7},{7,0},{8,9},{9,10},{10,1... | collective-permute-start | bytes 835592 | tf_op jit(solution)/shard_map/ppermute | solution.py:405
  8.5 17.0 %collective-permute-start.3 = (f32[272,256]{1,0:T(8,128)S(1)}, f32[272,256]{1,0:T(8,128)S(1)}, u32[]{:S(2)}, u32[]{:S(2)}) collective-permute-start(f32[272,256]{1,0:T(8,128)S(1)} %get-tuple-element.77.own_ref), channel_id=1, source_target_pairs={{0,1},{1,2},{2,3},{3,4},{4,5},{5,6},{6,7},{7,0},{8,9},{9,10},{10,1... | collective-permute-start | bytes 835592 | tf_op jit(solution)/shard_map/ppermute | solution.py:405
  19.6 8.9 %collective-permute-start.1 = (f32[272,256]{1,0:T(8,128)S(1)}, f32[272,256]{1,0:T(8,128)S(1)}, u32[]{:S(2)}, u32[]{:S(2)}) collective-permute-start(f32[272,256]{1,0:T(8,128)S(1)} %shard_map.88), channel_id=1, source_target_pairs={{0,2},{1,3},{2,4},{3,5},{4,6},{5,7},{6,0},{7,1},{8,10},{9,11},{10,... | collective-permute-start | bytes 835592 | tf_op jit(solution)/shard_map/ppermute | solution.py:405
  26.1 12.2 %collective-permute-start.4 = (f32[272,256]{1,0:T(8,128)S(1)}, f32[272,256]{1,0:T(8,128)S(1)}, u32[]{:S(2)}, u32[]{:S(2)}) collective-permute-start(f32[272,256]{1,0:T(8,128)S(1)} %shard_map.91), channel_id=1, source_target_pairs={{0,2},{1,3},{2,4},{3,5},{4,6},{5,7},{6,0},{7,1},{8,10},{9,11},{10,... | collective-permute-start | bytes 835592 | tf_op jit(solution)/shard_map/ppermute | solution.py:405
  33.6 10.5 %collective-permute-start.9 = (f32[272,256]{1,0:T(8,128)S(1)}, f32[272,256]{1,0:T(8,128)S(1)}, u32[]{:S(2)}, u32[]{:S(2)}) collective-permute-start(f32[272,256]{1,0:T(8,128)S(1)} %get-tuple-element.90.own_ref), channel_id=1, source_target_pairs={{0,7},{1,0},{2,1},{3,2},{4,3},{5,4},{6,5},{7,6},{8,15},{9,8},{10,9... | collective-permute-start | bytes 835592 | tf_op jit(solution)/shard_map/ppermute | solution.py:405
  43.4 10.3 %collective-permute-start.5 = (f32[1024,128]{1,0:T(8,128)S(1)}, f32[1024,128]{1,0:T(8,128)S(1)}, u32[]{:S(2)}, u32[]{:S(2)}) collective-permute-start(f32[1024,128]{1,0:T(8,128)S(1)} %get-tuple-element.85), channel_id=1, source_target_pairs={{0,8},{1,9},{2,10},{3,11},{4,12},{5,13},{6,14},{7,15},{8,0},{9,1},... | collective-permute-start | bytes 1572872 | tf_op jit(solution)/shard_map/ppermute | solution.py:307
  44.0 8.6 %collective-permute-start.10 = (f32[272,256]{1,0:T(8,128)S(1)}, f32[272,256]{1,0:T(8,128)S(1)}, u32[]{:S(2)}, u32[]{:S(2)}) collective-permute-start(f32[272,256]{1,0:T(8,128)S(1)} %get-tuple-element.91.own_ref), channel_id=1, source_target_pairs={{0,7},{1,0},{2,1},{3,2},{4,3},{5,4},{6,5},{7,6},{8,15},{9,8},{10,9... | collective-permute-start | bytes 835592 | tf_op jit(solution)/shard_map/ppermute | solution.py:405
  44.7 14.5 %collective-permute-start.14 = (f32[272,256]{1,0:T(8,128)S(1)}, f32[272,256]{1,0:T(8,128)S(1)}, u32[]{:S(2)}, u32[]{:S(2)}) collective-permute-start(f32[272,256]{1,0:T(8,128)S(1)} %shard_map.94), channel_id=1, source_target_pairs={{0,6},{1,7},{2,0},{3,1},{4,2},{5,3},{6,4},{7,5},{8,14},{9,15},{10,... | collective-permute-start | bytes 835592 | tf_op jit(solution)/shard_map/ppermute | solution.py:405
  53.2 9.6 %collective-permute-start.15 = (f32[272,256]{1,0:T(8,128)S(1)}, f32[272,256]{1,0:T(8,128)S(1)}, u32[]{:S(2)}, u32[]{:S(2)}) collective-permute-start(f32[272,256]{1,0:T(8,128)S(1)} %shard_map.95), channel_id=1, source_target_pairs={{0,6},{1,7},{2,0},{3,1},{4,2},{5,3},{6,4},{7,5},{8,14},{9,15},{10,... | collective-permute-start | bytes 835592 | tf_op jit(solution)/shard_map/ppermute | solution.py:405
  53.8 10.6 %collective-permute-start.6 = (f32[512,128]{1,0:T(8,128)S(1)}, f32[512,128]{1,0:T(8,128)S(1)}, u32[]{:S(2)}, u32[]{:S(2)}) collective-permute-start(f32[512,128]{1,0:T(8,128)S(1)} %get-tuple-element.87), channel_id=1, source_target_pairs={{0,16},{1,17},{2,18},{3,19},{4,20},{5,21},{6,22},{7,23},{8,24},{9,... | collective-permute-start | bytes 786440 | tf_op jit(solution)/shard_map/ppermute | solution.py:307
  55.4 13.3 %collective-permute-start.7 = (f32[512,128]{1,0:T(8,128)S(1)}, f32[512,128]{1,0:T(8,128)S(1)}, u32[]{:S(2)}, u32[]{:S(2)}) collective-permute-start(f32[512,128]{1,0:T(8,128)S(1)} %get-tuple-element.88), channel_id=1, source_target_pairs={{0,1},{1,0},{2,3},{3,2},{4,5},{5,4},{6,7},{7,6},{8,9},{9,8},{10,11... | collective-permute-start | bytes 786440 | tf_op jit(solution)/shard_map/ppermute | solution.py:307
  59.1 10.3 %collective-permute-start.8 = (f32[512,128]{1,0:T(8,128)S(1)}, f32[512,128]{1,0:T(8,128)S(1)}, u32[]{:S(2)}, u32[]{:S(2)}) collective-permute-start(f32[512,128]{1,0:T(8,128)S(1)} %get-tuple-element.89), channel_id=1, source_target_pairs={{0,17},{1,16},{2,19},{3,18},{4,21},{5,20},{6,23},{7,22},{8,25},{9,... | collective-permute-start | bytes 786440 | tf_op jit(solution)/shard_map/ppermute | solution.py:307
  69.6 11.0 %collective-permute-start.19 = (f32[256,128]{1,0:T(8,128)S(1)}, f32[256,128]{1,0:T(8,128)S(1)}, u32[]{:S(2)}, u32[]{:S(2)}) collective-permute-start(f32[256,128]{1,0:T(8,128)S(1)} %shard_map.101.refs_0_), channel_id=1, source_target_pairs={{0,17},{1,16},{2,19},{3,18},{4,21},{5,20},{6,23},{7,22},{8,25},{9,... | collective-permute-start | bytes 393224 | tf_op jit(solution)/shard_map/ppermute | solution.py:307
  71.4 9.2 %collective-permute-start.18 = (f32[256,128]{1,0:T(8,128)S(1)}, f32[256,128]{1,0:T(8,128)S(1)}, u32[]{:S(2)}, u32[]{:S(2)}) collective-permute-start(f32[256,128]{1,0:T(8,128)S(1)} %shard_map.101.refs_0_), channel_id=1, source_target_pairs={{0,1},{1,0},{2,3},{3,2},{4,5},{5,4},{6,7},{7,6},{8,9},{9,8},{10,11... | collective-permute-start | bytes 393224 | tf_op jit(solution)/shard_map/ppermute | solution.py:307
  72.6 8.0 %collective-permute-start.17 = (f32[256,128]{1,0:T(8,128)S(1)}, f32[256,128]{1,0:T(8,128)S(1)}, u32[]{:S(2)}, u32[]{:S(2)}) collective-permute-start(f32[256,128]{1,0:T(8,128)S(1)} %shard_map.101.refs_0_), channel_id=1, source_target_pairs={{0,16},{1,17},{2,18},{3,19},{4,20},{5,21},{6,22},{7,23},{8,24},{9,... | collective-permute-start | bytes 393224 | tf_op jit(solution)/shard_map/ppermute | solution.py:307
  74.0 6.5 %collective-permute-start.13 = (f32[128,128]{1,0:T(8,128)S(1)}, f32[128,128]{1,0:T(8,128)S(1)}, u32[]{:S(2)}, u32[]{:S(2)}) collective-permute-start(f32[128,128]{1,0:T(8,128)S(1)} %get-tuple-element.99), channel_id=1, source_target_pairs={{0,6},{1,7},{2,4},{3,5},{4,2},{5,3},{6,0},{7,1},{8,14},{9,15},{10,... | collective-permute-start | bytes 196616 | tf_op jit(solution)/shard_map/ppermute | solution.py:307
  80.6 7.6 %collective-permute-start.22 = (f32[128,128]{1,0:T(8,128)S(1)}, f32[128,128]{1,0:T(8,128)S(1)}, u32[]{:S(2)}, u32[]{:S(2)}) collective-permute-start(f32[128,128]{1,0:T(8,128)S(1)} %shard_map.97.refs_0_), channel_id=1, source_target_pairs={{0,6},{1,7},{2,4},{3,5},{4,2},{5,3},{6,0},{7,1},{8,14},{9,15},{10,... | collective-permute-start | bytes 196616 | tf_op jit(solution)/shard_map/ppermute | solution.py:307
  83.7 5.3 %collective-permute-start.21 = (f32[128,128]{1,0:T(8,128)S(1)}, f32[128,128]{1,0:T(8,128)S(1)}, u32[]{:S(2)}, u32[]{:S(2)}) collective-permute-start(f32[128,128]{1,0:T(8,128)S(1)} %shard_map.97.refs_0_), channel_id=1, source_target_pairs={{0,4},{1,5},{2,6},{3,7},{4,0},{5,1},{6,2},{7,3},{8,12},{9,13},{10,... | collective-permute-start | bytes 196616 | tf_op jit(solution)/shard_map/ppermute | solution.py:307
  85.1 10.0 %collective-permute-start.28 = (f32[256,128]{1,0:T(8,128)S(1)}, f32[256,128]{1,0:T(8,128)S(1)}, u32[]{:S(2)}, u32[]{:S(2)}) collective-permute-start(f32[256,128]{1,0:T(8,128)S(1)} %shard_map.103.refs_0_), channel_id=1, source_target_pairs={{0,6},{1,7},{2,4},{3,5},{4,2},{5,3},{6,0},{7,1},{8,14},{9,15},{10,... | collective-permute-start | bytes 393224 | tf_op jit(solution)/shard_map/ppermute | solution.py:307
  89.1 12.2 %collective-permute-start.25 = (f32[512,128]{1,0:T(8,128)S(1)}, f32[512,128]{1,0:T(8,128)S(1)}, u32[]{:S(2)}, u32[]{:S(2)}) collective-permute-start(f32[512,128]{1,0:T(8,128)S(1)} %shard_map.102.refs_0_), channel_id=1, source_target_pairs={{0,17},{1,16},{2,19},{3,18},{4,21},{5,20},{6,23},{7,22},{8,25},{9,... | collective-permute-start | bytes 786440 | tf_op jit(solution)/shard_map/ppermute | solution.py:307
  90.9 10.4 %collective-permute-start.24 = (f32[512,128]{1,0:T(8,128)S(1)}, f32[512,128]{1,0:T(8,128)S(1)}, u32[]{:S(2)}, u32[]{:S(2)}) collective-permute-start(f32[512,128]{1,0:T(8,128)S(1)} %shard_map.102.refs_0_), channel_id=1, source_target_pairs={{0,1},{1,0},{2,3},{3,2},{4,5},{5,4},{6,7},{7,6},{8,9},{9,8},{10,11... | collective-permute-start | bytes 786440 | tf_op jit(solution)/shard_map/ppermute | solution.py:307
  92.6 8.6 %collective-permute-start.23 = (f32[512,128]{1,0:T(8,128)S(1)}, f32[512,128]{1,0:T(8,128)S(1)}, u32[]{:S(2)}, u32[]{:S(2)}) collective-permute-start(f32[512,128]{1,0:T(8,128)S(1)} %shard_map.102.refs_0_), channel_id=1, source_target_pairs={{0,16},{1,17},{2,18},{3,19},{4,20},{5,21},{6,22},{7,23},{8,24},{9,... | collective-permute-start | bytes 786440 | tf_op jit(solution)/shard_map/ppermute | solution.py:307
  92.7 7.3 %collective-permute-start.27 = (f32[256,128]{1,0:T(8,128)S(1)}, f32[256,128]{1,0:T(8,128)S(1)}, u32[]{:S(2)}, u32[]{:S(2)}) collective-permute-start(f32[256,128]{1,0:T(8,128)S(1)} %shard_map.103.refs_0_), channel_id=1, source_target_pairs={{0,4},{1,5},{2,6},{3,7},{4,0},{5,1},{6,2},{7,3},{8,12},{9,13},{10,... | collective-permute-start | bytes 393224 | tf_op jit(solution)/shard_map/ppermute | solution.py:307
  95.1 6.1 %collective-permute-start.26 = (f32[256,128]{1,0:T(8,128)S(1)}, f32[256,128]{1,0:T(8,128)S(1)}, u32[]{:S(2)}, u32[]{:S(2)}) collective-permute-start(f32[256,128]{1,0:T(8,128)S(1)} %shard_map.103.refs_0_), channel_id=1, source_target_pairs={{0,2},{1,3},{2,0},{3,1},{4,6},{5,7},{6,4},{7,5},{8,10},{9,11},{10,... | collective-permute-start | bytes 393224 | tf_op jit(solution)/shard_map/ppermute | solution.py:307
  (17 other events, 130.7 us)

commit v8 on v7

--- a/solution.py
+++ b/solution.py
@@ -76,7 +76,8 @@
                 state = dot(vals, feat[rows], TN)
                 norm = jnp.sum(feat[rows].astype(F32), axis=0, keepdims=True)
                 both = jnp.concatenate([state, tall_rows(norm)], axis=0)
-                block_ref[i, c] = both
+                if c < block_ref.shape[1]:
+                    block_ref[i, c] = both
                 part = flag(starts[c] == starts[count - 1]) * both
                 tail = part if tail is None else tail + part
             tall = tail.shape[0]
@@ -391,7 +392,7 @@
         weights = [weights[i : i + stack].reshape(rows, hd) for i in range(0, hk, stack)]
         out = local_call(
             functools.partial(key_kernel, count, parts, hd),
-            [array((hk, rows, feats), BF16), array((hk, count, tall, feats), F32)]
+            [array((hk, rows, feats), BF16), array((hk, max(count - 1, 1), tall, feats), F32)]
             + [rows_of((hi - lo) * tall, feats) for lo, hi in parts],
             3.0,
             jnp.concatenate([k2, v2] + weights, axis=1),

time: 106 us -> 106 us (level)
  transfers between devices with their start and end apart: 34 -> 34, of which waited for: 12 -> 12; matrix products, arithmetic and copies ran while one was open for 0% -> 0% of each run, Pallas kernels for 20% -> 21%
where the time goes in v8:
time: 106 us
  starting transfers between devices  41.1 us (39%)
  waiting for transfers between devices  35.7 us (34%)
  Pallas kernels  25.7 us (24%)
  local copies, waits for them, and re-layouts  1.56 us (1%)
  other arithmetic  1.08 us (1%)
    ppermute x26, starting transfers between devices, send(): return lax.ppermute(x, ('dp', 'seq'), perm)  29.1 us
    pallas_call x20, Pallas kernels, local_call(): pl.pallas_call(body, out_shape=out_shape, in_specs=[SMEM] * len(first) +...  25.7 us
    ppermute x8, waiting for transfers between devices, shift(): return lax.ppermute(own, 'seq', ring)  19.4 us
    ppermute x26, waiting for transfers between devices, send(): return lax.ppermute(x, ('dp', 'seq'), perm)  16.3 us
    ppermute x8, starting transfers between devices, shift(): return lax.ppermute(own, 'seq', ring)  12 us
  transfers between devices with their start and end apart: 34, of which 12 were waited for; matrix products, arithmetic and copies ran while one was open for 0% of the time, Pallas kernels for 21%

profile of v8, /device:TPU:0, one launch (start us, length us, event | category | flops | bytes accessed | tf_op | source)
XLA Modules:
  0.0 106.1 jit_solution(14067137344524463937)
XLA Ops:
  3.3 2.2 %shard_map.86 = (bf16[4,256,256]{2,1,0:T(8,128)(2,1)S(1)}, f32[4,1,136,256]{3,2,1,0:T(8,128)S(1)}, f32[272,256]{1,0:T(8,128)S(1)}, f32[272,256]{1,0:T(8,128)S(1)}) custom-call(s32[1,8]{1,0:T(1,128)S(1)} %copy-done.6, bf16[256,1280]{1,0:T(8,128)(2,1)S(1)} %pad_maximum_fusion.packed_ref), custom_call_target="tpu_custom_call" | custom-call | flops 3000000000 | tf_op jit(solution)/shard_map/pallas_call | solution.py:242
  5.5 3.0 %collective-permute-start = (f32[272,256]{1,0:T(8,128)S(1)}, f32[272,256]{1,0:T(8,128)S(1)}, u32[]{:S(2)}, u32[]{:S(2)}) collective-permute-start(f32[272,256]{1,0:T(8,128)S(1)} %get-tuple-element.68.own_ref), channel_id=1, source_target_pairs={{0,1},{1,2},{2,3},{3,4},{4,5},{5,6},{6,7},{7,0},{8,9},{9,10},{10,1... | collective-permute-start | bytes 835592 | tf_op jit(solution)/shard_map/ppermute | solution.py:406
  10.0 9.0 %collective-permute-done.came_ref.refs_11_ = f32[272,256]{1,0:T(8,128)S(1)} collective-permute-done((f32[272,256]{1,0:T(8,128)S(1)}, f32[272,256]{1,0:T(8,128)S(1)}, u32[]{:S(2)}, u32[]{:S(2)}) %collective-permute-start) | collective-permute-done | bytes 278560 | tf_op jit(solution)/shard_map/ppermute | solution.py:406
  19.7 2.9 %shard_map.90 = (f32[2,2,128,1024]{3,2,1,0:T(8,128)S(1)}, f32[2,2,128,1024]{3,2,1,0:T(8,128)S(1)}, bf16[2,2,256,1024]{3,2,1,0:T(8,128)(2,1)S(1)}, f32[2,2,128,10...) custom-call(bf16[256,4096]{1,0:T(8,128)(2,1)S(1)} %bitcast.10, ...), custom_call_target="tpu_custom_call" | custom-call | flops 1500000000 | tf_op jit(solution)/shard_map/pallas_call | solution.py:242
  22.6 2.9 %shard_map.87 = (f32[2,2,128,1024]{3,2,1,0:T(8,128)S(1)}, f32[2,2,128,1024]{3,2,1,0:T(8,128)S(1)}, bf16[2,2,256,1024]{3,2,1,0:T(8,128)(2,1)S(1)}, f32[2,2,128,10...) custom-call(bf16[256,4096]{1,0:T(8,128)(2,1)S(1)} %bitcast.11, ...), custom_call_target="tpu_custom_call" | custom-call | flops 1500000000 | tf_op jit(solution)/shard_map/pallas_call | solution.py:242
  26.2 1.6 %collective-permute-start.4 = (f32[272,256]{1,0:T(8,128)S(1)}, f32[272,256]{1,0:T(8,128)S(1)}, u32[]{:S(2)}, u32[]{:S(2)}) collective-permute-start(f32[272,256]{1,0:T(8,128)S(1)} %shard_map.91), channel_id=1, source_target_pairs={{0,2},{1,3},{2,4},{3,5},{4,6},{5,7},{6,0},{7,1},{8,10},{9,11},{10,... | collective-permute-start | bytes 835592 | tf_op jit(solution)/shard_map/ppermute | solution.py:406
  28.5 5.5 %shard_map.89 = (f32[1024,128]{1,0:T(8,128)S(1)}, f32[1024,128]{1,0:T(8,128)S(1)}, f32[272,256]{1,0:T(8,128)S(1)}, f32[2,2,136,256]{3,2,1,0:T(8,128)S(1)}, f32[2,2,128,256]{3,2,1,0:T(8,128)S(1)}) custom-call(s32[1,8]{1,0:T(1,128)S(1)} %copy-done.6, bf16[256,4096]{1,0:T(8,128)(2,1)S(1)} %bitcast.12, bf16[256,512]{1,0:T(8,128)(2,1)S(1)} %bitcast.17, ...), custom_call_target="tpu_custom_call" | custom-call | flops 6000000000 | tf_op jit(solution)/shard_map/pallas_call | solution.py:242
  34.0 4.7 %collective-permute-start.9 = (f32[272,256]{1,0:T(8,128)S(1)}, f32[272,256]{1,0:T(8,128)S(1)}, u32[]{:S(2)}, u32[]{:S(2)}) collective-permute-start(f32[272,256]{1,0:T(8,128)S(1)} %get-tuple-element.90.own_ref), channel_id=1, source_target_pairs={{0,7},{1,0},{2,1},{3,2},{4,3},{5,4},{6,5},{7,6},{8,15},{9,8},{10,9... | collective-permute-start | bytes 835592 | tf_op jit(solution)/shard_map/ppermute | solution.py:406
  38.7 5.1 %shard_map.92 = (f32[1024,128]{1,0:T(8,128)S(1)}, f32[1024,128]{1,0:T(8,128)S(1)}, f32[272,256]{1,0:T(8,128)S(1)}, f32[2,2,136,256]{3,2,1,0:T(8,128)S(1)}, f32[2,2,128,256]{3,2,1,0:T(8,128)S(1)}) custom-call(s32[1,8]{1,0:T(1,128)S(1)} %copy-done.6, bf16[256,4096]{1,0:T(8,128)(2,1)S(1)} %bitcast.13, bf16[256,512]{1,0:T(8,128)(2,1)S(1)} %bitcast.18, ...), custom_call_target="tpu_custom_call" | custom-call | flops 6000000000 | tf_op jit(solution)/shard_map/pallas_call | solution.py:242
  45.6 7.4 %collective-permute-done.10.came_ref.refs_6_ = f32[272,256]{1,0:T(8,128)S(1)} collective-permute-done((f32[272,256]{1,0:T(8,128)S(1)}, f32[272,256]{1,0:T(8,128)S(1)}, u32[]{:S(2)}, u32[]{:S(2)}) %collective-permute-start.10) | collective-permute-done | bytes 278560 | tf_op jit(solution)/shard_map/ppermute | solution.py:406
  55.7 3.7 %collective-permute-start.7 = (f32[512,128]{1,0:T(8,128)S(1)}, f32[512,128]{1,0:T(8,128)S(1)}, u32[]{:S(2)}, u32[]{:S(2)}) collective-permute-start(f32[512,128]{1,0:T(8,128)S(1)} %get-tuple-element.88), channel_id=1, source_target_pairs={{0,1},{1,0},{2,3},{3,2},{4,5},{5,4},{6,7},{7,6},{8,9},{9,8},{10,11... | collective-permute-start | bytes 786440 | tf_op jit(solution)/shard_map/ppermute | solution.py:308
  61.0 2.2 %collective-permute-done.15.refs_7_ = f32[272,256]{1,0:T(8,128)S(1)} collective-permute-done((f32[272,256]{1,0:T(8,128)S(1)}, f32[272,256]{1,0:T(8,128)S(1)}, u32[]{:S(2)}, u32[]{:S(2)}) %collective-permute-start.15) | collective-permute-done | bytes 278560 | tf_op jit(solution)/shard_map/ppermute | solution.py:406
  64.8 4.3 %collective-permute-done.7.refs_2_ = f32[512,128]{1,0:T(8,128)S(1)} collective-permute-done((f32[512,128]{1,0:T(8,128)S(1)}, f32[512,128]{1,0:T(8,128)S(1)}, u32[]{:S(2)}, u32[]{:S(2)}) %collective-permute-start.7) | collective-permute-done | bytes 262176 | tf_op jit(solution)/shard_map/ppermute | solution.py:308
  70.0 1.8 %collective-permute-start.19 = (f32[256,128]{1,0:T(8,128)S(1)}, f32[256,128]{1,0:T(8,128)S(1)}, u32[]{:S(2)}, u32[]{:S(2)}) collective-permute-start(f32[256,128]{1,0:T(8,128)S(1)} %shard_map.101.refs_0_), channel_id=1, source_target_pairs={{0,17},{1,16},{2,19},{3,18},{4,21},{5,20},{6,23},{7,22},{8,25},{9,... | collective-permute-start | bytes 393224 | tf_op jit(solution)/shard_map/ppermute | solution.py:308
  74.4 3.5 %collective-permute-start.13 = (f32[128,128]{1,0:T(8,128)S(1)}, f32[128,128]{1,0:T(8,128)S(1)}, u32[]{:S(2)}, u32[]{:S(2)}) collective-permute-start(f32[128,128]{1,0:T(8,128)S(1)} %get-tuple-element.99), channel_id=1, source_target_pairs={{0,6},{1,7},{2,4},{3,5},{4,2},{5,3},{6,0},{7,1},{8,14},{9,15},{10,... | collective-permute-start | bytes 196616 | tf_op jit(solution)/shard_map/ppermute | solution.py:308
  78.7 2.2 %collective-permute-done.13.refs_3_ = f32[128,128]{1,0:T(8,128)S(1)} collective-permute-done((f32[128,128]{1,0:T(8,128)S(1)}, f32[128,128]{1,0:T(8,128)S(1)}, u32[]{:S(2)}, u32[]{:S(2)}) %collective-permute-start.13) | collective-permute-done | bytes 65568 | tf_op jit(solution)/shard_map/ppermute | solution.py:308
  81.0 3.1 %collective-permute-start.22 = (f32[128,128]{1,0:T(8,128)S(1)}, f32[128,128]{1,0:T(8,128)S(1)}, u32[]{:S(2)}, u32[]{:S(2)}) collective-permute-start(f32[128,128]{1,0:T(8,128)S(1)} %shard_map.97.refs_0_), channel_id=1, source_target_pairs={{0,6},{1,7},{2,4},{3,5},{4,2},{5,3},{6,0},{7,1},{8,14},{9,15},{10,... | collective-permute-start | bytes 196616 | tf_op jit(solution)/shard_map/ppermute | solution.py:308
  85.5 3.1 %collective-permute-start.28 = (f32[256,128]{1,0:T(8,128)S(1)}, f32[256,128]{1,0:T(8,128)S(1)}, u32[]{:S(2)}, u32[]{:S(2)}) collective-permute-start(f32[256,128]{1,0:T(8,128)S(1)} %shard_map.103.refs_0_), channel_id=1, source_target_pairs={{0,6},{1,7},{2,4},{3,5},{4,2},{5,3},{6,0},{7,1},{8,14},{9,15},{10,... | collective-permute-start | bytes 393224 | tf_op jit(solution)/shard_map/ppermute | solution.py:308
  89.5 1.8 %collective-permute-start.25 = (f32[512,128]{1,0:T(8,128)S(1)}, f32[512,128]{1,0:T(8,128)S(1)}, u32[]{:S(2)}, u32[]{:S(2)}) collective-permute-start(f32[512,128]{1,0:T(8,128)S(1)} %shard_map.102.refs_0_), channel_id=1, source_target_pairs={{0,17},{1,16},{2,19},{3,18},{4,21},{5,20},{6,23},{7,22},{8,25},{9,... | collective-permute-start | bytes 786440 | tf_op jit(solution)/shard_map/ppermute | solution.py:308
  91.3 2.6 %collective-permute-start.24 = (f32[512,128]{1,0:T(8,128)S(1)}, f32[512,128]{1,0:T(8,128)S(1)}, u32[]{:S(2)}, u32[]{:S(2)}) collective-permute-start(f32[512,128]{1,0:T(8,128)S(1)} %shard_map.102.refs_0_), channel_id=1, source_target_pairs={{0,1},{1,0},{2,3},{3,2},{4,5},{5,4},{6,7},{7,6},{8,9},{9,8},{10,11... | collective-permute-start | bytes 786440 | tf_op jit(solution)/shard_map/ppermute | solution.py:308
  93.8 1.7 %collective-permute-start.27 = (f32[256,128]{1,0:T(8,128)S(1)}, f32[256,128]{1,0:T(8,128)S(1)}, u32[]{:S(2)}, u32[]{:S(2)}) collective-permute-start(f32[256,128]{1,0:T(8,128)S(1)} %shard_map.103.refs_0_), channel_id=1, source_target_pairs={{0,4},{1,5},{2,6},{3,7},{4,0},{5,1},{6,2},{7,3},{8,12},{9,13},{10,... | collective-permute-start | bytes 393224 | tf_op jit(solution)/shard_map/ppermute | solution.py:308
  96.0 4.3 %collective-permute-done.27.refs_2_ = f32[256,128]{1,0:T(8,128)S(1)} collective-permute-done((f32[256,128]{1,0:T(8,128)S(1)}, f32[256,128]{1,0:T(8,128)S(1)}, u32[]{:S(2)}, u32[]{:S(2)}) %collective-permute-start.27) | collective-permute-done | bytes 131104 | tf_op jit(solution)/shard_map/ppermute | solution.py:308
  102.8 1.7 %collective-permute-done.33.refs_9_ = f32[256,128]{1,0:T(8,128)S(1)} collective-permute-done((f32[256,128]{1,0:T(8,128)S(1)}, f32[256,128]{1,0:T(8,128)S(1)}, u32[]{:S(2)}, u32[]{:S(2)}) %collective-permute-start.33) | collective-permute-done | bytes 131104 | tf_op jit(solution)/shard_map/ppermute | solution.py:308
  104.6 1.6 %shard_map.105 = (f32[4096,128]{1,0:T(8,128)}, f32[512,128]{1,0:T(8,128)}) custom-call(f32[512,128]{1,0:T(8,128)S(1)} %shard_map.102.refs_0_, f32[512,128]{1,0:T(8,128)S(1)} %collective-permute-done.23.refs_1_, f32[512,128]{1,0:T(8,128)S(1)} %collective-permute-done.24.refs_2_, f32[512,128]{1,0:T(8,128)S(1)} %collective-permute-done.25.refs_3_, ...), custom_call_target="tpu_custom_call" | custom-call | flops 1000000000 | tf_op jit(solution)/shard_map/pallas_call | solution.py:242
  (80 shorter events, 23.3 us)
Async XLA Ops:
  5.5 13.5 %collective-permute-start = (f32[272,256]{1,0:T(8,128)S(1)}, f32[272,256]{1,0:T(8,128)S(1)}, u32[]{:S(2)}, u32[]{:S(2)}) collective-permute-start(f32[272,256]{1,0:T(8,128)S(1)} %get-tuple-element.68.own_ref), channel_id=1, source_target_pairs={{0,1},{1,2},{2,3},{3,4},{4,5},{5,6},{6,7},{7,0},{8,9},{9,10},{10,1... | collective-permute-start | bytes 835592 | tf_op jit(solution)/shard_map/ppermute | solution.py:406
  8.5 17.1 %collective-permute-start.3 = (f32[272,256]{1,0:T(8,128)S(1)}, f32[272,256]{1,0:T(8,128)S(1)}, u32[]{:S(2)}, u32[]{:S(2)}) collective-permute-start(f32[272,256]{1,0:T(8,128)S(1)} %get-tuple-element.77.own_ref), channel_id=1, source_target_pairs={{0,1},{1,2},{2,3},{3,4},{4,5},{5,6},{6,7},{7,0},{8,9},{9,10},{10,1... | collective-permute-start | bytes 835592 | tf_op jit(solution)/shard_map/ppermute | solution.py:406
  19.6 8.9 %collective-permute-start.1 = (f32[272,256]{1,0:T(8,128)S(1)}, f32[272,256]{1,0:T(8,128)S(1)}, u32[]{:S(2)}, u32[]{:S(2)}) collective-permute-start(f32[272,256]{1,0:T(8,128)S(1)} %shard_map.88), channel_id=1, source_target_pairs={{0,2},{1,3},{2,4},{3,5},{4,6},{5,7},{6,0},{7,1},{8,10},{9,11},{10,... | collective-permute-start | bytes 835592 | tf_op jit(solution)/shard_map/ppermute | solution.py:406
  26.2 12.5 %collective-permute-start.4 = (f32[272,256]{1,0:T(8,128)S(1)}, f32[272,256]{1,0:T(8,128)S(1)}, u32[]{:S(2)}, u32[]{:S(2)}) collective-permute-start(f32[272,256]{1,0:T(8,128)S(1)} %shard_map.91), channel_id=1, source_target_pairs={{0,2},{1,3},{2,4},{3,5},{4,6},{5,7},{6,0},{7,1},{8,10},{9,11},{10,... | collective-permute-start | bytes 835592 | tf_op jit(solution)/shard_map/ppermute | solution.py:406
  34.0 10.5 %collective-permute-start.9 = (f32[272,256]{1,0:T(8,128)S(1)}, f32[272,256]{1,0:T(8,128)S(1)}, u32[]{:S(2)}, u32[]{:S(2)}) collective-permute-start(f32[272,256]{1,0:T(8,128)S(1)} %get-tuple-element.90.own_ref), channel_id=1, source_target_pairs={{0,7},{1,0},{2,1},{3,2},{4,3},{5,4},{6,5},{7,6},{8,15},{9,8},{10,9... | collective-permute-start | bytes 835592 | tf_op jit(solution)/shard_map/ppermute | solution.py:406
  43.8 10.3 %collective-permute-start.5 = (f32[1024,128]{1,0:T(8,128)S(1)}, f32[1024,128]{1,0:T(8,128)S(1)}, u32[]{:S(2)}, u32[]{:S(2)}) collective-permute-start(f32[1024,128]{1,0:T(8,128)S(1)} %get-tuple-element.85), channel_id=1, source_target_pairs={{0,8},{1,9},{2,10},{3,11},{4,12},{5,13},{6,14},{7,15},{8,0},{9,1},... | collective-permute-start | bytes 1572872 | tf_op jit(solution)/shard_map/ppermute | solution.py:308
  44.3 8.6 %collective-permute-start.10 = (f32[272,256]{1,0:T(8,128)S(1)}, f32[272,256]{1,0:T(8,128)S(1)}, u32[]{:S(2)}, u32[]{:S(2)}) collective-permute-start(f32[272,256]{1,0:T(8,128)S(1)} %get-tuple-element.91.own_ref), channel_id=1, source_target_pairs={{0,7},{1,0},{2,1},{3,2},{4,3},{5,4},{6,5},{7,6},{8,15},{9,8},{10,9... | collective-permute-start | bytes 835592 | tf_op jit(solution)/shard_map/ppermute | solution.py:406
  45.0 14.4 %collective-permute-start.14 = (f32[272,256]{1,0:T(8,128)S(1)}, f32[272,256]{1,0:T(8,128)S(1)}, u32[]{:S(2)}, u32[]{:S(2)}) collective-permute-start(f32[272,256]{1,0:T(8,128)S(1)} %shard_map.94), channel_id=1, source_target_pairs={{0,6},{1,7},{2,0},{3,1},{4,2},{5,3},{6,4},{7,5},{8,14},{9,15},{10,... | collective-permute-start | bytes 835592 | tf_op jit(solution)/shard_map/ppermute | solution.py:406
  53.6 9.6 %collective-permute-start.15 = (f32[272,256]{1,0:T(8,128)S(1)}, f32[272,256]{1,0:T(8,128)S(1)}, u32[]{:S(2)}, u32[]{:S(2)}) collective-permute-start(f32[272,256]{1,0:T(8,128)S(1)} %shard_map.95), channel_id=1, source_target_pairs={{0,6},{1,7},{2,0},{3,1},{4,2},{5,3},{6,4},{7,5},{8,14},{9,15},{10,... | collective-permute-start | bytes 835592 | tf_op jit(solution)/shard_map/ppermute | solution.py:406
  54.2 10.6 %collective-permute-start.6 = (f32[512,128]{1,0:T(8,128)S(1)}, f32[512,128]{1,0:T(8,128)S(1)}, u32[]{:S(2)}, u32[]{:S(2)}) collective-permute-start(f32[512,128]{1,0:T(8,128)S(1)} %get-tuple-element.87), channel_id=1, source_target_pairs={{0,16},{1,17},{2,18},{3,19},{4,20},{5,21},{6,22},{7,23},{8,24},{9,... | collective-permute-start | bytes 786440 | tf_op jit(solution)/shard_map/ppermute | solution.py:308
  55.7 13.3 %collective-permute-start.7 = (f32[512,128]{1,0:T(8,128)S(1)}, f32[512,128]{1,0:T(8,128)S(1)}, u32[]{:S(2)}, u32[]{:S(2)}) collective-permute-start(f32[512,128]{1,0:T(8,128)S(1)} %get-tuple-element.88), channel_id=1, source_target_pairs={{0,1},{1,0},{2,3},{3,2},{4,5},{5,4},{6,7},{7,6},{8,9},{9,8},{10,11... | collective-permute-start | bytes 786440 | tf_op jit(solution)/shard_map/ppermute | solution.py:308
  59.5 10.3 %collective-permute-start.8 = (f32[512,128]{1,0:T(8,128)S(1)}, f32[512,128]{1,0:T(8,128)S(1)}, u32[]{:S(2)}, u32[]{:S(2)}) collective-permute-start(f32[512,128]{1,0:T(8,128)S(1)} %get-tuple-element.89), channel_id=1, source_target_pairs={{0,17},{1,16},{2,19},{3,18},{4,21},{5,20},{6,23},{7,22},{8,25},{9,... | collective-permute-start | bytes 786440 | tf_op jit(solution)/shard_map/ppermute | solution.py:308
  70.0 11.0 %collective-permute-start.19 = (f32[256,128]{1,0:T(8,128)S(1)}, f32[256,128]{1,0:T(8,128)S(1)}, u32[]{:S(2)}, u32[]{:S(2)}) collective-permute-start(f32[256,128]{1,0:T(8,128)S(1)} %shard_map.101.refs_0_), channel_id=1, source_target_pairs={{0,17},{1,16},{2,19},{3,18},{4,21},{5,20},{6,23},{7,22},{8,25},{9,... | collective-permute-start | bytes 393224 | tf_op jit(solution)/shard_map/ppermute | solution.py:308
  71.8 9.2 %collective-permute-start.18 = (f32[256,128]{1,0:T(8,128)S(1)}, f32[256,128]{1,0:T(8,128)S(1)}, u32[]{:S(2)}, u32[]{:S(2)}) collective-permute-start(f32[256,128]{1,0:T(8,128)S(1)} %shard_map.101.refs_0_), channel_id=1, source_target_pairs={{0,1},{1,0},{2,3},{3,2},{4,5},{5,4},{6,7},{7,6},{8,9},{9,8},{10,11... | collective-permute-start | bytes 393224 | tf_op jit(solution)/shard_map/ppermute | solution.py:308
  73.0 8.0 %collective-permute-start.17 = (f32[256,128]{1,0:T(8,128)S(1)}, f32[256,128]{1,0:T(8,128)S(1)}, u32[]{:S(2)}, u32[]{:S(2)}) collective-permute-start(f32[256,128]{1,0:T(8,128)S(1)} %shard_map.101.refs_0_), channel_id=1, source_target_pairs={{0,16},{1,17},{2,18},{3,19},{4,20},{5,21},{6,22},{7,23},{8,24},{9,... | collective-permute-start | bytes 393224 | tf_op jit(solution)/shard_map/ppermute | solution.py:308
  74.4 6.5 %collective-permute-start.13 = (f32[128,128]{1,0:T(8,128)S(1)}, f32[128,128]{1,0:T(8,128)S(1)}, u32[]{:S(2)}, u32[]{:S(2)}) collective-permute-start(f32[128,128]{1,0:T(8,128)S(1)} %get-tuple-element.99), channel_id=1, source_target_pairs={{0,6},{1,7},{2,4},{3,5},{4,2},{5,3},{6,0},{7,1},{8,14},{9,15},{10,... | collective-permute-start | bytes 196616 | tf_op jit(solution)/shard_map/ppermute | solution.py:308
  81.0 7.6 %collective-permute-start.22 = (f32[128,128]{1,0:T(8,128)S(1)}, f32[128,128]{1,0:T(8,128)S(1)}, u32[]{:S(2)}, u32[]{:S(2)}) collective-permute-start(f32[128,128]{1,0:T(8,128)S(1)} %shard_map.97.refs_0_), channel_id=1, source_target_pairs={{0,6},{1,7},{2,4},{3,5},{4,2},{5,3},{6,0},{7,1},{8,14},{9,15},{10,... | collective-permute-start | bytes 196616 | tf_op jit(solution)/shard_map/ppermute | solution.py:308
  84.1 5.3 %collective-permute-start.21 = (f32[128,128]{1,0:T(8,128)S(1)}, f32[128,128]{1,0:T(8,128)S(1)}, u32[]{:S(2)}, u32[]{:S(2)}) collective-permute-start(f32[128,128]{1,0:T(8,128)S(1)} %shard_map.97.refs_0_), channel_id=1, source_target_pairs={{0,4},{1,5},{2,6},{3,7},{4,0},{5,1},{6,2},{7,3},{8,12},{9,13},{10,... | collective-permute-start | bytes 196616 | tf_op jit(solution)/shard_map/ppermute | solution.py:308
  85.5 10.0 %collective-permute-start.28 = (f32[256,128]{1,0:T(8,128)S(1)}, f32[256,128]{1,0:T(8,128)S(1)}, u32[]{:S(2)}, u32[]{:S(2)}) collective-permute-start(f32[256,128]{1,0:T(8,128)S(1)} %shard_map.103.refs_0_), channel_id=1, source_target_pairs={{0,6},{1,7},{2,4},{3,5},{4,2},{5,3},{6,0},{7,1},{8,14},{9,15},{10,... | collective-permute-start | bytes 393224 | tf_op jit(solution)/shard_map/ppermute | solution.py:308
  89.5 12.1 %collective-permute-start.25 = (f32[512,128]{1,0:T(8,128)S(1)}, f32[512,128]{1,0:T(8,128)S(1)}, u32[]{:S(2)}, u32[]{:S(2)}) collective-permute-start(f32[512,128]{1,0:T(8,128)S(1)} %shard_map.102.refs_0_), channel_id=1, source_target_pairs={{0,17},{1,16},{2,19},{3,18},{4,21},{5,20},{6,23},{7,22},{8,25},{9,... | collective-permute-start | bytes 786440 | tf_op jit(solution)/shard_map/ppermute | solution.py:308
  91.3 10.3 %collective-permute-start.24 = (f32[512,128]{1,0:T(8,128)S(1)}, f32[512,128]{1,0:T(8,128)S(1)}, u32[]{:S(2)}, u32[]{:S(2)}) collective-permute-start(f32[512,128]{1,0:T(8,128)S(1)} %shard_map.102.refs_0_), channel_id=1, source_target_pairs={{0,1},{1,0},{2,3},{3,2},{4,5},{5,4},{6,7},{7,6},{8,9},{9,8},{10,11... | collective-permute-start | bytes 786440 | tf_op jit(solution)/shard_map/ppermute | solution.py:308
  93.8 7.8 %collective-permute-start.23 = (f32[512,128]{1,0:T(8,128)S(1)}, f32[512,128]{1,0:T(8,128)S(1)}, u32[]{:S(2)}, u32[]{:S(2)}) collective-permute-start(f32[512,128]{1,0:T(8,128)S(1)} %shard_map.102.refs_0_), channel_id=1, source_target_pairs={{0,16},{1,17},{2,18},{3,19},{4,20},{5,21},{6,22},{7,23},{8,24},{9,... | collective-permute-start | bytes 786440 | tf_op jit(solution)/shard_map/ppermute | solution.py:308
  93.8 6.4 %collective-permute-start.27 = (f32[256,128]{1,0:T(8,128)S(1)}, f32[256,128]{1,0:T(8,128)S(1)}, u32[]{:S(2)}, u32[]{:S(2)}) collective-permute-start(f32[256,128]{1,0:T(8,128)S(1)} %shard_map.103.refs_0_), channel_id=1, source_target_pairs={{0,4},{1,5},{2,6},{3,7},{4,0},{5,1},{6,2},{7,3},{8,12},{9,13},{10,... | collective-permute-start | bytes 393224 | tf_op jit(solution)/shard_map/ppermute | solution.py:308
  95.5 6.0 %collective-permute-start.26 = (f32[256,128]{1,0:T(8,128)S(1)}, f32[256,128]{1,0:T(8,128)S(1)}, u32[]{:S(2)}, u32[]{:S(2)}) collective-permute-start(f32[256,128]{1,0:T(8,128)S(1)} %shard_map.103.refs_0_), channel_id=1, source_target_pairs={{0,2},{1,3},{2,0},{3,1},{4,6},{5,7},{6,4},{7,5},{8,10},{9,11},{10,... | collective-permute-start | bytes 393224 | tf_op jit(solution)/shard_map/ppermute | solution.py:308
  (17 other events, 130.7 us)
